TPU v7x, 512 devices: a whole 4x4x16 slice. The times are simulated.
512 devices in a mesh: blk: 32 (over z_lo, y, core), head: 16 (over z_hi, x).
Axes of the slice: x: 4, y: 4, z: 16 (z_hi: 4, z_lo: 4; z = z_hi * 4 + z_lo), core: 2. Of those that a mesh axis runs over, the one named last changes fastest.
Arguments:
- queries: bfloat16 [65536, 2048], P(('blk', 'head')), may hold values from -300 to 300
- keys: bfloat16 [65536, 1024], P(('blk', 'head')), may hold values from -6 to 6
- values: bfloat16 [65536, 1024], P(('blk', 'head')), may hold values from -6 to 6
Outputs:
- context: bfloat16 [65536, 2048], P(('blk', 'head'))
All inputs are finite; a program needn't handle non-finite values.
Results may differ from a plain program's by a relative error of at most 0.0095.
Values may be sent and summed in bfloat16 or wider, within the bound.
No kernel may reach another device: no remote copies, remote signals or barrier semaphores. Data moves between devices by JAX's collectives and lax.ppermute only.
A program may use at most 64 MiB of HBM per device.

v0:
```python
from functools import partial

import jax
import jax.numpy as jnp
from jax import lax
from jax.sharding import PartitionSpec as P

KVH = 8
HD = 128


masked_value = -1e30
head_scale = 0.08838834764831845


def spread(block, axis, owner):
    block = jnp.where(lax.axis_index(axis) == owner, block, jnp.zeros_like(block))
    return lax.psum(block, axis)


def absorb(state, q_block, k_block, v_block, offset):
    peak, total, summed = state
    scores = (
        jnp.einsum("qkgd,skd->kgqs", q_block, k_block, preferred_element_type=jnp.float32)
        * head_scale
        + offset
    )
    new_peak = jnp.maximum(peak, jnp.max(scores, axis=-1))
    rescale = jnp.exp(peak - new_peak)
    expo = jnp.exp(scores - new_peak[..., None])
    total = total * rescale + jnp.sum(expo, axis=-1)
    summed = summed * rescale[..., None] + jnp.einsum(
        "kgqs,skd->kgqd", expo.astype(jnp.bfloat16), v_block, preferred_element_type=jnp.float32
    )
    return (new_peak, total, summed)


def absorb_tile(q_block, k_tiles, v_tiles, offset, position, state):
    return absorb(state, q_block, k_tiles[position], v_tiles[position], offset)


def attend(q_heads, k_heads, v_heads, anchor_k, anchor_v, is_anchor):
    block_len = q_heads.shape[0]
    kv_count = k_heads.shape[1] // HD
    q_count = q_heads.shape[1] // HD
    group = q_count // kv_count
    rows = min(512, block_len)
    count = block_len // rows
    q_all = q_heads.reshape(block_len, kv_count, group, HD)
    k_tiles = k_heads.reshape(count, rows, kv_count, HD)
    v_tiles = v_heads.reshape(count, rows, kv_count, HD)
    anchor_k_tiles = anchor_k.reshape(count, rows, kv_count, HD)
    anchor_v_tiles = anchor_v.reshape(count, rows, kv_count, HD)
    row_ids = lax.broadcasted_iota(jnp.int32, (rows, rows), 0)
    col_ids = lax.broadcasted_iota(jnp.int32, (rows, rows), 1)
    causal = jnp.where(row_ids >= col_ids, 0.0, masked_value).astype(jnp.float32)
    anchor_offset = jnp.where(is_anchor, masked_value, 0.0).astype(jnp.float32)
    pieces = []
    for block_index in range(count):
        q_block = q_all[block_index * rows : (block_index + 1) * rows]
        start = (
            jnp.full((kv_count, group, rows), masked_value, jnp.float32),
            jnp.zeros((kv_count, group, rows), jnp.float32),
            jnp.zeros((kv_count, group, rows, HD), jnp.float32),
        )
        state = absorb(start, q_block, k_tiles[block_index], v_tiles[block_index], causal)
        earlier = partial(absorb_tile, q_block, k_tiles, v_tiles, jnp.float32(0.0))
        state = lax.fori_loop(0, block_index, earlier, state)
        anchored = partial(absorb_tile, q_block, anchor_k_tiles, anchor_v_tiles, anchor_offset)
        state = lax.fori_loop(0, count, anchored, state)
        peak, total, summed = state
        result = summed / total[..., None]
        pieces.append(result.transpose(2, 0, 1, 3).reshape(rows, q_count * HD).astype(jnp.bfloat16))
    return jnp.concatenate(pieces, 0)


def widened_heads(block, repeats):
    tok_rows = block.shape[0]
    return jnp.repeat(block.reshape(tok_rows, KVH, HD), repeats, axis=1).reshape(
        tok_rows, KVH * repeats * HD
    )


def local(queries, keys, values):
    head_count = lax.axis_size("head")
    repeats = max(1, head_count // KVH)
    q_heads, k_heads, v_heads = (
        lax.all_to_all(queries, "head", split_axis=1, concat_axis=0, tiled=True),
        lax.all_to_all(
            widened_heads(keys, repeats), "head", split_axis=1, concat_axis=0, tiled=True
        ),
        lax.all_to_all(
            widened_heads(values, repeats), "head", split_axis=1, concat_axis=0, tiled=True
        ),
    )
    anchor_k, anchor_v = (spread(k_heads, "blk", 0), spread(v_heads, "blk", 0))
    is_anchor = lax.axis_index("blk") == 0
    mixed = attend(q_heads, k_heads, v_heads, anchor_k, anchor_v, is_anchor)
    return lax.all_to_all(mixed, "head", split_axis=0, concat_axis=1, tiled=True)


def solution(mesh):
    in_specs = (P(("blk", "head"), None), P(("blk", "head"), None), P(("blk", "head"), None))
    out_specs = P(("blk", "head"), None)
    return jax.shard_map(local, mesh=mesh, in_specs=in_specs, out_specs=out_specs, check_vma=False)
```

profile of v0, /device:TPU:1, one launch (start us, length us, event | category | flops | bytes accessed | tf_op | source)
XLA Modules:
  0.0 507.3 jit_solution(7179230019407598204)
XLA Ops:
  8.4 18.3 %all-to-all-start = ((bf16[128,16,128]{2,0,1:T(8,128)(2,1)}), bf16[128,16,128]{2,0,1:T(8,128)(2,1)S(1)}, u32[]{:S(2)}, u32[]{:S(2)}) async-start(bf16[128,16,128]{2,0,1:T(8,128)(2,1)} %bitcast.66), calls=%async_computation | async-start | bytes 1048576 | tf_op jit(solution)/shard_map/all_to_all | solution.py:89
  27.8 18.5 %all-to-all-done = bf16[128,16,128]{2,0,1:T(8,128)(2,1)S(1)} async-done(((bf16[128,16,128]{2,0,1:T(8,128)(2,1)}), bf16[128,16,128]{2,0,1:T(8,128)(2,1)S(1)}, u32[]{:S(2)}, u32[]{:S(2)}) %all-to-all-start) | async-done | bytes 524320 | tf_op jit(solution)/shard_map/all_to_all | solution.py:89
  46.3 16.9 %all-to-all-start.1 = ((bf16[128,16,128]{0,2,1:T(8,128)(2,1)}), bf16[128,16,128]{0,2,1:T(8,128)(2,1)S(1)}, u32[]{:S(2)}, u32[]{:S(2)}) async-start(bf16[128,16,128]{0,2,1:T(8,128)(2,1)} %bitcast.69), calls=%async_computation.1 | async-start | bytes 1048576 | tf_op jit(solution)/shard_map/all_to_all | solution.py:88
  63.3 17.4 %all-to-all-done.1 = bf16[128,16,128]{0,2,1:T(8,128)(2,1)S(1)} async-done(((bf16[128,16,128]{0,2,1:T(8,128)(2,1)}), bf16[128,16,128]{0,2,1:T(8,128)(2,1)S(1)}, u32[]{:S(2)}, u32[]{:S(2)}) %all-to-all-start.1) | async-done | bytes 524320 | tf_op jit(solution)/shard_map/all_to_all | solution.py:88
  81.6 8.3 %all-to-all-start.2 = ((bf16[128,16,128]{2,0,1:T(8,128)(2,1)}), bf16[128,16,128]{2,0,1:T(8,128)(2,1)S(1)}, u32[]{:S(2)}, u32[]{:S(2)}) async-start(bf16[128,16,128]{2,0,1:T(8,128)(2,1)} %bitcast.77), calls=%async_computation.2 | async-start | bytes 1048576 | tf_op jit(solution)/shard_map/all_to_all | solution.py:92
  91.2 1.3 fusion.139
  92.5 14.2 %all-to-all-done.2 = bf16[128,16,128]{2,0,1:T(8,128)(2,1)S(1)} async-done(((bf16[128,16,128]{2,0,1:T(8,128)(2,1)}), bf16[128,16,128]{2,0,1:T(8,128)(2,1)S(1)}, u32[]{:S(2)}, u32[]{:S(2)}) %all-to-all-start.2) | async-done | bytes 524320 | tf_op jit(solution)/shard_map/all_to_all | solution.py:92
  113.7 2.9 while.113
  117.5 1.3 fusion.138
  120.6 1.5 fusion.103
  123.2 1.9 while.111
  125.1 300.4 %all-reduce.3.cloned.1.call-done = (bf16[4,512,1,128]{3,1,0,2:T(8,128)(2,1)}, bf16[4,512,1,128]{3,1,0,2:T(8,128)(2,1)}) async-done(((bf16[4,512,1,128]{3,1,0,2:T(8,128)(2,1)}, bf16[4,512,1,128]{3,1,0,2:T(8,128)(2,1)}), (bf16[4,512,1,128]{3,1,0,2:T(8,128)(2,1)}, bf16[4,512,1,128]{3,1,0,2:T(8,128)(2,1)})) %all-reduce.3.cloned.1.call-update) | async-done | bytes 1048592 | tf_op jit(solution)/shard_map/psum | solution.py:18
  425.5 11.1 %while.110 = (s32[]{:T(128)}, f32[1,1,512]{2,1,0:T(1,128)S(1)}, f32[1,1,512]{2,1,0:T(1,128)S(1)}, f32[1,1,512,128]{3,2,1,0:T(8,128)S(1)}, bf16[4,512,1,128]{3,1,...) while((s32[]{:T(128)}, f32[1,1,512]{2,1,0:T(1,128)S(1)}, ...), condition=%wide.region_15.16_spmd, body=%wide.region_12.0_spmd.sunk | while | flops 136184832 | bytes 4097629 | solution.py:70
  429.7 1.3 fusion.198
  432.5 1.3 fusion.198
  435.3 1.3 fusion.198
  436.6 11.1 %while.109 = (s32[]{:T(128)}, f32[1,1,512]{2,1,0:T(1,128)S(1)}, f32[1,1,512]{2,1,0:T(1,128)S(1)}, f32[1,1,512,128]{3,2,1,0:T(8,128)S(1)}, bf16[4,512,1,128]{3,1,...) while((s32[]{:T(128)}, f32[1,1,512]{2,1,0:T(1,128)S(1)}, ...), condition=%wide.region_7.8_spmd, body=%wide.region_4.7_spmd.sunk | while | flops 136184832 | bytes 4097629 | solution.py:70
  438.1 1.3 fusion.193
  440.8 1.3 fusion.193
  443.6 1.3 fusion.193
  446.4 1.3 fusion.193
  447.7 11.1 %while.114 = (s32[]{:T(128)}, f32[1,1,512]{2,1,0:T(1,128)S(1)}, f32[1,1,512]{2,1,0:T(1,128)S(1)}, f32[1,1,512,128]{3,2,1,0:T(8,128)S(1)}, bf16[4,512,1,128]{3,1,...) while((s32[]{:T(128)}, f32[1,1,512]{2,1,0:T(1,128)S(1)}, ...), condition=%wide.region_35.36_spmd, body=%wide.region_32.0_spmd.sunk | while | flops 136184832 | bytes 4097629 | solution.py:70
  449.2 1.3 fusion.218
  452.0 1.3 fusion.218
  454.7 1.3 fusion.218
  457.5 1.3 fusion.218
  458.9 11.1 %while.112 = (s32[]{:T(128)}, f32[1,1,512]{2,1,0:T(1,128)S(1)}, f32[1,1,512]{2,1,0:T(1,128)S(1)}, f32[1,1,512,128]{3,2,1,0:T(8,128)S(1)}, bf16[4,512,1,128]{3,1,...) while((s32[]{:T(128)}, f32[1,1,512]{2,1,0:T(1,128)S(1)}, ...), condition=%wide.region_25.26_spmd, body=%wide.region_22.0_spmd.sunk | while | flops 136184832 | bytes 4097629 | solution.py:70
  460.3 1.3 fusion.208
  463.1 1.3 fusion.208
  465.9 1.3 fusion.208
  468.7 1.3 fusion.208
  470.5 28.7 %all_to_all.67 = bf16[16,128,128]{2,1,0:T(8,128)(2,1)S(1)} all-to-all(bf16[16,128,128]{2,1,0:T(8,128)(2,1)S(1)} %bitcast.529), channel_id=1, replica_groups=mesh['blk'=32,'head'=16] {'head'}, dimensions={0} | all-to-all | bytes 1048576 | tf_op jit(solution)/shard_map/all_to_all | solution.py:99
  (174 shorter events, 46.3 us)
Async XLA Ops:
  6.5 1.0 copy-start
  8.4 18.3 %copy-start.5 = (bf16[128,2048]{1,0:T(8,128)(2,1)S(1)}, bf16[128,2048]{1,0:T(8,128)(2,1)}, u32[]{:S(2)}) copy-start(bf16[128,2048]{1,0:T(8,128)(2,1)} %param.15) | copy-start | bytes 1572868
  8.4 37.9 %all-to-all-start = ((bf16[128,16,128]{2,0,1:T(8,128)(2,1)}), bf16[128,16,128]{2,0,1:T(8,128)(2,1)S(1)}, u32[]{:S(2)}, u32[]{:S(2)}) async-start(bf16[128,16,128]{2,0,1:T(8,128)(2,1)} %bitcast.66), calls=%async_computation | async-start | bytes 1048576 | tf_op jit(solution)/shard_map/all_to_all | solution.py:89
  46.3 17.0 %copy-start.8 = (bf16[128,1024]{1,0:T(8,128)(2,1)S(1)}, bf16[128,1024]{1,0:T(8,128)(2,1)}, u32[]{:S(2)}) copy-start(bf16[128,1024]{1,0:T(8,128)(2,1)} %param.17) | copy-start | bytes 786436
  46.3 34.4 %all-to-all-start.1 = ((bf16[128,16,128]{0,2,1:T(8,128)(2,1)}), bf16[128,16,128]{0,2,1:T(8,128)(2,1)S(1)}, u32[]{:S(2)}, u32[]{:S(2)}) async-start(bf16[128,16,128]{0,2,1:T(8,128)(2,1)} %bitcast.69), calls=%async_computation.1 | async-start | bytes 1048576 | tf_op jit(solution)/shard_map/all_to_all | solution.py:88
  81.6 25.2 %all-to-all-start.2 = ((bf16[128,16,128]{2,0,1:T(8,128)(2,1)}), bf16[128,16,128]{2,0,1:T(8,128)(2,1)S(1)}, u32[]{:S(2)}, u32[]{:S(2)}) async-start(bf16[128,16,128]{2,0,1:T(8,128)(2,1)} %bitcast.77), calls=%async_computation.2 | async-start | bytes 1048576 | tf_op jit(solution)/shard_map/all_to_all | solution.py:92
  89.9 335.6 %all-reduce.3.cloned.1.call-start = ((), (), s32[]{:S(2)}) async-start(), calls=%async_computation.4 | async-start | bytes 2097152 | tf_op jit(solution)/shard_map/psum | solution.py:18
  91.2 17.9 %copy-start.1 = (f32[512,512]{1,0:T(8,128)}, f32[512,512]{1,0:T(8,128)S(1)}, u32[]{:S(2)}) copy-start(f32[512,512]{1,0:T(8,128)S(1)} %get-tuple-element.1234) | copy-start | bytes 3145732
  107.7 1.2 copy-start.3
  109.9 1.2 copy-start.2
  112.4 0.9 copy-start.7
  116.6 0.9 copy-start.9
  120.5 1.6 copy-start.6
  120.5 1.6 copy-start.4
  122.5 0.7 copy-start.10
Sparse Core Ops, SparseCore 0:
  120.6 304.8 all-reduce.2
where the time goes:
time: 510 us; the launch traced here: 507 us
  waiting for transfers between devices  351 us (69%)
  matrix products  49.1 us (10%)
  starting transfers between devices  43.7 us (9%)
  blocking collectives  28.7 us (6%)
  between operations  13.7 us (3%)
  local copies, waits for them, and re-layouts  11.1 us (2%)
  other arithmetic  9.71 us (2%)
    psum x1, waiting for transfers between devices, spread(): return lax.psum(block, axis)  300 us
    all_to_all x1, blocking collectives, local(): lax.all_to_all(mixed, 'head', split_axis=0, concat_axis=1, tiled=True)  28.7 us
    dot_general x26, matrix products, absorb(): jnp.einsum('qkgd,skd->kgqs', q_block, k_block, preferred_element_type=jnp...  24.6 us
    dot_general x26, matrix products, absorb(): jnp.einsum('kgqs,skd->kgqd', expo.astype(jnp.bfloat16), v_block, preferre...  24.5 us
    all_to_all x1, waiting for transfers between devices, local(): lax.all_to_all(widened_heads(keys, repeats), 'head', split_axis=1, concat...  18.5 us
    all_to_all x1, starting transfers between devices, local(): lax.all_to_all(widened_heads(keys, repeats), 'head', split_axis=1, concat...  18.3 us
    all_to_all x1, waiting for transfers between devices, local(): lax.all_to_all(queries, 'head', split_axis=1, concat_axis=0, tiled=True)  17.4 us
    all_to_all x1, starting transfers between devices, local(): lax.all_to_all(queries, 'head', split_axis=1, concat_axis=0, tiled=True)  16.9 us
  transfers between devices with their start and end apart: 4, of which 4 were waited for; matrix products, arithmetic and copies ran while one was open for 1% of the time, Pallas kernels for 0%

commit v1 on v0

v1 whole, which is shorter than its diff:
```python
import functools

import jax
import jax.numpy as jnp
from jax import lax
from jax.experimental import pallas as pl
from jax.experimental.pallas import tpu as pltpu
from jax.sharding import PartitionSpec as P

HD = 128
BF = jnp.bfloat16
F32 = jnp.float32
masked_value = -1e30
exp2_scale = 0.08838834764831845 * 1.4426950408889634

ZL, YY, CC, ZH, XX = 4, 4, 2, 4, 4


def device_index(zl, y, c, zh, x):
    return ((zl * YY + y) * CC + c) * (ZH * XX) + zh * XX + x


def pairs(move):
    found = []
    for zl in range(ZL):
        for y in range(YY):
            for c in range(CC):
                for zh in range(ZH):
                    for x in range(XX):
                        to = move(zl, y, c, zh, x)
                        if to is not None:
                            found.append((device_index(zl, y, c, zh, x), device_index(*to)))
    return found


def send(block, move):
    return lax.ppermute(block, ("blk", "head"), pairs(move))


def absorb_tile(q, k, v, state, keep=None):
    peak, total, summed = state
    scores = lax.dot_general(k, q, (((1,), (1,)), ((), ())), preferred_element_type=F32)
    if keep is not None:
        scores = jnp.where(keep, scores, masked_value)
    new_peak = jnp.maximum(peak, jnp.max(scores, axis=0, keepdims=True))
    expo = jnp.exp2((scores - new_peak) * exp2_scale)
    rescale = jnp.exp2((peak - new_peak) * exp2_scale)
    total = total * rescale + jnp.sum(expo, axis=0, keepdims=True)
    summed = summed * rescale + lax.dot_general(
        v, expo.astype(BF), (((0,), (0,)), ((), ())), preferred_element_type=F32
    )
    return new_peak, total, summed


def absorb_pair(refs, q_ref, k, v, keep=None, start=None):
    for g in range(2):
        q = q_ref[:, g * HD : (g + 1) * HD]
        state = start or tuple(ref[g] for ref in refs)
        for ref, part in zip(refs, absorb_tile(q, k, v, state, keep)):
            ref[g] = part


def own_kernel(where_ref, q_ref, ok, ov, *outs):
    refs, where_out = outs[:3], outs[3]
    x = where_ref[0]
    for n in range(3):
        where_out[n] = where_ref[n]
    rows = q_ref.shape[0]

    def place(r):
        return jnp.bitwise_and(x + XX - r // 128, XX - 1) * 128 + r % 128

    key_at = place(lax.broadcasted_iota(jnp.int32, (rows, rows), 0))
    query_at = place(lax.broadcasted_iota(jnp.int32, (rows, rows), 1))
    start = (
        jnp.full((1, rows), masked_value, F32),
        jnp.zeros((1, rows), F32),
        jnp.zeros((HD, rows), F32),
    )
    absorb_pair(refs, q_ref, ok[...], ov[...], key_at <= query_at, start)


def middle_kernel(where_ref, q_ref, p_ref, t_ref, s_ref, ak, av, bk, bv, nk, nv, *refs):
    zh, blk = where_ref[1], where_ref[2]
    for ref, before in zip(refs, (p_ref, t_ref, s_ref)):
        ref[...] = before[...]

    @pl.when(blk > 0)
    def _():
        tile = 512

        def step(t, _):
            at = pl.ds(pl.multiple_of(t * tile, tile), tile)
            absorb_pair(refs, q_ref, nk[at, :], nv[at, :])
            return 0

        lax.fori_loop(0, nk.shape[0] // tile, step, 0)

    @pl.when(zh > 0)
    def _():
        absorb_pair(refs, q_ref, ak[...], av[...])

    @pl.when(zh == 3)
    def _():
        absorb_pair(refs, q_ref, bk[...], bv[...])


def last_kernel(where_ref, q_ref, peak_ref, total_ref, summed_ref, ak, av, bk, bv, *rest):
    outs, own = rest[:4], rest[4:]
    for mine, ref in zip(own, (peak_ref, total_ref, summed_ref)):
        mine[...] = ref[...]

    @pl.when(where_ref[1] > 1)
    def _():
        k = jnp.concatenate([ak[...], bk[...]], 0)
        v = jnp.concatenate([av[...], bv[...]], 0)
        absorb_pair(own, q_ref, k, v)

    for g in range(2):
        result = (own[2][g] / own[1][g]).T.astype(BF)
        for n, out in enumerate(outs):
            out[:, g * HD : (g + 1) * HD] = result[n * 128 : (n + 1) * 128]


def head_specs(rows):
    return [
        pl.BlockSpec((rows, HD), lambda h, w: (0, h)),
        pl.BlockSpec((rows, HD), lambda h, w: (0, 2 + h)),
    ]


def state_shapes(heads, rows):
    return [(heads, 1, rows), (heads, 1, rows), (heads, HD, rows)]


def state_specs(rows):
    return [pl.BlockSpec(shape, lambda h, w: (h, 0, 0)) for shape in state_shapes(2, rows)]


def attention_call(body, name, where, q, state, parts, out_specs, out_shape, scratch, share=1):
    rows = q.shape[0]
    keys = sum(part.shape[0] for part in parts)
    in_specs = [pl.BlockSpec((rows, 2 * HD), lambda h, w: (0, h))]
    if state:
        in_specs += state_specs(rows)
    operands = [q, *state]
    for part in parts:
        in_specs += head_specs(part.shape[0])
        operands += [part, part]
    return pl.pallas_call(
        body,
        grid_spec=pltpu.PrefetchScalarGridSpec(
            num_scalar_prefetch=1,
            grid=(2,),
            in_specs=in_specs,
            out_specs=out_specs,
            scratch_shapes=scratch,
        ),
        out_shape=out_shape,
        compiler_params=pltpu.CompilerParams(vmem_limit_bytes=40 * 1024 * 1024),
        cost_estimate=pl.CostEstimate(
            flops=4 * 4 * rows * keys * HD // share, bytes_accessed=(8 << 20) // share, transcendentals=4 * rows * keys // share
        ),
        name=name,
    )(where, *operands)


def own_part(where, q, own):
    rows = q.shape[0]
    return attention_call(
        own_kernel,
        "own_attention",
        where,
        q,
        (),
        (own,),
        state_specs(rows) + [pl.BlockSpec(memory_space=pltpu.SMEM)],
        [jax.ShapeDtypeStruct(shape, F32) for shape in state_shapes(4, rows)]
        + [jax.ShapeDtypeStruct((3,), jnp.int32)],
        [],
        64,
    )


def middle(where, q, state, parts):
    rows = q.shape[0]
    return attention_call(
        middle_kernel,
        "middle_attention",
        where,
        q,
        state,
        parts,
        state_specs(rows),
        [jax.ShapeDtypeStruct(shape, F32) for shape in state_shapes(4, rows)],
        [],
    )


def last(where, q, state, parts):
    rows = q.shape[0]
    return attention_call(
        last_kernel,
        "last_attention",
        where,
        q,
        state,
        parts,
        [pl.BlockSpec((128, 2 * HD), lambda h, w: (0, h))] * 4,
        [jax.ShapeDtypeStruct((128, 4 * HD), BF)] * 4,
        [pltpu.VMEM(shape, F32) for shape in state_shapes(2, rows)],
    )


def ring(coordinate, step, size):
    return (coordinate + step) % size


def x_shift(step):
    return lambda zl, y, c, zh, x: (zl, y, c, zh, ring(x, step, XX))


def strip_of_anchor(raw, zl, y):
    part = raw.shape[0] // YY
    held = raw[:part]
    for to in range(1, YY):
        got = send(
            raw[to * part : (to + 1) * part],
            lambda zl, y, c, zh, x: (zl, to, c, zh, x) if (zl, y, c) == (0, 0, 0) else None,
        )
        held = jnp.where(y == to, got, held)
    for swap in ((1, 0, 3, 2), (3, 2, 1, 0)):
        got = send(held, lambda zl, y, c, zh, x: (zl, y, c, swap[zh], x) if (zl, c) == (0, 0) else None)
        held = jnp.concatenate([held, got], 0)
    first = lambda zl, c: (zl, c) == (0, 0)
    two = send(held, lambda zl, y, c, zh, x: (2, y, c, zh, x) if first(zl, c) else None)
    one = send(held, lambda zl, y, c, zh, x: (1, y, c, zh, x) if first(zl, c) else None)
    three = send(held, lambda zl, y, c, zh, x: (3, y, c, ring(zh, 3, ZH), x) if first(zl, c) else None)
    return jnp.where(zl == 0, held, jnp.where(zl == 1, one, jnp.where(zl == 2, two, three)))


def gather_y(block):
    half = block.shape[0] // 2
    up = lambda zl, y, c, zh, x: (zl, ring(y, 1, YY), c, zh, x) if c == 0 else None
    down = lambda zl, y, c, zh, x: (zl, ring(y, 3, YY), c, zh, x) if c == 0 else None
    low, high = send(block, up), send(block, down)
    low2, high2 = send(low[:half], up), send(high[half:], down)
    return jnp.concatenate([block, low, high, low2, high2], 0)


def local(queries, keys, values):
    blk = lax.axis_index("blk")
    head = lax.axis_index("head")
    zh, x = head // XX, head % XX
    zl, y, c = blk // (YY * CC), (blk // CC) % YY, blk % CC
    where = jnp.stack([x, zh, blk]).astype(jnp.int32)
    tok = queries.shape[0]

    width = keys.shape[1]
    raw = jnp.concatenate([keys, values], 1)

    def kv_of_head(block, among=lambda c: True):
        def piece(s):
            at = ring(x, s, XX) * 256
            rows = block.shape[0]
            return jnp.concatenate(
                [lax.dynamic_slice(block, (0, start + at), (rows, 256)) for start in (0, width)], 1
            )

        def move(s):
            return lambda zl, y, c, zh, x: (zl, y, c, zh, ring(x, s, XX)) if among(c) else None

        return jnp.concatenate([piece(0)] + [send(piece(s), move(s)) for s in (1, 2, 3)], 0)

    def q_piece(s):
        return lax.dynamic_slice(queries, (0, ring(x, s, XX) * 512), (tok, 512))

    always = blk < 32

    strip, own = lax.cond(
        always,
        lambda: (strip_of_anchor(raw, zl, y), kv_of_head(raw)),
        lambda: (jnp.zeros_like(raw), jnp.zeros((4 * tok, 512), BF)),
    )

    half = own.shape[0] // 2
    got_a = send(own, lambda zl, y, c, zh, x: (zl, y, c, zh + 1, x) if zh < 3 else None)
    got_b = send(own, lambda zl, y, c, zh, x: (zl, y, c, ring(zh, 3, ZH), x) if zh < 2 else None)

    def whole_anchor():
        whole = gather_y(kv_of_head(strip, lambda c: c == 0))
        copied = send(whole, lambda zl, y, c, zh, x: (zl, y, 1, zh, x) if c == 0 else None)
        q = [send(q_piece(s), x_shift(s)) for s in (2, 3)]
        return jnp.where(c == 0, whole, copied), *q, where

    anchor, q2, q3, where = lax.cond(
        always,
        whole_anchor,
        lambda: (jnp.zeros((2048, 512), BF),) + (jnp.zeros((tok, 512), BF),) * 2 + (where - 1,),
    )
    q = jnp.concatenate([q_piece(0), send(q_piece(1), x_shift(1)), q2, q3], 0)

    *state, where = own_part(where, q, own)
    arrived = where[2] >= 0
    got_a2 = send(
        jnp.where(arrived, got_a[:half], own[:half]),
        lambda zl, y, c, zh, x: (zl, y, c, zh + 1, x) if zh in (1, 2) else None,
    )
    got_b2 = send(
        jnp.where(arrived, got_b[half:], own[half:]),
        lambda zl, y, c, zh, x: (zl, y, c, ring(zh, 3, ZH), x) if zh in (0, 3) else None,
    )
    state = middle(where, q, state, (got_a, got_b, anchor))
    pieces = last(where, q, state, (got_a2, got_b2))
    out = jnp.zeros((tok, XX * 512), BF)
    for s in range(XX):
        piece = pieces[s] if s == 0 else send(pieces[s], x_shift(XX - s))
        out = lax.dynamic_update_slice(out, piece, (0, ring(x, s, XX) * 512))
    return out


def solution(mesh):
    spec = P(("blk", "head"), None)
    return jax.shard_map(local, mesh=mesh, in_specs=(spec,) * 3, out_specs=spec, check_vma=False)
```

time: 510 us -> 191 us (0.37)
  the two profiles are of different devices: /device:TPU:1 before, /device:TPU:408 now
where the time goes in v1:
time: 191 us
  starting transfers between devices  100 us (52%)
  waiting for transfers between devices  49.8 us (26%)
  Pallas kernels  23.3 us (12%)
  other arithmetic  8.51 us (4%)
  local copies, waits for them, and re-layouts  7.45 us (4%)
    ppermute x29, starting transfers between devices, send(): return lax.ppermute(block, ('blk', 'head'), pairs(move))  100 us
    ppermute x29, waiting for transfers between devices, send(): return lax.ppermute(block, ('blk', 'head'), pairs(move))  49.8 us
    pallas_call x3, Pallas kernels, attention_call(): pl.pallas_call(body, grid_spec=pltpu.PrefetchScalarGridSpec(num_scalar_pr...  23.3 us
    cond x8, local copies, waits for them, and re-layouts  5.11 us
  transfers between devices with their start and end apart: 29, of which 13 were waited for; matrix products, arithmetic and copies ran while one was open for 6% of the time, Pallas kernels for 10%

profile of v1, /device:TPU:408, one launch (start us, length us, event | category | flops | bytes accessed | tf_op | source)
XLA Modules:
  0.0 190.5 jit_solution(11243059007700756387)
XLA Ops:
  1.1 60.7 %conditional.2 = (bf16[128,2048]{1,0:T(8,128)(2,1)S(1)}, bf16[512,512]{1,0:T(8,128)(2,1)S(1)}) conditional(s32[]{:T(128)} %convert_element_type.4, () %tuple.23, (s32[]{:T(128)}, pred[]{:T(512)}, s32[]{:T(128)}, s32[]{:T(128)}, bf16[128,2048]{1,0:T(8,128)(2,1)S(1)}, /*index=5*/s32[]{:T(128)}, pred[]{:T(512)}, s32[]{:T(128)}, s32[]{:T(128)}, ...), branch_computations={%region_0.1_spmd, %region_1.2_spmd} | conditional | flops 8061042 | bytes 20055720 | solution.py:280
  3.9 5.4 %collective-permute-done.10 = bf16[32,2048]{1,0:T(8,128)(2,1)S(1)} collective-permute-done((bf16[32,2048]{1,0:T(8,128)(2,1)S(1)}, bf16[32,2048]{1,0:T(8,128)(2,1)S(1)}, u32[]{:S(2)}, u32[]{:S(2)}) %collective-permute-start.10) | collective-permute-done | bytes 131104 | tf_op jit(solution)/shard_map/cond/branch_1_fun/ppermute | solution.py:37
  9.4 5.5 %collective-permute-start.13 = (bf16[32,2048]{1,0:T(8,128)(2,1)S(1)}, bf16[32,2048]{1,0:T(8,128)(2,1)S(1)}, u32[]{:S(2)}, u32[]{:S(2)}) collective-permute-start(bf16[32,2048]{1,0:T(8,128)(2,1)S(1)} %select_select_fusion.1), channel_id=1, source_target_pairs={{0,4},{1,5},{2,6},{3,7},{4,0},{5,1},{6,2},{7,3},{8,12},{9,13},{10,... | collective-permute-start | bytes 393224 | tf_op jit(solution)/shard_map/cond/branch_1_fun/ppermute | solution.py:37
  14.8 5.3 %collective-permute-done.13 = bf16[32,2048]{1,0:T(8,128)(2,1)S(1)} collective-permute-done((bf16[32,2048]{1,0:T(8,128)(2,1)S(1)}, bf16[32,2048]{1,0:T(8,128)(2,1)S(1)}, u32[]{:S(2)}, u32[]{:S(2)}) %collective-permute-start.13) | collective-permute-done | bytes 131104 | tf_op jit(solution)/shard_map/cond/branch_1_fun/ppermute | solution.py:37
  22.3 10.1 %collective-permute-done.14 = bf16[64,2048]{1,0:T(8,128)(2,1)S(1)} collective-permute-done((bf16[64,2048]{1,0:T(8,128)(2,1)S(1)}, bf16[64,2048]{1,0:T(8,128)(2,1)S(1)}, u32[]{:S(2)}, u32[]{:S(2)}) %collective-permute-start.14) | collective-permute-done | bytes 262176 | tf_op jit(solution)/shard_map/cond/branch_1_fun/ppermute | solution.py:37
  37.1 3.4 %collective-permute-start.18 = (bf16[128,512]{1,0:T(8,128)(2,1)S(1)}, bf16[128,512]{1,0:T(8,128)(2,1)S(1)}, u32[]{:S(2)}, u32[]{:S(2)}) collective-permute-start(bf16[128,512]{1,0:T(8,128)(2,1)S(1)} %pad_maximum_fusion.3), channel_id=1, source_target_pairs={{0,1},{1,2},{2,3},{3,0},{4,5},{5,6},{6,7},{7,4},{8,9},{9,10},{10,1... | collective-permute-start | bytes 393224 | tf_op jit(solution)/shard_map/cond/branch_1_fun/ppermute | solution.py:37
  40.6 4.6 %collective-permute-start.19 = (bf16[128,512]{1,0:T(8,128)(2,1)S(1)}, bf16[128,512]{1,0:T(8,128)(2,1)S(1)}, u32[]{:S(2)}, u32[]{:S(2)}) collective-permute-start(bf16[128,512]{1,0:T(8,128)(2,1)S(1)} %pad_maximum_fusion.4), channel_id=1, source_target_pairs={{0,2},{1,3},{2,0},{3,1},{4,6},{5,7},{6,4},{7,5},{8,10},{9,11},{10,... | collective-permute-start | bytes 393224 | tf_op jit(solution)/shard_map/cond/branch_1_fun/ppermute | solution.py:37
  45.3 4.4 %collective-permute-start.20 = (bf16[128,512]{1,0:T(8,128)(2,1)S(1)}, bf16[128,512]{1,0:T(8,128)(2,1)S(1)}, u32[]{:S(2)}, u32[]{:S(2)}) collective-permute-start(bf16[128,512]{1,0:T(8,128)(2,1)S(1)} %pad_maximum_fusion.5), channel_id=1, source_target_pairs={{0,3},{1,0},{2,1},{3,2},{4,7},{5,4},{6,5},{7,6},{8,11},{9,8},{10,9... | collective-permute-start | bytes 393224 | tf_op jit(solution)/shard_map/cond/branch_1_fun/ppermute | solution.py:37
  49.8 2.5 %collective-permute-done.20 = bf16[128,512]{1,0:T(8,128)(2,1)S(1)} collective-permute-done((bf16[128,512]{1,0:T(8,128)(2,1)S(1)}, bf16[128,512]{1,0:T(8,128)(2,1)S(1)}, u32[]{:S(2)}, u32[]{:S(2)}) %collective-permute-start.20) | collective-permute-done | bytes 131104 | tf_op jit(solution)/shard_map/cond/branch_1_fun/ppermute | solution.py:37
  54.7 5.6 %collective-permute-done.16 = bf16[128,2048]{1,0:T(8,128)(2,1)S(1)} collective-permute-done((bf16[128,2048]{1,0:T(8,128)(2,1)S(1)}, bf16[128,2048]{1,0:T(8,128)(2,1)S(1)}, u32[]{:S(2)}, u32[]{:S(2)}) %collective-permute-start.16) | collective-permute-done | bytes 524320 | tf_op jit(solution)/shard_map/cond/branch_1_fun/ppermute | solution.py:37
  64.5 67.0 %conditional.3 = (bf16[2048,512]{1,0:T(8,128)(2,1)}, bf16[128,512]{1,0:T(8,128)(2,1)}, bf16[128,512]{1,0:T(8,128)(2,1)}, s32[3]{0:T(128)S(1)}) conditional(s32[]{:T(128)} %convert_element_type.4, s32[3]{0:T(128)S(1)} %pad_add_fusion, (s32[]{:T(128)}, s32[]{:T(128)}, bf16[128,2048]{1,0:T(8,128)(2,1)S(1)}, bf16[128,2048]{1,0:T(8,128)(2,1)S(1)}, ...), branch_computations={%region_2.3_spmd, %region_3.4_spmd} | conditional | flops 4718684 | bytes 32245164 | solution.py:296
  64.6 4.3 %collective-permute-start = (bf16[128,512]{1,0:T(8,128)(2,1)S(1)}, bf16[128,512]{1,0:T(8,128)(2,1)S(1)}, u32[]{:S(2)}, u32[]{:S(2)}) collective-permute-start(bf16[128,512]{1,0:T(8,128)(2,1)S(1)} %pad_maximum_fusion.7), channel_id=1, source_target_pairs={{0,1},{1,2},{2,3},{3,0},{4,5},{5,6},{6,7},{7,4},{8,9},{9,10},{10,1... | collective-permute-start | bytes 393224 | tf_op jit(solution)/shard_map/cond/branch_1_fun/ppermute | solution.py:37
  69.0 3.8 %collective-permute-start.1 = (bf16[128,512]{1,0:T(8,128)(2,1)S(1)}, bf16[128,512]{1,0:T(8,128)(2,1)S(1)}, u32[]{:S(2)}, u32[]{:S(2)}) collective-permute-start(bf16[128,512]{1,0:T(8,128)(2,1)S(1)} %pad_maximum_fusion.8), channel_id=1, source_target_pairs={{0,2},{1,3},{2,0},{3,1},{4,6},{5,7},{6,4},{7,5},{8,10},{9,11},{10,... | collective-permute-start | bytes 393224 | tf_op jit(solution)/shard_map/cond/branch_1_fun/ppermute | solution.py:37
  72.8 4.5 %collective-permute-start.2 = (bf16[128,512]{1,0:T(8,128)(2,1)S(1)}, bf16[128,512]{1,0:T(8,128)(2,1)S(1)}, u32[]{:S(2)}, u32[]{:S(2)}) collective-permute-start(bf16[128,512]{1,0:T(8,128)(2,1)S(1)} %pad_maximum_fusion.9), channel_id=1, source_target_pairs={{0,3},{1,0},{2,1},{3,2},{4,7},{5,4},{6,5},{7,6},{8,11},{9,8},{10,9... | collective-permute-start | bytes 393224 | tf_op jit(solution)/shard_map/cond/branch_1_fun/ppermute | solution.py:37
  77.4 2.5 %collective-permute-done.2 = bf16[128,512]{1,0:T(8,128)(2,1)S(1)} collective-permute-done((bf16[128,512]{1,0:T(8,128)(2,1)S(1)}, bf16[128,512]{1,0:T(8,128)(2,1)S(1)}, u32[]{:S(2)}, u32[]{:S(2)}) %collective-permute-start.2) | collective-permute-done | bytes 131104 | tf_op jit(solution)/shard_map/cond/branch_1_fun/ppermute | solution.py:37
  79.9 16.5 %collective-permute-start.3 = (bf16[512,512]{1,0:T(8,128)(2,1)S(1)}, bf16[512,512]{1,0:T(8,128)(2,1)S(1)}, u32[]{:S(2)}, u32[]{:S(2)}) collective-permute-start(bf16[512,512]{1,0:T(8,128)(2,1)S(1)} %pad_maximum_fusion.6), channel_id=1, source_target_pairs={{0,32},{1,33},{2,34},{3,35},{4,36},{5,37},{6,38},{7,39},{8,40},{9,... | collective-permute-start | bytes 1572872 | tf_op jit(solution)/shard_map/cond/branch_1_fun/ppermute | solution.py:37
  100.4 2.7 %collective-permute-done.3 = bf16[512,512]{1,0:T(8,128)(2,1)S(1)} collective-permute-done((bf16[512,512]{1,0:T(8,128)(2,1)S(1)}, bf16[512,512]{1,0:T(8,128)(2,1)S(1)}, u32[]{:S(2)}, u32[]{:S(2)}) %collective-permute-start.3) | collective-permute-done | bytes 524320 | tf_op jit(solution)/shard_map/cond/branch_1_fun/ppermute | solution.py:37
  103.1 5.6 %collective-permute-start.5 = (bf16[256,512]{1,0:T(8,128)(2,1)S(1)}, bf16[256,512]{1,0:T(8,128)(2,1)S(1)}, u32[]{:S(2)}, u32[]{:S(2)}) collective-permute-start(bf16[256,512]{1,0:T(8,128)(2,1)S(1)} %slice.38), channel_id=1, source_target_pairs={{0,32},{1,33},{2,34},{3,35},{4,36},{5,37},{6,38},{7,39},{8,40},{9,... | collective-permute-start | bytes 786440 | tf_op jit(solution)/shard_map/cond/branch_1_fun/ppermute | solution.py:37
  113.8 5.1 %collective-permute-done.6 = bf16[256,512]{1,0:T(8,128)(2,1)S(1)} collective-permute-done((bf16[256,512]{1,0:T(8,128)(2,1)S(1)}, bf16[256,512]{1,0:T(8,128)(2,1)S(1)}, u32[]{:S(2)}, u32[]{:S(2)}) %collective-permute-start.6) | collective-permute-done | bytes 262176 | tf_op jit(solution)/shard_map/cond/branch_1_fun/ppermute | solution.py:37
  119.6 2.6 %collective-permute-start.7 = (bf16[2048,512]{1,0:T(8,128)(2,1)}, bf16[2048,512]{1,0:T(8,128)(2,1)}, u32[]{:S(2)}, u32[]{:S(2)}) collective-permute-start(bf16[2048,512]{1,0:T(8,128)(2,1)} %constant_dynamic-update-slice_fusion), channel_id=1, source_target_pairs={{0,16},{1,17},{2,18},{3,19},{4,20},{5,21},{6,22},{7,23},{8,24},{9,... | collective-permute-start | bytes 6291464 | tf_op jit(solution)/shard_map/cond/branch_1_fun/ppermute | solution.py:37
  124.2 4.1 %collective-permute-start.9 = (bf16[128,512]{1,0:T(8,128)(2,1)S(1)}, bf16[128,512]{1,0:T(8,128)(2,1)}, u32[]{:S(2)}, u32[]{:S(2)}) collective-permute-start(bf16[128,512]{1,0:T(8,128)(2,1)S(1)} %get-tuple-element.153), channel_id=1, source_target_pairs={{0,3},{1,0},{2,1},{3,2},{4,7},{5,4},{6,5},{7,6},{8,11},{9,8},{10,9... | collective-permute-start | bytes 393224 | tf_op jit(solution)/shard_map/cond/branch_1_fun/ppermute | solution.py:37
  128.3 3.1 %broadcast_select_fusion = bf16[2048,512]{1,0:T(8,128)(2,1)} fusion(bf16[2048,512]{1,0:T(8,128)(2,1)} %constant_dynamic-update-slice_fusion, bf16[2048,512]{1,0:T(8,128)(2,1)} %collective-permute-done.7, pred[]{:T(512)S(6)} %eq.40), kind=kLoop, calls=%fused_computation.17 | loop fusion | flops 1048576 | bytes 6291457 | tf_op jit(solution)/shard_map/cond/branch_1_fun/jit(_where)/select_n | solution.py:294
  131.5 3.9 %collective-permute-start.21 = (bf16[128,512]{1,0:T(8,128)(2,1)S(1)}, bf16[128,512]{1,0:T(8,128)(2,1)S(1)}, u32[]{:S(2)}, u32[]{:S(2)}) collective-permute-start(bf16[128,512]{1,0:T(8,128)(2,1)S(1)} %get-tuple-element.166), channel_id=1, source_target_pairs={{0,1},{1,2},{2,3},{3,0},{4,5},{5,6},{6,7},{7,4},{8,9},{9,10},{10,1... | collective-permute-start | bytes 393224 | tf_op jit(solution)/shard_map/ppermute | solution.py:37
  135.4 4.2 %collective-permute-done.21 = bf16[128,512]{1,0:T(8,128)(2,1)S(1)} collective-permute-done((bf16[128,512]{1,0:T(8,128)(2,1)S(1)}, bf16[128,512]{1,0:T(8,128)(2,1)S(1)}, u32[]{:S(2)}, u32[]{:S(2)}) %collective-permute-start.21) | collective-permute-done | bytes 131104 | tf_op jit(solution)/shard_map/ppermute | solution.py:37
  140.6 3.3 %own_attention.1 = (f32[4,1,512]{2,1,0:T(1,128)S(1)}, f32[4,1,512]{2,1,0:T(1,128)S(1)}, f32[4,128,512]{2,1,0:T(8,128)S(1)}, s32[3]{0:T(128)S(1)}) custom-call(s32[3]{0:T(128)S(1)} %get-tuple-element.110.where_ref, bf16[512,512]{1,0:T(8,128)(2,1)S(1)} %pad_maximum_fusion.11.q_ref, bf16[512,512]{1,0:T(8,128)(2,1)S(1)} %get-tuple-element.113.ok.ov, ...), custom_call_target="tpu_custom_call" | custom-call | flops 8388608 | bytes 131072 | tf_op jit(solution)/shard_map/own_attention/pallas_call | solution.py:150
  146.5 8.5 %collective-permute-start.25 = (bf16[256,512]{1,0:T(8,128)(2,1)S(1)}, bf16[256,512]{1,0:T(8,128)(2,1)S(1)}, u32[]{:S(2)}, u32[]{:S(2)}) collective-permute-start(bf16[256,512]{1,0:T(8,128)(2,1)S(1)} %get-tuple-element.163), channel_id=1, source_target_pairs={{0,12},{1,13},{2,14},{3,15},{12,8},{13,9},{14,10},{15,11},{16,28},... | collective-permute-start | bytes 786440 | tf_op jit(solution)/shard_map/ppermute | solution.py:37
  155.0 16.4 %middle_attention.1 = (f32[4,1,512]{2,1,0:T(1,128)S(1)}, f32[4,1,512]{2,1,0:T(1,128)S(1)}, f32[4,128,512]{2,1,0:T(8,128)S(1)}) custom-call(s32[3]{0:T(128)S(1)} %get-tuple-element.114.where_ref, bf16[512,512]{1,0:T(8,128)(2,1)S(1)} %pad_maximum_fusion.11.q_ref, f32[4,1,512]{2,1,0:T(1,128)S(1)} %get-tuple-element.115.p_ref, ...), custom_call_target="tpu_custom_call" | custom-call | flops 3221225472 | bytes 8388608 | tf_op jit(solution)/shard_map/middle_attention/pallas_call | solution.py:150
  171.5 3.6 %last_attention.1 = (bf16[128,512]{1,0:T(8,128)(2,1)S(1)}, bf16[128,512]{1,0:T(8,128)(2,1)S(1)}, bf16[128,512]{1,0:T(8,128)(2,1)S(1)}, bf16[128,512]{1,0:T(8,128)(2,1)S(1)}) custom-call(s32[3]{0:T(128)S(1)} %get-tuple-element.114.where_ref, bf16[512,512]{1,0:T(8,128)(2,1)S(1)} %pad_maximum_fusion.11.q_ref, f32[4,1,512]{2,1,0:T(1,128)S(1)} %get-tuple-element.119.peak_ref, ...), custom_call_target="tpu_custom_call" | custom-call | flops 536870912 | bytes 8388608 | tf_op jit(solution)/shard_map/last_attention/pallas_call | solution.py:150
  175.0 3.8 %collective-permute-start.26 = (bf16[128,512]{1,0:T(8,128)(2,1)S(1)}, bf16[128,512]{1,0:T(8,128)(2,1)S(1)}, u32[]{:S(2)}, u32[]{:S(2)}) collective-permute-start(bf16[128,512]{1,0:T(8,128)(2,1)S(1)} %get-tuple-element.123), channel_id=1, source_target_pairs={{0,3},{1,0},{2,1},{3,2},{4,7},{5,4},{6,5},{7,6},{8,11},{9,8},{10,9... | collective-permute-start | bytes 393224 | tf_op jit(solution)/shard_map/ppermute | solution.py:37
  178.9 2.9 %collective-permute-start.27 = (bf16[128,512]{1,0:T(8,128)(2,1)S(1)}, bf16[128,512]{1,0:T(8,128)(2,1)S(1)}, u32[]{:S(2)}, u32[]{:S(2)}) collective-permute-start(bf16[128,512]{1,0:T(8,128)(2,1)S(1)} %get-tuple-element.124), channel_id=1, source_target_pairs={{0,2},{1,3},{2,0},{3,1},{4,6},{5,7},{6,4},{7,5},{8,10},{9,11},{10,... | collective-permute-start | bytes 393224 | tf_op jit(solution)/shard_map/ppermute | solution.py:37
  184.3 2.9 %collective-permute-done.27 = bf16[128,512]{1,0:T(8,128)(2,1)S(1)} collective-permute-done((bf16[128,512]{1,0:T(8,128)(2,1)S(1)}, bf16[128,512]{1,0:T(8,128)(2,1)S(1)}, u32[]{:S(2)}, u32[]{:S(2)}) %collective-permute-start.27) | collective-permute-done | bytes 131104 | tf_op jit(solution)/shard_map/ppermute | solution.py:37
  187.3 2.6 %collective-permute-done.28 = bf16[128,512]{1,0:T(8,128)(2,1)S(1)} collective-permute-done((bf16[128,512]{1,0:T(8,128)(2,1)S(1)}, bf16[128,512]{1,0:T(8,128)(2,1)S(1)}, u32[]{:S(2)}, u32[]{:S(2)}) %collective-permute-start.28) | collective-permute-done | bytes 131104 | tf_op jit(solution)/shard_map/ppermute | solution.py:37
  (75 shorter events, 35.3 us)
Async XLA Ops:
  1.1 63.4 %copy-start.1 = (bf16[128,2048]{1,0:T(8,128)(2,1)S(1)}, bf16[128,2048]{1,0:T(8,128)(2,1)}, u32[]{:S(2)}) copy-start(bf16[128,2048]{1,0:T(8,128)(2,1)} %param.7) | copy-start | bytes 1572868
  1.1 8.2 %collective-permute-start.10 = (bf16[32,2048]{1,0:T(8,128)(2,1)S(1)}, bf16[32,2048]{1,0:T(8,128)(2,1)S(1)}, u32[]{:S(2)}, u32[]{:S(2)}) collective-permute-start(bf16[32,2048]{1,0:T(8,128)(2,1)S(1)} %get-tuple-element.152), channel_id=1, source_target_pairs={{0,96},{1,97},{2,98},{3,99},{4,100},{5,101},{6,102},{7,103},{8,104... | collective-permute-start | bytes 393224 | tf_op jit(solution)/shard_map/cond/branch_1_fun/ppermute | solution.py:37
  2.6 6.8 %collective-permute-start.11 = (bf16[32,2048]{1,0:T(8,128)(2,1)S(1)}, bf16[32,2048]{1,0:T(8,128)(2,1)S(1)}, u32[]{:S(2)}, u32[]{:S(2)}) collective-permute-start(bf16[32,2048]{1,0:T(8,128)(2,1)S(1)} %get-tuple-element.151), channel_id=1, source_target_pairs={{0,64},{1,65},{2,66},{3,67},{4,68},{5,69},{6,70},{7,71},{8,72},{9,... | collective-permute-start | bytes 393224 | tf_op jit(solution)/shard_map/cond/branch_1_fun/ppermute | solution.py:37
  3.2 6.1 %collective-permute-start.12 = (bf16[32,2048]{1,0:T(8,128)(2,1)S(1)}, bf16[32,2048]{1,0:T(8,128)(2,1)S(1)}, u32[]{:S(2)}, u32[]{:S(2)}) collective-permute-start(bf16[32,2048]{1,0:T(8,128)(2,1)S(1)} %get-tuple-element.150), channel_id=1, source_target_pairs={{0,32},{1,33},{2,34},{3,35},{4,36},{5,37},{6,38},{7,39},{8,40},{9,... | collective-permute-start | bytes 393224 | tf_op jit(solution)/shard_map/cond/branch_1_fun/ppermute | solution.py:37
  9.4 10.8 %collective-permute-start.13 = (bf16[32,2048]{1,0:T(8,128)(2,1)S(1)}, bf16[32,2048]{1,0:T(8,128)(2,1)S(1)}, u32[]{:S(2)}, u32[]{:S(2)}) collective-permute-start(bf16[32,2048]{1,0:T(8,128)(2,1)S(1)} %select_select_fusion.1), channel_id=1, source_target_pairs={{0,4},{1,5},{2,6},{3,7},{4,0},{5,1},{6,2},{7,3},{8,12},{9,13},{10,... | collective-permute-start | bytes 393224 | tf_op jit(solution)/shard_map/cond/branch_1_fun/ppermute | solution.py:37
  20.2 12.2 %collective-permute-start.14 = (bf16[64,2048]{1,0:T(8,128)(2,1)S(1)}, bf16[64,2048]{1,0:T(8,128)(2,1)S(1)}, u32[]{:S(2)}, u32[]{:S(2)}) collective-permute-start(bf16[64,2048]{1,0:T(8,128)(2,1)S(1)} %pad_maximum_fusion.2), channel_id=1, source_target_pairs={{0,12},{1,13},{2,14},{3,15},{4,8},{5,9},{6,10},{7,11},{8,4},{9,5},... | collective-permute-start | bytes 786440 | tf_op jit(solution)/shard_map/cond/branch_1_fun/ppermute | solution.py:37
  32.4 22.4 %collective-permute-start.15 = (bf16[128,2048]{1,0:T(8,128)(2,1)S(1)}, bf16[128,2048]{1,0:T(8,128)(2,1)S(1)}, u32[]{:S(2)}, u32[]{:S(2)}) collective-permute-start(bf16[128,2048]{1,0:T(8,128)(2,1)S(1)} %pad_maximum_fusion), channel_id=1, source_target_pairs={{0,128},{1,129},{2,130},{3,131},{4,132},{5,133},{6,134},{7,135},{8... | collective-permute-start | bytes 1572872 | tf_op jit(solution)/shard_map/cond/branch_1_fun/ppermute | solution.py:37
  33.7 26.6 %collective-permute-start.16 = (bf16[128,2048]{1,0:T(8,128)(2,1)S(1)}, bf16[128,2048]{1,0:T(8,128)(2,1)S(1)}, u32[]{:S(2)}, u32[]{:S(2)}) collective-permute-start(bf16[128,2048]{1,0:T(8,128)(2,1)S(1)} %pad_maximum_fusion), channel_id=1, source_target_pairs={{0,256},{1,257},{2,258},{3,259},{4,260},{5,261},{6,262},{7,263},{8... | collective-permute-start | bytes 1572872 | tf_op jit(solution)/shard_map/cond/branch_1_fun/ppermute | solution.py:37
  35.0 25.3 %collective-permute-start.17 = (bf16[128,2048]{1,0:T(8,128)(2,1)S(1)}, bf16[128,2048]{1,0:T(8,128)(2,1)}, u32[]{:S(2)}, u32[]{:S(2)}) collective-permute-start(bf16[128,2048]{1,0:T(8,128)(2,1)S(1)} %pad_maximum_fusion), channel_id=1, source_target_pairs={{0,396},{1,397},{2,398},{3,399},{4,384},{5,385},{6,386},{7,387},{8... | collective-permute-start | bytes 1572872 | tf_op jit(solution)/shard_map/cond/branch_1_fun/ppermute | solution.py:37
  37.1 8.2 %collective-permute-start.18 = (bf16[128,512]{1,0:T(8,128)(2,1)S(1)}, bf16[128,512]{1,0:T(8,128)(2,1)S(1)}, u32[]{:S(2)}, u32[]{:S(2)}) collective-permute-start(bf16[128,512]{1,0:T(8,128)(2,1)S(1)} %pad_maximum_fusion.3), channel_id=1, source_target_pairs={{0,1},{1,2},{2,3},{3,0},{4,5},{5,6},{6,7},{7,4},{8,9},{9,10},{10,1... | collective-permute-start | bytes 393224 | tf_op jit(solution)/shard_map/cond/branch_1_fun/ppermute | solution.py:37
  40.6 9.2 %collective-permute-start.19 = (bf16[128,512]{1,0:T(8,128)(2,1)S(1)}, bf16[128,512]{1,0:T(8,128)(2,1)S(1)}, u32[]{:S(2)}, u32[]{:S(2)}) collective-permute-start(bf16[128,512]{1,0:T(8,128)(2,1)S(1)} %pad_maximum_fusion.4), channel_id=1, source_target_pairs={{0,2},{1,3},{2,0},{3,1},{4,6},{5,7},{6,4},{7,5},{8,10},{9,11},{10,... | collective-permute-start | bytes 393224 | tf_op jit(solution)/shard_map/cond/branch_1_fun/ppermute | solution.py:37
  45.3 6.9 %collective-permute-start.20 = (bf16[128,512]{1,0:T(8,128)(2,1)S(1)}, bf16[128,512]{1,0:T(8,128)(2,1)S(1)}, u32[]{:S(2)}, u32[]{:S(2)}) collective-permute-start(bf16[128,512]{1,0:T(8,128)(2,1)S(1)} %pad_maximum_fusion.5), channel_id=1, source_target_pairs={{0,3},{1,0},{2,1},{3,2},{4,7},{5,4},{6,5},{7,6},{8,11},{9,8},{10,9... | collective-permute-start | bytes 393224 | tf_op jit(solution)/shard_map/cond/branch_1_fun/ppermute | solution.py:37
  52.3 0.7 copy-start.2
  61.7 83.4 %collective-permute-start.22 = (bf16[512,512]{1,0:T(8,128)(2,1)S(1)}, bf16[512,512]{1,0:T(8,128)(2,1)S(1)}, u32[]{:S(2)}, u32[]{:S(2)}) collective-permute-start(bf16[512,512]{1,0:T(8,128)(2,1)S(1)} %get-tuple-element.113.ok.ov), channel_id=1, source_target_pairs={{0,4},{1,5},{2,6},{3,7},{4,8},{5,9},{6,10},{7,11},{8,12},{9,13},{1... | collective-permute-start | bytes 1572872 | tf_op jit(solution)/shard_map/ppermute | solution.py:37
  63.0 82.1 %collective-permute-start.23 = (bf16[512,512]{1,0:T(8,128)(2,1)S(1)}, bf16[512,512]{1,0:T(8,128)(2,1)S(1)}, u32[]{:S(2)}, u32[]{:S(2)}) collective-permute-start(bf16[512,512]{1,0:T(8,128)(2,1)S(1)} %get-tuple-element.113.ok.ov), channel_id=1, source_target_pairs={{0,12},{1,13},{2,14},{3,15},{4,0},{5,1},{6,2},{7,3},{16,28},{17,29... | collective-permute-start | bytes 1572872 | tf_op jit(solution)/shard_map/ppermute | solution.py:37
  64.6 12.7 %collective-permute-start = (bf16[128,512]{1,0:T(8,128)(2,1)S(1)}, bf16[128,512]{1,0:T(8,128)(2,1)S(1)}, u32[]{:S(2)}, u32[]{:S(2)}) collective-permute-start(bf16[128,512]{1,0:T(8,128)(2,1)S(1)} %pad_maximum_fusion.7), channel_id=1, source_target_pairs={{0,1},{1,2},{2,3},{3,0},{4,5},{5,6},{6,7},{7,4},{8,9},{9,10},{10,1... | collective-permute-start | bytes 393224 | tf_op jit(solution)/shard_map/cond/branch_1_fun/ppermute | solution.py:37
  69.0 8.4 %collective-permute-start.1 = (bf16[128,512]{1,0:T(8,128)(2,1)S(1)}, bf16[128,512]{1,0:T(8,128)(2,1)S(1)}, u32[]{:S(2)}, u32[]{:S(2)}) collective-permute-start(bf16[128,512]{1,0:T(8,128)(2,1)S(1)} %pad_maximum_fusion.8), channel_id=1, source_target_pairs={{0,2},{1,3},{2,0},{3,1},{4,6},{5,7},{6,4},{7,5},{8,10},{9,11},{10,... | collective-permute-start | bytes 393224 | tf_op jit(solution)/shard_map/cond/branch_1_fun/ppermute | solution.py:37
  72.8 7.0 %collective-permute-start.2 = (bf16[128,512]{1,0:T(8,128)(2,1)S(1)}, bf16[128,512]{1,0:T(8,128)(2,1)S(1)}, u32[]{:S(2)}, u32[]{:S(2)}) collective-permute-start(bf16[128,512]{1,0:T(8,128)(2,1)S(1)} %pad_maximum_fusion.9), channel_id=1, source_target_pairs={{0,3},{1,0},{2,1},{3,2},{4,7},{5,4},{6,5},{7,6},{8,11},{9,8},{10,9... | collective-permute-start | bytes 393224 | tf_op jit(solution)/shard_map/cond/branch_1_fun/ppermute | solution.py:37
  79.9 23.2 %collective-permute-start.3 = (bf16[512,512]{1,0:T(8,128)(2,1)S(1)}, bf16[512,512]{1,0:T(8,128)(2,1)S(1)}, u32[]{:S(2)}, u32[]{:S(2)}) collective-permute-start(bf16[512,512]{1,0:T(8,128)(2,1)S(1)} %pad_maximum_fusion.6), channel_id=1, source_target_pairs={{0,32},{1,33},{2,34},{3,35},{4,36},{5,37},{6,38},{7,39},{8,40},{9,... | collective-permute-start | bytes 1572872 | tf_op jit(solution)/shard_map/cond/branch_1_fun/ppermute | solution.py:37
  96.4 13.0 %collective-permute-start.4 = (bf16[512,512]{1,0:T(8,128)(2,1)S(1)}, bf16[512,512]{1,0:T(8,128)(2,1)S(1)}, u32[]{:S(2)}, u32[]{:S(2)}) collective-permute-start(bf16[512,512]{1,0:T(8,128)(2,1)S(1)} %pad_maximum_fusion.6), channel_id=1, source_target_pairs={{0,96},{1,97},{2,98},{3,99},{4,100},{5,101},{6,102},{7,103},{8,104... | collective-permute-start | bytes 1572872 | tf_op jit(solution)/shard_map/cond/branch_1_fun/ppermute | solution.py:37
  103.1 9.9 %collective-permute-start.5 = (bf16[256,512]{1,0:T(8,128)(2,1)S(1)}, bf16[256,512]{1,0:T(8,128)(2,1)S(1)}, u32[]{:S(2)}, u32[]{:S(2)}) collective-permute-start(bf16[256,512]{1,0:T(8,128)(2,1)S(1)} %slice.38), channel_id=1, source_target_pairs={{0,32},{1,33},{2,34},{3,35},{4,36},{5,37},{6,38},{7,39},{8,40},{9,... | collective-permute-start | bytes 786440 | tf_op jit(solution)/shard_map/cond/branch_1_fun/ppermute | solution.py:37
  109.4 9.5 %collective-permute-start.6 = (bf16[256,512]{1,0:T(8,128)(2,1)S(1)}, bf16[256,512]{1,0:T(8,128)(2,1)S(1)}, u32[]{:S(2)}, u32[]{:S(2)}) collective-permute-start(bf16[256,512]{1,0:T(8,128)(2,1)S(1)} %slice.39), channel_id=1, source_target_pairs={{0,96},{1,97},{2,98},{3,99},{4,100},{5,101},{6,102},{7,103},{8,104... | collective-permute-start | bytes 786440 | tf_op jit(solution)/shard_map/cond/branch_1_fun/ppermute | solution.py:37
  119.6 8.8 %collective-permute-start.7 = (bf16[2048,512]{1,0:T(8,128)(2,1)}, bf16[2048,512]{1,0:T(8,128)(2,1)}, u32[]{:S(2)}, u32[]{:S(2)}) collective-permute-start(bf16[2048,512]{1,0:T(8,128)(2,1)} %constant_dynamic-update-slice_fusion), channel_id=1, source_target_pairs={{0,16},{1,17},{2,18},{3,19},{4,20},{5,21},{6,22},{7,23},{8,24},{9,... | collective-permute-start | bytes 6291464 | tf_op jit(solution)/shard_map/cond/branch_1_fun/ppermute | solution.py:37
  122.2 9.2 %collective-permute-start.8 = (bf16[128,512]{1,0:T(8,128)(2,1)S(1)}, bf16[128,512]{1,0:T(8,128)(2,1)}, u32[]{:S(2)}, u32[]{:S(2)}) collective-permute-start(bf16[128,512]{1,0:T(8,128)(2,1)S(1)} %get-tuple-element.154), channel_id=1, source_target_pairs={{0,2},{1,3},{2,0},{3,1},{4,6},{5,7},{6,4},{7,5},{8,10},{9,11},{10,... | collective-permute-start | bytes 393224 | tf_op jit(solution)/shard_map/cond/branch_1_fun/ppermute | solution.py:37
  124.2 7.3 %collective-permute-start.9 = (bf16[128,512]{1,0:T(8,128)(2,1)S(1)}, bf16[128,512]{1,0:T(8,128)(2,1)}, u32[]{:S(2)}, u32[]{:S(2)}) collective-permute-start(bf16[128,512]{1,0:T(8,128)(2,1)S(1)} %get-tuple-element.153), channel_id=1, source_target_pairs={{0,3},{1,0},{2,1},{3,2},{4,7},{5,4},{6,5},{7,6},{8,11},{9,8},{10,9... | collective-permute-start | bytes 393224 | tf_op jit(solution)/shard_map/cond/branch_1_fun/ppermute | solution.py:37
  131.5 8.1 %collective-permute-start.21 = (bf16[128,512]{1,0:T(8,128)(2,1)S(1)}, bf16[128,512]{1,0:T(8,128)(2,1)S(1)}, u32[]{:S(2)}, u32[]{:S(2)}) collective-permute-start(bf16[128,512]{1,0:T(8,128)(2,1)S(1)} %get-tuple-element.166), channel_id=1, source_target_pairs={{0,1},{1,2},{2,3},{3,0},{4,5},{5,6},{6,7},{7,4},{8,9},{9,10},{10,1... | collective-permute-start | bytes 393224 | tf_op jit(solution)/shard_map/ppermute | solution.py:37
  145.2 26.2 %collective-permute-start.24 = (bf16[256,512]{1,0:T(8,128)(2,1)S(1)}, bf16[256,512]{1,0:T(8,128)(2,1)S(1)}, u32[]{:S(2)}, u32[]{:S(2)}) collective-permute-start(bf16[256,512]{1,0:T(8,128)(2,1)S(1)} %get-tuple-element.164), channel_id=1, source_target_pairs={{4,8},{5,9},{6,10},{7,11},{8,12},{9,13},{10,14},{11,15},{20,24},{2... | collective-permute-start | bytes 786440 | tf_op jit(solution)/shard_map/ppermute | solution.py:37
  146.5 24.9 %collective-permute-start.25 = (bf16[256,512]{1,0:T(8,128)(2,1)S(1)}, bf16[256,512]{1,0:T(8,128)(2,1)S(1)}, u32[]{:S(2)}, u32[]{:S(2)}) collective-permute-start(bf16[256,512]{1,0:T(8,128)(2,1)S(1)} %get-tuple-element.163), channel_id=1, source_target_pairs={{0,12},{1,13},{2,14},{3,15},{12,8},{13,9},{14,10},{15,11},{16,28},... | collective-permute-start | bytes 786440 | tf_op jit(solution)/shard_map/ppermute | solution.py:37
  175.0 9.2 %collective-permute-start.26 = (bf16[128,512]{1,0:T(8,128)(2,1)S(1)}, bf16[128,512]{1,0:T(8,128)(2,1)S(1)}, u32[]{:S(2)}, u32[]{:S(2)}) collective-permute-start(bf16[128,512]{1,0:T(8,128)(2,1)S(1)} %get-tuple-element.123), channel_id=1, source_target_pairs={{0,3},{1,0},{2,1},{3,2},{4,7},{5,4},{6,5},{7,6},{8,11},{9,8},{10,9... | collective-permute-start | bytes 393224 | tf_op jit(solution)/shard_map/ppermute | solution.py:37
  178.9 8.4 %collective-permute-start.27 = (bf16[128,512]{1,0:T(8,128)(2,1)S(1)}, bf16[128,512]{1,0:T(8,128)(2,1)S(1)}, u32[]{:S(2)}, u32[]{:S(2)}) collective-permute-start(bf16[128,512]{1,0:T(8,128)(2,1)S(1)} %get-tuple-element.124), channel_id=1, source_target_pairs={{0,2},{1,3},{2,0},{3,1},{4,6},{5,7},{6,4},{7,5},{8,10},{9,11},{10,... | collective-permute-start | bytes 393224 | tf_op jit(solution)/shard_map/ppermute | solution.py:37
  181.8 8.1 %collective-permute-start.28 = (bf16[128,512]{1,0:T(8,128)(2,1)S(1)}, bf16[128,512]{1,0:T(8,128)(2,1)S(1)}, u32[]{:S(2)}, u32[]{:S(2)}) collective-permute-start(bf16[128,512]{1,0:T(8,128)(2,1)S(1)} %get-tuple-element.125), channel_id=1, source_target_pairs={{0,1},{1,2},{2,3},{3,0},{4,5},{5,6},{6,7},{7,4},{8,9},{9,10},{10,1... | collective-permute-start | bytes 393224 | tf_op jit(solution)/shard_map/ppermute | solution.py:37
  187.3 2.6 %copy-start = (bf16[128,2048]{1,0:T(8,128)(2,1)}, bf16[128,2048]{1,0:T(8,128)(2,1)S(1)}, u32[]{:S(2)}) copy-start(bf16[128,2048]{1,0:T(8,128)(2,1)S(1)} %constant_dynamic-update-slice_fusion.8) | copy-start | bytes 1572868

commit v2 on v1

v2 whole, which is shorter than its diff:
```python
import functools

import jax
import jax.numpy as jnp
from jax import lax
from jax.experimental import pallas as pl
from jax.experimental.pallas import tpu as pltpu
from jax.sharding import PartitionSpec as P

HD = 128
BF = jnp.bfloat16
F32 = jnp.float32
masked_value = -1e30
exp2_scale = 0.08838834764831845 * 1.4426950408889634

AXES = ("zl", "y", "c", "zh", "x")
SIZES = (4, 4, 2, 4, 4)
HEADS_X = 4


def exchange(block, axes):
    return lax.all_to_all(block, axes, split_axis=0, concat_axis=0, tiled=True)


def gathered(block, axis, size):
    return exchange(jnp.concatenate([block] * size, 0), axis)


def absorb_tile(q, k, v, state, keep=None):
    peak, total, summed = state
    scores = lax.dot_general(k, q, (((1,), (1,)), ((), ())), preferred_element_type=F32)
    if keep is not None:
        scores = jnp.where(keep, scores, masked_value)
    new_peak = jnp.maximum(peak, jnp.max(scores, axis=0, keepdims=True))
    expo = jnp.exp2((scores - new_peak) * exp2_scale)
    rescale = jnp.exp2((peak - new_peak) * exp2_scale)
    total = total * rescale + jnp.sum(expo, axis=0, keepdims=True)
    summed = summed * rescale + lax.dot_general(
        v, expo.astype(BF), (((0,), (0,)), ((), ())), preferred_element_type=F32
    )
    return new_peak, total, summed


def absorb_pair(refs, q_ref, k, v, keep=None, start=None):
    for g in range(2):
        q = q_ref[:, g * HD : (g + 1) * HD]
        state = start or tuple(ref[g] for ref in refs)
        for ref, part in zip(refs, absorb_tile(q, k, v, state, keep)):
            ref[g] = part


def own_kernel(where_ref, q_ref, ok, ov, *outs):
    refs, where_out = outs[:3], outs[3]
    for n in range(3):
        where_out[n] = where_ref[n]
    rows = q_ref.shape[0]

    key_at = lax.broadcasted_iota(jnp.int32, (rows, rows), 0)
    query_at = lax.broadcasted_iota(jnp.int32, (rows, rows), 1)
    start = (
        jnp.full((1, rows), masked_value, F32),
        jnp.zeros((1, rows), F32),
        jnp.zeros((HD, rows), F32),
    )
    absorb_pair(refs, q_ref, ok[...], ov[...], key_at <= query_at, start)


def middle_kernel(where_ref, q_ref, p_ref, t_ref, s_ref, ak, av, bk, bv, nk, nv, mk, mv, *refs):
    zh, blk = where_ref[1], where_ref[2]
    for ref, before in zip(refs, (p_ref, t_ref, s_ref)):
        ref[...] = before[...]

    @pl.when(blk > 0)
    def _():
        tile = 512

        def step(t, _):
            at = pl.ds(pl.multiple_of(t * tile, tile), tile)
            absorb_pair(refs, q_ref, nk[at, :], nv[at, :])
            absorb_pair(refs, q_ref, mk[at, :], mv[at, :])
            return 0

        lax.fori_loop(0, nk.shape[0] // tile, step, 0)

    @pl.when(zh > 0)
    def _():
        absorb_pair(refs, q_ref, ak[...], av[...])

    @pl.when(zh == 3)
    def _():
        absorb_pair(refs, q_ref, bk[...], bv[...])


def last_kernel(where_ref, q_ref, peak_ref, total_ref, summed_ref, ak, av, bk, bv, out_ref, *own):
    for mine, ref in zip(own, (peak_ref, total_ref, summed_ref)):
        mine[...] = ref[...]

    @pl.when(where_ref[1] > 1)
    def _():
        k = jnp.concatenate([ak[...], bk[...]], 0)
        v = jnp.concatenate([av[...], bv[...]], 0)
        absorb_pair(own, q_ref, k, v)

    for g in range(2):
        out_ref[:, g * HD : (g + 1) * HD] = (own[2][g] / own[1][g]).T.astype(BF)


def head_specs(rows):
    return [
        pl.BlockSpec((rows, HD), lambda h, w: (0, h)),
        pl.BlockSpec((rows, HD), lambda h, w: (0, 2 + h)),
    ]


def state_shapes(heads, rows):
    return [(heads, 1, rows), (heads, 1, rows), (heads, HD, rows)]


def state_specs(rows):
    return [pl.BlockSpec(shape, lambda h, w: (h, 0, 0)) for shape in state_shapes(2, rows)]


def attention_call(body, name, where, q, state, parts, out_specs, out_shape, scratch, share=1):
    rows = q.shape[0]
    keys = sum(part.shape[0] for part in parts)
    in_specs = [pl.BlockSpec((rows, 2 * HD), lambda h, w: (0, h))]
    if state:
        in_specs += state_specs(rows)
    operands = [q, *state]
    for part in parts:
        in_specs += head_specs(part.shape[0])
        operands += [part, part]
    return pl.pallas_call(
        body,
        grid_spec=pltpu.PrefetchScalarGridSpec(
            num_scalar_prefetch=1,
            grid=(2,),
            in_specs=in_specs,
            out_specs=out_specs,
            scratch_shapes=scratch,
        ),
        out_shape=out_shape,
        compiler_params=pltpu.CompilerParams(vmem_limit_bytes=40 * 1024 * 1024),
        cost_estimate=pl.CostEstimate(
            flops=4 * 4 * rows * keys * HD // share, bytes_accessed=(8 << 20) // share, transcendentals=4 * rows * keys // share
        ),
        name=name,
    )(where, *operands)


def own_part(where, q, own):
    rows = q.shape[0]
    return attention_call(
        own_kernel,
        "own_attention",
        where,
        q,
        (),
        (own,),
        state_specs(rows) + [pl.BlockSpec(memory_space=pltpu.SMEM)],
        [jax.ShapeDtypeStruct(shape, F32) for shape in state_shapes(4, rows)]
        + [jax.ShapeDtypeStruct((3,), jnp.int32)],
        [],
        64,
    )


def middle(where, q, state, parts):
    rows = q.shape[0]
    return attention_call(
        middle_kernel,
        "middle_attention",
        where,
        q,
        state,
        parts,
        state_specs(rows),
        [jax.ShapeDtypeStruct(shape, F32) for shape in state_shapes(4, rows)],
        [],
    )


def last(where, q, state, parts):
    rows = q.shape[0]
    return attention_call(
        last_kernel,
        "last_attention",
        where,
        q,
        state,
        parts,
        pl.BlockSpec((rows, 2 * HD), lambda h, w: (0, h)),
        jax.ShapeDtypeStruct((rows, 4 * HD), BF),
        [pltpu.VMEM(shape, F32) for shape in state_shapes(2, rows)],
    )


def local(queries, keys, values):
    zl, y, c, zh, x = (lax.axis_index(name) for name in AXES)
    blk = (zl * SIZES[1] + y) * SIZES[2] + c
    where = jnp.stack([x, zh, blk]).astype(jnp.int32)

    own = exchange(
        jnp.concatenate(
            [
                jnp.concatenate([keys[:, n * 256 : (n + 1) * 256], values[:, n * 256 : (n + 1) * 256]], 1)
                for n in range(HEADS_X)
            ],
            0,
        ),
        "x",
    )
    rows = own.shape[0]

    piece = exchange(own, ("zl", "y", "c"))[: rows // 32]
    strip = gathered(gathered(piece, "zh", 4), "zl", 4)

    half = rows // 2
    own, strip = lax.cond(blk < 32, lambda: (own, strip), lambda: (own - own, strip - strip))
    got_a = lax.ppermute(own, "zh", [(0, 1), (1, 2), (2, 3)])
    got_b = lax.ppermute(own, "zh", [(0, 3), (1, 0)])

    def whole_anchor():
        here = gathered(strip, "y", 4)
        return here, lax.ppermute(here, "c", [(0, 1), (1, 0)]), where

    def no_anchor():
        return (jnp.zeros((1024, 512), BF),) * 2 + (where - 1,)

    here, there, where = lax.cond(blk < 32, whole_anchor, no_anchor)
    q = exchange(
        jnp.concatenate([queries[:, n * 512 : (n + 1) * 512] for n in range(HEADS_X)], 0), "x"
    )
    *state, where = own_part(where, q, own)
    arrived = where[2] >= 0
    got_a2 = lax.ppermute(jnp.where(arrived, got_a[:half], own[:half]), "zh", [(1, 2), (2, 3)])
    got_b2 = lax.ppermute(jnp.where(arrived, got_b[half:], own[half:]), "zh", [(3, 2), (0, 3)])
    state = middle(where, q, state, (got_a, got_b, here, there))
    out = exchange(last(where, q, state, (got_a2, got_b2)), "x")
    width = rows // HEADS_X
    return jnp.concatenate([out[n * width : (n + 1) * width] for n in range(HEADS_X)], 1)


def solution(mesh):
    spec = P(AXES, None)
    split = jax.sharding.Mesh(mesh.devices.reshape(SIZES), AXES)
    return jax.shard_map(local, mesh=split, in_specs=(spec,) * 3, out_specs=spec, check_vma=False)
```

time: 191 us -> 168 us (0.88)
  the two profiles are of different devices: /device:TPU:408 before, /device:TPU:1 now
where the time goes in v2:
time: 168 us
  blocking collectives  102 us (61%)
  waiting for transfers between devices  28.9 us (17%)
  starting transfers between devices  17 us (10%)
  Pallas kernels  15.2 us (9%)
  other arithmetic  1.86 us (1%)
  local copies, waits for them, and re-layouts  1.82 us (1%)
    all_to_all x6, blocking collectives, exchange(): return lax.all_to_all(block, axes, split_axis=0, concat_axis=0, tiled=True)  102 us
    pallas_call x3, Pallas kernels, attention_call(): pl.pallas_call(body, grid_spec=pltpu.PrefetchScalarGridSpec(num_scalar_pr...  15.2 us
    ppermute x1, waiting for transfers between devices, local(): got_b = lax.ppermute(own, 'zh', [(0, 3), (1, 0)])  10.9 us
    ppermute x1, waiting for transfers between devices, local(): lax.ppermute(jnp.where(arrived, got_b[half:], own[half:]), 'zh', [(3, 2),...  7.92 us
    all_to_all x1, waiting for transfers between devices, exchange(): return lax.all_to_all(block, axes, split_axis=0, concat_axis=0, tiled=True)  7.52 us
    ppermute x1, starting transfers between devices, whole_anchor(): return (here, lax.ppermute(here, 'c', [(0, 1), (1, 0)]), where)  5.91 us
    all_to_all x1, starting transfers between devices, exchange(): return lax.all_to_all(block, axes, split_axis=0, concat_axis=0, tiled=True)  4.59 us
  transfers between devices with their start and end apart: 6, of which 4 were waited for; matrix products, arithmetic and copies ran while one was open for 0% of the time, Pallas kernels for 8%

profile of v2, /device:TPU:1, one launch (start us, length us, event | category | flops | bytes accessed | tf_op | source)
XLA Modules:
  0.0 167.6 jit_solution(16984209727170213759)
XLA Ops:
  0.0 1.1 fusion.1
  1.2 11.6 %all_to_all.75 = bf16[4,128,512]{2,1,0:T(8,128)(2,1)S(1)} all-to-all(bf16[4,128,512]{2,1,0:T(8,128)(2,1)S(1)} %bitcast.37), channel_id=1, replica_groups=mesh['zl'=4,'y'=4,'c'=2,'zh'=4,'x'=4] {'x'}, dimensions={0} | all-to-all | bytes 1048576 | tf_op jit(solution)/shard_map/all_to_all | solution.py:22
  12.7 0.0 copy-start
  12.7 28.5 %all_to_all.76 = bf16[32,16,512]{2,1,0:T(8,128)(2,1)S(1)} all-to-all(bf16[32,16,512]{2,1,0:T(8,128)(2,1)S(1)} %bitcast.30), channel_id=1, replica_groups=mesh['zl'=4,'y'=4,'c'=2,'zh'=4,'x'=4] {'zl','y','c'}, dimensions={0} | all-to-all | bytes 1048576 | tf_op jit(solution)/shard_map/all_to_all | solution.py:22
  41.3 23.6 %all_to_all.77 = bf16[4,16,512]{2,1,0:T(8,128)(2,1)S(1)} all-to-all(bf16[4,16,512]{2,1,0:T(8,128)(2,1)S(1)} %bitcast.39), channel_id=1, replica_groups=mesh['zl'=4,'y'=4,'c'=2,'zh'=4,'x'=4] {'zh'}, dimensions={0} | all-to-all | bytes 131072 | tf_op jit(solution)/shard_map/all_to_all | solution.py:22
  64.8 0.7 pad_maximum_fusion.3
  65.6 4.6 %all-to-all-start.4 = ((bf16[4,64,512]{2,1,0:T(8,128)(2,1)}), bf16[4,64,512]{2,1,0:T(8,128)(2,1)S(1)}, u32[]{:S(2)}, u32[]{:S(2)}) async-start(bf16[4,64,512]{2,1,0:T(8,128)(2,1)} %bitcast.11), calls=%async_computation.4 | async-start | bytes 524288 | tf_op jit(solution)/shard_map/all_to_all | solution.py:22
  70.2 0.0 copy-done
  70.2 7.5 %all-to-all-done.4 = bf16[4,64,512]{2,1,0:T(8,128)(2,1)S(1)} async-done(((bf16[4,64,512]{2,1,0:T(8,128)(2,1)}), bf16[4,64,512]{2,1,0:T(8,128)(2,1)S(1)}, u32[]{:S(2)}, u32[]{:S(2)}) %all-to-all-start.4) | async-done | bytes 262176 | tf_op jit(solution)/shard_map/all_to_all | solution.py:22
  77.7 0.1 conditional.2
  77.8 1.3 collective-permute-start.1
  79.1 1.9 %collective-permute-start.2 = (bf16[512,512]{1,0:T(8,128)(2,1)S(1)}, bf16[512,512]{1,0:T(8,128)(2,1)S(1)}, u32[]{:S(2)}, u32[]{:S(2)}) collective-permute-start(bf16[512,512]{1,0:T(8,128)(2,1)S(1)} %get-tuple-element.36.ok.ov), channel_id=1, source_target_pairs={{0,12},{4,0},{1,13},{5,1},{2,14},{6,2},{3,15},{7,3},{16,28},{20,16... | collective-permute-start | bytes 1572872 | tf_op jit(solution)/shard_map/ppermute | solution.py:221
  81.0 0.1 pad_add_fusion
  81.2 23.8 %conditional.3 = (bf16[1024,512]{1,0:T(8,128)(2,1)}, bf16[1024,512]{1,0:T(8,128)(2,1)}, s32[3]{0:T(128)S(1)}) conditional(s32[]{:T(128)} %convert_element_type.4, s32[3]{0:T(128)S(1)} %pad_add_fusion, (bf16[256,512]{1,0:T(8,128)(2,1)S(1)}, s32[3]{0:T(128)S(1)}) %tuple.21), branch_computations={%region_2.0_spmd, %region_3.0_spmd} | conditional | flops 4194304 | bytes 7602240 | solution.py:230
  81.2 0.1 pad_maximum_fusion
  81.3 15.2 %all_to_all.74 = bf16[4,256,512]{2,1,0:T(8,128)(2,1)} all-to-all(bf16[4,256,512]{2,1,0:T(8,128)(2,1)S(1)} %bitcast.35), channel_id=1, replica_groups=mesh['zl'=4,'y'=4,'c'=2,'zh'=4,'x'=4] {'y'}, dimensions={0} | all-to-all | bytes 2097152 | tf_op jit(solution)/shard_map/cond/branch_1_fun/all_to_all | solution.py:22
  96.4 5.9 %collective-permute-start = (bf16[1024,512]{1,0:T(8,128)(2,1)}, bf16[1024,512]{1,0:T(8,128)(2,1)}, u32[]{:S(2)}, u32[]{:S(2)}) collective-permute-start(bf16[1024,512]{1,0:T(8,128)(2,1)} %bitcast.1), channel_id=1, source_target_pairs={{0,16},{16,0},{1,17},{17,1},{2,18},{18,2},{3,19},{19,3},{4,20},{20... | collective-permute-start | bytes 3145736 | tf_op jit(solution)/shard_map/cond/branch_1_fun/ppermute | solution.py:225
  102.4 2.6 %collective-permute-done = bf16[1024,512]{1,0:T(8,128)(2,1)} collective-permute-done((bf16[1024,512]{1,0:T(8,128)(2,1)}, bf16[1024,512]{1,0:T(8,128)(2,1)}, u32[]{:S(2)}, u32[]{:S(2)}) %collective-permute-start) | collective-permute-done | bytes 1048608 | tf_op jit(solution)/shard_map/cond/branch_1_fun/ppermute | solution.py:225
  105.0 11.6 %all_to_all.78 = bf16[4,128,512]{2,1,0:T(8,128)(2,1)S(1)} all-to-all(bf16[4,128,512]{2,1,0:T(8,128)(2,1)S(1)} %bitcast.36), channel_id=1, replica_groups=mesh['zl'=4,'y'=4,'c'=2,'zh'=4,'x'=4] {'x'}, dimensions={0} | all-to-all | bytes 1048576 | tf_op jit(solution)/shard_map/all_to_all | solution.py:22
  116.6 2.9 %own_attention.1 = (f32[4,1,512]{2,1,0:T(1,128)S(1)}, f32[4,1,512]{2,1,0:T(1,128)S(1)}, f32[4,128,512]{2,1,0:T(8,128)S(1)}, s32[3]{0:T(128)S(1)}) custom-call(s32[3]{0:T(128)S(1)} %get-tuple-element.35.where_ref, bf16[512,512]{1,0:T(8,128)(2,1)S(1)} %bitcast.26, bf16[512,512]{1,0:T(8,128)(2,1)S(1)} %get-tuple-element.36.ok.ov, ...), custom_call_target="tpu_custom_call" | custom-call | flops 8388608 | bytes 131072 | tf_op jit(solution)/shard_map/own_attention/pallas_call | solution.py:133
  119.5 0.6 slice.95
  120.8 0.0 collective-permute-done.1.ak.av
  120.8 10.9 %collective-permute-done.2.bk.bv = bf16[512,512]{1,0:T(8,128)(2,1)S(1)} collective-permute-done((bf16[512,512]{1,0:T(8,128)(2,1)S(1)}, bf16[512,512]{1,0:T(8,128)(2,1)S(1)}, u32[]{:S(2)}, u32[]{:S(2)}) %collective-permute-start.2) | collective-permute-done | bytes 524320 | tf_op jit(solution)/shard_map/ppermute | solution.py:221
  131.7 0.1 slice_select_fusion
  131.7 0.7 collective-permute-start.3
  132.4 2.6 %collective-permute-start.4 = (bf16[256,512]{1,0:T(8,128)(2,1)S(1)}, bf16[256,512]{1,0:T(8,128)(2,1)S(1)}, u32[]{:S(2)}, u32[]{:S(2)}) collective-permute-start(bf16[256,512]{1,0:T(8,128)(2,1)S(1)} %get-tuple-element.50), channel_id=1, source_target_pairs={{12,8},{0,12},{13,9},{1,13},{14,10},{2,14},{15,11},{3,15},{28,24},... | collective-permute-start | bytes 786440 | tf_op jit(solution)/shard_map/ppermute | solution.py:237
  135.0 11.1 %middle_attention.1 = (f32[4,1,512]{2,1,0:T(1,128)S(1)}, f32[4,1,512]{2,1,0:T(1,128)S(1)}, f32[4,128,512]{2,1,0:T(8,128)S(1)}) custom-call(s32[3]{0:T(128)S(1)} %get-tuple-element.37.where_ref, bf16[512,512]{1,0:T(8,128)(2,1)S(1)} %bitcast.27, f32[4,1,512]{2,1,0:T(1,128)S(1)} %get-tuple-element.38.p_ref, f32[4,1,512]{2,1,0:T(1,128)S(1)} %get-tuple-element.39.t_ref, ...), custom_call_target="tpu_custom_call" | custom-call | flops 3221225472 | bytes 8388608 | tf_op jit(solution)/shard_map/middle_attention/pallas_call | solution.py:133
  146.1 0.0 collective-permute-done.3.ak.av
  146.1 7.9 %collective-permute-done.4.bk.bv = bf16[256,512]{1,0:T(8,128)(2,1)S(1)} collective-permute-done((bf16[256,512]{1,0:T(8,128)(2,1)S(1)}, bf16[256,512]{1,0:T(8,128)(2,1)S(1)}, u32[]{:S(2)}, u32[]{:S(2)}) %collective-permute-start.4) | collective-permute-done | bytes 262176 | tf_op jit(solution)/shard_map/ppermute | solution.py:237
  154.0 1.2 last_attention.1
  155.2 11.5 %all_to_all.79 = bf16[4,128,512]{2,1,0:T(8,128)(2,1)S(1)} all-to-all(bf16[4,128,512]{2,1,0:T(8,128)(2,1)S(1)} %bitcast.29), channel_id=1, replica_groups=mesh['zl'=4,'y'=4,'c'=2,'zh'=4,'x'=4] {'x'}, dimensions={0} | all-to-all | bytes 1048576 | tf_op jit(solution)/shard_map/all_to_all | solution.py:22
  166.7 0.8 pad_maximum_fusion.2
  (8 shorter events, 0.2 us)
Async XLA Ops:
  12.7 57.4 %copy-start = (bf16[128,2048]{1,0:T(8,128)(2,1)S(1)}, bf16[128,2048]{1,0:T(8,128)(2,1)}, u32[]{:S(2)}) copy-start(bf16[128,2048]{1,0:T(8,128)(2,1)} %param.7) | copy-start | bytes 1572868
  65.6 12.2 %all-to-all-start.4 = ((bf16[4,64,512]{2,1,0:T(8,128)(2,1)}), bf16[4,64,512]{2,1,0:T(8,128)(2,1)S(1)}, u32[]{:S(2)}, u32[]{:S(2)}) async-start(bf16[4,64,512]{2,1,0:T(8,128)(2,1)} %bitcast.11), calls=%async_computation.4 | async-start | bytes 524288 | tf_op jit(solution)/shard_map/all_to_all | solution.py:22
  77.8 43.0 %collective-permute-start.1 = (bf16[512,512]{1,0:T(8,128)(2,1)S(1)}, bf16[512,512]{1,0:T(8,128)(2,1)S(1)}, u32[]{:S(2)}, u32[]{:S(2)}) collective-permute-start(bf16[512,512]{1,0:T(8,128)(2,1)S(1)} %get-tuple-element.36.ok.ov), channel_id=1, source_target_pairs={{0,4},{4,8},{8,12},{1,5},{5,9},{9,13},{2,6},{6,10},{10,14},{3,7},{... | collective-permute-start | bytes 1572872 | tf_op jit(solution)/shard_map/ppermute | solution.py:220
  79.1 52.5 %collective-permute-start.2 = (bf16[512,512]{1,0:T(8,128)(2,1)S(1)}, bf16[512,512]{1,0:T(8,128)(2,1)S(1)}, u32[]{:S(2)}, u32[]{:S(2)}) collective-permute-start(bf16[512,512]{1,0:T(8,128)(2,1)S(1)} %get-tuple-element.36.ok.ov), channel_id=1, source_target_pairs={{0,12},{4,0},{1,13},{5,1},{2,14},{6,2},{3,15},{7,3},{16,28},{20,16... | collective-permute-start | bytes 1572872 | tf_op jit(solution)/shard_map/ppermute | solution.py:221
  96.4 8.5 %collective-permute-start = (bf16[1024,512]{1,0:T(8,128)(2,1)}, bf16[1024,512]{1,0:T(8,128)(2,1)}, u32[]{:S(2)}, u32[]{:S(2)}) collective-permute-start(bf16[1024,512]{1,0:T(8,128)(2,1)} %bitcast.1), channel_id=1, source_target_pairs={{0,16},{16,0},{1,17},{17,1},{2,18},{18,2},{3,19},{19,3},{4,20},{20... | collective-permute-start | bytes 3145736 | tf_op jit(solution)/shard_map/cond/branch_1_fun/ppermute | solution.py:225
  131.7 14.4 %collective-permute-start.3 = (bf16[256,512]{1,0:T(8,128)(2,1)S(1)}, bf16[256,512]{1,0:T(8,128)(2,1)S(1)}, u32[]{:S(2)}, u32[]{:S(2)}) collective-permute-start(bf16[256,512]{1,0:T(8,128)(2,1)S(1)} %get-tuple-element.51), channel_id=1, source_target_pairs={{4,8},{8,12},{5,9},{9,13},{6,10},{10,14},{7,11},{11,15},{20,24},{2... | collective-permute-start | bytes 786440 | tf_op jit(solution)/shard_map/ppermute | solution.py:236
  132.4 21.6 %collective-permute-start.4 = (bf16[256,512]{1,0:T(8,128)(2,1)S(1)}, bf16[256,512]{1,0:T(8,128)(2,1)S(1)}, u32[]{:S(2)}, u32[]{:S(2)}) collective-permute-start(bf16[256,512]{1,0:T(8,128)(2,1)S(1)} %get-tuple-element.50), channel_id=1, source_target_pairs={{12,8},{0,12},{13,9},{1,13},{14,10},{2,14},{15,11},{3,15},{28,24},... | collective-permute-start | bytes 786440 | tf_op jit(solution)/shard_map/ppermute | solution.py:237

commit v3 on v2

--- a/solution.py
+++ b/solution.py
@@ -26,43 +26,56 @@
     return exchange(jnp.concatenate([block] * size, 0), axis)
 
 
-def absorb_tile(q, k, v, state, keep=None):
-    peak, total, summed = state
-    scores = lax.dot_general(k, q, (((1,), (1,)), ((), ())), preferred_element_type=F32)
-    if keep is not None:
-        scores = jnp.where(keep, scores, masked_value)
-    new_peak = jnp.maximum(peak, jnp.max(scores, axis=0, keepdims=True))
-    expo = jnp.exp2((scores - new_peak) * exp2_scale)
-    rescale = jnp.exp2((peak - new_peak) * exp2_scale)
-    total = total * rescale + jnp.sum(expo, axis=0, keepdims=True)
-    summed = summed * rescale + lax.dot_general(
-        v, expo.astype(BF), (((0,), (0,)), ((), ())), preferred_element_type=F32
-    )
-    return new_peak, total, summed
-
-
-def absorb_pair(refs, q_ref, k, v, keep=None, start=None):
-    for g in range(2):
-        q = q_ref[:, g * HD : (g + 1) * HD]
-        state = start or tuple(ref[g] for ref in refs)
-        for ref, part in zip(refs, absorb_tile(q, k, v, state, keep)):
-            ref[g] = part
+def absorb(refs, q_ref, tiles, causal=False):
+    rows = q_ref.shape[0]
+    width = rows // 2
+    chains = [(g, n) for g in range(2) for n in range(2)]
+
+    def scores_of(chain):
+        g, n = chain
+        q = q_ref[n * width : (n + 1) * width, g * HD : (g + 1) * HD]
+        found = []
+        for k, _ in tiles:
+            k = k[: (n + 1) * width] if causal else k[...]
+            found.append(lax.dot_general(k, q, (((1,), (1,)), ((), ())), preferred_element_type=F32))
+        if causal:
+            key_at = lax.broadcasted_iota(jnp.int32, found[0].shape, 0)
+            query_at = lax.broadcasted_iota(jnp.int32, found[0].shape, 1) + n * width
+            found = [jnp.where(key_at <= query_at, found[0], masked_value)]
+        return found
+
+    following = scores_of(chains[0])
+    for at, (g, n) in enumerate(chains):
+        found = following
+        if at + 1 < len(chains):
+            following = scores_of(chains[at + 1])
+        columns = slice(n * width, (n + 1) * width)
+        new_peak = functools.reduce(
+            jnp.maximum, [jnp.max(scores, axis=0, keepdims=True) for scores in found]
+        )
+        if not causal:
+            peak, total, summed = (ref[g, :, columns] for ref in refs)
+            new_peak = jnp.maximum(peak, new_peak)
+            rescale = jnp.exp2((peak - new_peak) * exp2_scale)
+            new_total, new_summed = total * rescale, summed * rescale
+        else:
+            new_total, new_summed = 0.0, 0.0
+        for scores, (_, v) in zip(found, tiles):
+            expo = jnp.exp2((scores - new_peak) * exp2_scale)
+            v = v[: (n + 1) * width] if causal else v[...]
+            new_total += jnp.sum(expo, axis=0, keepdims=True)
+            new_summed += lax.dot_general(
+                v, expo.astype(BF), (((0,), (0,)), ((), ())), preferred_element_type=F32
+            )
+        for ref, part in zip(refs, (new_peak, new_total, new_summed)):
+            ref[g, :, columns] = part
 
 
 def own_kernel(where_ref, q_ref, ok, ov, *outs):
     refs, where_out = outs[:3], outs[3]
     for n in range(3):
         where_out[n] = where_ref[n]
-    rows = q_ref.shape[0]
-
-    key_at = lax.broadcasted_iota(jnp.int32, (rows, rows), 0)
-    query_at = lax.broadcasted_iota(jnp.int32, (rows, rows), 1)
-    start = (
-        jnp.full((1, rows), masked_value, F32),
-        jnp.zeros((1, rows), F32),
-        jnp.zeros((HD, rows), F32),
-    )
-    absorb_pair(refs, q_ref, ok[...], ov[...], key_at <= query_at, start)
+    absorb(refs, q_ref, [(ok, ov)], causal=True)
 
 
 def middle_kernel(where_ref, q_ref, p_ref, t_ref, s_ref, ak, av, bk, bv, nk, nv, mk, mv, *refs):
@@ -76,19 +89,18 @@
 
         def step(t, _):
             at = pl.ds(pl.multiple_of(t * tile, tile), tile)
-            absorb_pair(refs, q_ref, nk[at, :], nv[at, :])
-            absorb_pair(refs, q_ref, mk[at, :], mv[at, :])
+            absorb(refs, q_ref, [(nk[at, :], nv[at, :]), (mk[at, :], mv[at, :])])
             return 0
 
         lax.fori_loop(0, nk.shape[0] // tile, step, 0)
 
-    @pl.when(zh > 0)
-    def _():
-        absorb_pair(refs, q_ref, ak[...], av[...])
+    @pl.when(jnp.logical_and(zh > 0, zh < 3))
+    def _():
+        absorb(refs, q_ref, [(ak, av)])
 
     @pl.when(zh == 3)
     def _():
-        absorb_pair(refs, q_ref, bk[...], bv[...])
+        absorb(refs, q_ref, [(ak, av), (bk, bv)])
 
 
 def last_kernel(where_ref, q_ref, peak_ref, total_ref, summed_ref, ak, av, bk, bv, out_ref, *own):
@@ -97,9 +109,7 @@
 
     @pl.when(where_ref[1] > 1)
     def _():
-        k = jnp.concatenate([ak[...], bk[...]], 0)
-        v = jnp.concatenate([av[...], bv[...]], 0)
-        absorb_pair(own, q_ref, k, v)
+        absorb(own, q_ref, [(ak, av), (bk, bv)])
 
     for g in range(2):
         out_ref[:, g * HD : (g + 1) * HD] = (own[2][g] / own[1][g]).T.astype(BF)
@@ -177,6 +187,7 @@
         state_specs(rows),
         [jax.ShapeDtypeStruct(shape, F32) for shape in state_shapes(4, rows)],
         [],
+        10**6,
     )
 
 
@@ -212,29 +223,33 @@
     )
     rows = own.shape[0]
 
-    piece = exchange(own, ("zl", "y", "c"))[: rows // 32]
-    strip = gathered(gathered(piece, "zh", 4), "zl", 4)
-
     half = rows // 2
-    own, strip = lax.cond(blk < 32, lambda: (own, strip), lambda: (own - own, strip - strip))
     got_a = lax.ppermute(own, "zh", [(0, 1), (1, 2), (2, 3)])
     got_b = lax.ppermute(own, "zh", [(0, 3), (1, 0)])
 
-    def whole_anchor():
-        here = gathered(strip, "y", 4)
-        return here, lax.ppermute(here, "c", [(0, 1), (1, 0)]), where
-
-    def no_anchor():
-        return (jnp.zeros((1024, 512), BF),) * 2 + (where - 1,)
-
-    here, there, where = lax.cond(blk < 32, whole_anchor, no_anchor)
+    piece, where = lax.cond(
+        blk < 32,
+        lambda: (exchange(own, ("zl", "y", "c"))[: rows // 32], where),
+        lambda: (jnp.zeros((rows // 32, 512), BF), where - 1),
+    )
     q = exchange(
         jnp.concatenate([queries[:, n * 512 : (n + 1) * 512] for n in range(HEADS_X)], 0), "x"
     )
     *state, where = own_part(where, q, own)
+    strip, where = lax.cond(
+        where[2] < 32,
+        lambda: (gathered(piece, ("zl", "zh"), 16), where),
+        lambda: (jnp.zeros((rows // 2, 512), BF), where - 1),
+    )
     arrived = where[2] >= 0
     got_a2 = lax.ppermute(jnp.where(arrived, got_a[:half], own[:half]), "zh", [(1, 2), (2, 3)])
     got_b2 = lax.ppermute(jnp.where(arrived, got_b[half:], own[half:]), "zh", [(3, 2), (0, 3)])
+
+    def whole_anchor():
+        here = gathered(strip, "y", 4)
+        return here, lax.ppermute(here, "c", [(0, 1), (1, 0)])
+
+    here, there = lax.cond(blk < 32, whole_anchor, lambda: (jnp.zeros((1024, 512), BF),) * 2)
     state = middle(where, q, state, (got_a, got_b, here, there))
     out = exchange(last(where, q, state, (got_a2, got_b2)), "x")
     width = rows // HEADS_X

time: 168 us -> 178 us (1.060)
  the two profiles are of different devices: /device:TPU:1 before, /device:TPU:416 now
where the time goes in v3:
time: 178 us
  blocking collectives  108 us (61%)
  starting transfers between devices  22 us (12%)
  waiting for transfers between devices  19.5 us (11%)
  Pallas kernels  19.3 us (11%)
  other arithmetic  4.16 us (2%)
  local copies, waits for them, and re-layouts  3.47 us (2%)
    all_to_all x4, blocking collectives, exchange(): return lax.all_to_all(block, axes, split_axis=0, concat_axis=0, tiled=True)  108 us
    pallas_call x3, Pallas kernels, attention_call(): pl.pallas_call(body, grid_spec=pltpu.PrefetchScalarGridSpec(num_scalar_pr...  19.3 us
    all_to_all x2, waiting for transfers between devices, exchange(): return lax.all_to_all(block, axes, split_axis=0, concat_axis=0, tiled=True)  16.5 us
    ppermute x1, starting transfers between devices, local(): lax.ppermute(jnp.where(arrived, got_b[half:], own[half:]), 'zh', [(3, 2),...  8.44 us
    all_to_all x2, starting transfers between devices, exchange(): return lax.all_to_all(block, axes, split_axis=0, concat_axis=0, tiled=True)  7.76 us
  transfers between devices with their start and end apart: 7, of which 3 were waited for; matrix products, arithmetic and copies ran while one was open for 3% of the time, Pallas kernels for 9%

profile of v3, /device:TPU:416, one launch (start us, length us, event | category | flops | bytes accessed | tf_op | source)
XLA Modules:
  0.0 177.5 jit_solution(2517971893353280888)
XLA Ops:
  0.0 1.1 fusion.2
  1.1 0.0 copy-start
  1.1 0.8 maximum_maximum_fusion
  2.0 4.3 %all-to-all-start.3 = ((bf16[4,128,512]{2,1,0:T(8,128)(2,1)}), bf16[4,128,512]{2,1,0:T(8,128)(2,1)}, u32[]{:S(2)}, u32[]{:S(2)}) async-start(bf16[4,128,512]{2,1,0:T(8,128)(2,1)} %bitcast.9), calls=%async_computation.3 | async-start | bytes 1048576 | tf_op jit(solution)/shard_map/all_to_all | solution.py:22
  6.2 0.1 pad_add_fusion
  6.4 0.8 pad_maximum_fusion.1
  7.2 8.7 %all-to-all-done.3 = bf16[4,128,512]{2,1,0:T(8,128)(2,1)} async-done(((bf16[4,128,512]{2,1,0:T(8,128)(2,1)}), bf16[4,128,512]{2,1,0:T(8,128)(2,1)}, u32[]{:S(2)}, u32[]{:S(2)}) %all-to-all-start.3) | async-done | bytes 524320 | tf_op jit(solution)/shard_map/all_to_all | solution.py:22
  15.9 22.3 %conditional.3 = (bf16[16,512]{1,0:T(8,128)(2,1)S(1)}, s32[3]{0:T(128)S(1)}) conditional(s32[]{:T(128)} %convert_element_type.10, s32[3]{0:T(128)S(1)} %pad_add_fusion, (bf16[512,512]{1,0:T(8,128)(2,1)}, s32[3]{0:T(128)S(1)}) %tuple.33), branch_computations={%region_0.0_spmd, %region_1.0_spmd} | conditional | flops 3 | bytes 1081360 | solution.py:230
  15.9 22.3 %all_to_all.56 = bf16[32,16,512]{2,1,0:T(8,128)(2,1)S(1)} all-to-all(bf16[32,16,512]{2,1,0:T(8,128)(2,1)} %bitcast), channel_id=1, replica_groups=mesh['zl'=4,'y'=4,'c'=2,'zh'=4,'x'=4] {'zl','y','c'}, dimensions={0} | all-to-all | bytes 1048576 | tf_op jit(solution)/shard_map/cond/branch_1_fun/all_to_all | solution.py:22
  38.3 3.5 %all-to-all-start.4 = ((bf16[4,128,512]{2,1,0:T(8,128)(2,1)}), bf16[4,128,512]{2,1,0:T(8,128)(2,1)S(1)}, u32[]{:S(2)}, u32[]{:S(2)}) async-start(bf16[4,128,512]{2,1,0:T(8,128)(2,1)} %bitcast.11), calls=%async_computation.4 | async-start | bytes 1048576 | tf_op jit(solution)/shard_map/all_to_all | solution.py:22
  41.7 1.3 collective-permute-start.1
  43.0 1.3 collective-permute-start.2
  44.3 7.8 %all-to-all-done.4 = bf16[4,128,512]{2,1,0:T(8,128)(2,1)S(1)} async-done(((bf16[4,128,512]{2,1,0:T(8,128)(2,1)}), bf16[4,128,512]{2,1,0:T(8,128)(2,1)S(1)}, u32[]{:S(2)}, u32[]{:S(2)}) %all-to-all-start.4) | async-done | bytes 524320 | tf_op jit(solution)/shard_map/all_to_all | solution.py:22
  52.1 3.5 %own_attention.1 = (f32[4,1,512]{2,1,0:T(1,128)S(1)}, f32[4,1,512]{2,1,0:T(1,128)S(1)}, f32[4,128,512]{2,1,0:T(8,128)S(1)}, s32[3]{0:T(128)S(1)}) custom-call(s32[3]{0:T(128)S(1)} %get-tuple-element.34.where_ref, bf16[512,512]{1,0:T(8,128)(2,1)S(1)} %bitcast.29, bf16[512,512]{1,0:T(8,128)(2,1)} %bitcast.10.ok.ov, bf16[512,512]{1,0:T(8,128)(2,1)} %bitcast.10.ok.ov), custom_call_target="tpu_custom_call" | custom-call | flops 8388608 | bytes 131072 | tf_op jit(solution)/shard_map/own_attention/pallas_call | solution.py:143
  55.6 0.6 slice.102
  56.9 54.1 %conditional.4 = (s32[3]{0:T(128)S(1)}, bf16[256,512]{1,0:T(8,128)(2,1)S(1)}) conditional(s32[]{:T(128)} %bitcast.13, s32[3]{0:T(128)S(1)} %get-tuple-element.35, (bf16[16,512]{1,0:T(8,128)(2,1)S(1)}, s32[3]{0:T(128)S(1)}) %tuple.34), branch_computations={%region_2.0_spmd, %region_3.0_spmd} | conditional | flops 3 | bytes 1048592 | solution.py:239
  57.1 53.9 %all_to_all.57 = bf16[16,16,512]{2,1,0:T(8,128)(2,1)S(1)} all-to-all(bf16[16,16,512]{2,1,0:T(8,128)(2,1)S(1)} %bitcast.35), channel_id=1, replica_groups=mesh['zl'=4,'y'=4,'c'=2,'zh'=4,'x'=4] {'zl','zh'}, dimensions={0} | all-to-all | bytes 524288 | tf_op jit(solution)/shard_map/cond/branch_1_fun/all_to_all | solution.py:22
  111.0 0.6 slice.103
  112.2 1.1 fusion
  113.3 0.8 slice_select_fusion.1
  114.1 1.3 collective-permute-start.3
  115.4 0.7 slice_select_fusion
  116.1 8.4 %collective-permute-start.4 = (bf16[256,512]{1,0:T(8,128)(2,1)}, bf16[256,512]{1,0:T(8,128)(2,1)S(1)}, u32[]{:S(2)}, u32[]{:S(2)}) collective-permute-start(bf16[256,512]{1,0:T(8,128)(2,1)} %slice_select_fusion), channel_id=1, source_target_pairs={{12,8},{0,12},{13,9},{1,13},{14,10},{2,14},{15,11},{3,15},{28,24},... | collective-permute-start | bytes 786440 | tf_op jit(solution)/shard_map/ppermute | solution.py:246
  124.6 22.2 %conditional.5 = (bf16[1024,512]{1,0:T(8,128)(2,1)}, bf16[1024,512]{1,0:T(8,128)(2,1)}) conditional(s32[]{:T(128)} %convert_element_type.10, () %tuple.35, bf16[256,512]{1,0:T(8,128)(2,1)S(1)} %get-tuple-element.41), branch_computations={%region_4.5_spmd, %region_5.6_spmd} | conditional | flops 4194304 | bytes 7602232 | solution.py:252
  124.6 0.1 pad_maximum_fusion
  124.6 17.3 %all_to_all.58 = bf16[4,256,512]{2,1,0:T(8,128)(2,1)} all-to-all(bf16[4,256,512]{2,1,0:T(8,128)(2,1)S(1)} %bitcast.33), channel_id=1, replica_groups=mesh['zl'=4,'y'=4,'c'=2,'zh'=4,'x'=4] {'y'}, dimensions={0} | all-to-all | bytes 2097152 | tf_op jit(solution)/shard_map/cond/branch_1_fun/all_to_all | solution.py:22
  141.9 1.9 %collective-permute-start = (bf16[1024,512]{1,0:T(8,128)(2,1)}, bf16[1024,512]{1,0:T(8,128)(2,1)}, u32[]{:S(2)}, u32[]{:S(2)}) collective-permute-start(bf16[1024,512]{1,0:T(8,128)(2,1)} %bitcast.5), channel_id=1, source_target_pairs={{0,16},{16,0},{1,17},{17,1},{2,18},{18,2},{3,19},{19,3},{4,20},{20... | collective-permute-start | bytes 3145736 | tf_op jit(solution)/shard_map/cond/branch_1_fun/ppermute | solution.py:250
  143.8 3.0 %collective-permute-done = bf16[1024,512]{1,0:T(8,128)(2,1)} collective-permute-done((bf16[1024,512]{1,0:T(8,128)(2,1)}, bf16[1024,512]{1,0:T(8,128)(2,1)}, u32[]{:S(2)}, u32[]{:S(2)}) %collective-permute-start) | collective-permute-done | bytes 1048608 | tf_op jit(solution)/shard_map/cond/branch_1_fun/ppermute | solution.py:250
  146.8 12.5 %middle_attention.1 = (f32[4,1,512]{2,1,0:T(1,128)S(1)}, f32[4,1,512]{2,1,0:T(1,128)S(1)}, f32[4,128,512]{2,1,0:T(8,128)S(1)}) custom-call(s32[3]{0:T(128)S(1)} %get-tuple-element.37.where_ref, bf16[512,512]{1,0:T(8,128)(2,1)S(1)} %bitcast.30, f32[4,1,512]{2,1,0:T(1,128)S(1)} %get-tuple-element.38.p_ref, f32[4,1,512]{2,1,0:T(1,128)S(1)} %get-tuple-element.39.t_ref, ...), custom_call_target="tpu_custom_call" | custom-call | flops 3221 | bytes 8 | tf_op jit(solution)/shard_map/middle_attention/pallas_call | solution.py:143
  159.3 3.3 %last_attention.1 = bf16[512,512]{1,0:T(8,128)(2,1)S(1)} custom-call(s32[3]{0:T(128)S(1)} %get-tuple-element.37.where_ref, bf16[512,512]{1,0:T(8,128)(2,1)S(1)} %bitcast.31, f32[4,1,512]{2,1,0:T(1,128)S(1)} %get-tuple-element.44.peak_ref, f32[4,1,512]{2,1,0:T(1,128)S(1)} %get-tuple-element.45.total_ref, f32[4,128,512]{2,1,0:T(8,128)S(1)} %get-tuple-element.46.summed_ref, ...), custom_call_target="tpu_custom_call" | custom-call | flops 536870912 | bytes 8388608 | tf_op jit(solution)/shard_map/last_attention/pallas_call | solution.py:143
  162.6 14.0 %all_to_all.59 = bf16[4,128,512]{2,1,0:T(8,128)(2,1)S(1)} all-to-all(bf16[4,128,512]{2,1,0:T(8,128)(2,1)S(1)} %bitcast.32), channel_id=1, replica_groups=mesh['zl'=4,'y'=4,'c'=2,'zh'=4,'x'=4] {'x'}, dimensions={0} | all-to-all | bytes 1048576 | tf_op jit(solution)/shard_map/all_to_all | solution.py:22
  176.7 0.8 pad_maximum_fusion.2
  (24 shorter events, 0.1 us)
Async XLA Ops:
  1.1 5.2 %copy-start = (bf16[128,2048]{1,0:T(8,128)(2,1)S(1)}, bf16[128,2048]{1,0:T(8,128)(2,1)}, u32[]{:S(2)}) copy-start(bf16[128,2048]{1,0:T(8,128)(2,1)} %param.9) | copy-start | bytes 1572868
  2.0 14.0 %all-to-all-start.3 = ((bf16[4,128,512]{2,1,0:T(8,128)(2,1)}), bf16[4,128,512]{2,1,0:T(8,128)(2,1)}, u32[]{:S(2)}, u32[]{:S(2)}) async-start(bf16[4,128,512]{2,1,0:T(8,128)(2,1)} %bitcast.9), calls=%async_computation.3 | async-start | bytes 1048576 | tf_op jit(solution)/shard_map/all_to_all | solution.py:22
  38.3 13.9 %all-to-all-start.4 = ((bf16[4,128,512]{2,1,0:T(8,128)(2,1)}), bf16[4,128,512]{2,1,0:T(8,128)(2,1)S(1)}, u32[]{:S(2)}, u32[]{:S(2)}) async-start(bf16[4,128,512]{2,1,0:T(8,128)(2,1)} %bitcast.11), calls=%async_computation.4 | async-start | bytes 1048576 | tf_op jit(solution)/shard_map/all_to_all | solution.py:22
  41.7 71.6 %collective-permute-start.1 = (bf16[512,512]{1,0:T(8,128)(2,1)}, bf16[512,512]{1,0:T(8,128)(2,1)S(1)}, u32[]{:S(2)}, u32[]{:S(2)}) collective-permute-start(bf16[512,512]{1,0:T(8,128)(2,1)} %bitcast.10.ok.ov), channel_id=1, source_target_pairs={{0,4},{4,8},{8,12},{1,5},{5,9},{9,13},{2,6},{6,10},{10,14},{3,7},{... | collective-permute-start | bytes 1572872 | tf_op jit(solution)/shard_map/ppermute | solution.py:227
  43.0 72.3 %collective-permute-start.2 = (bf16[512,512]{1,0:T(8,128)(2,1)}, bf16[512,512]{1,0:T(8,128)(2,1)S(1)}, u32[]{:S(2)}, u32[]{:S(2)}) collective-permute-start(bf16[512,512]{1,0:T(8,128)(2,1)} %bitcast.10.ok.ov), channel_id=1, source_target_pairs={{0,12},{4,0},{1,13},{5,1},{2,14},{6,2},{3,15},{7,3},{16,28},{20,16... | collective-permute-start | bytes 1572872 | tf_op jit(solution)/shard_map/ppermute | solution.py:228
  114.1 45.2 %collective-permute-start.3 = (bf16[256,512]{1,0:T(8,128)(2,1)}, bf16[256,512]{1,0:T(8,128)(2,1)S(1)}, u32[]{:S(2)}, u32[]{:S(2)}) collective-permute-start(bf16[256,512]{1,0:T(8,128)(2,1)} %slice_select_fusion.1), channel_id=1, source_target_pairs={{4,8},{8,12},{5,9},{9,13},{6,10},{10,14},{7,11},{11,15},{20,24},{2... | collective-permute-start | bytes 786440 | tf_op jit(solution)/shard_map/ppermute | solution.py:245
  116.1 43.2 %collective-permute-start.4 = (bf16[256,512]{1,0:T(8,128)(2,1)}, bf16[256,512]{1,0:T(8,128)(2,1)S(1)}, u32[]{:S(2)}, u32[]{:S(2)}) collective-permute-start(bf16[256,512]{1,0:T(8,128)(2,1)} %slice_select_fusion), channel_id=1, source_target_pairs={{12,8},{0,12},{13,9},{1,13},{14,10},{2,14},{15,11},{3,15},{28,24},... | collective-permute-start | bytes 786440 | tf_op jit(solution)/shard_map/ppermute | solution.py:246
  141.9 4.9 %collective-permute-start = (bf16[1024,512]{1,0:T(8,128)(2,1)}, bf16[1024,512]{1,0:T(8,128)(2,1)}, u32[]{:S(2)}, u32[]{:S(2)}) collective-permute-start(bf16[1024,512]{1,0:T(8,128)(2,1)} %bitcast.5), channel_id=1, source_target_pairs={{0,16},{16,0},{1,17},{17,1},{2,18},{18,2},{3,19},{19,3},{4,20},{20... | collective-permute-start | bytes 3145736 | tf_op jit(solution)/shard_map/cond/branch_1_fun/ppermute | solution.py:250

commit v4 on v3

--- a/solution.py
+++ b/solution.py
@@ -1,4 +1,5 @@
 import functools
+import itertools
 
 import jax
 import jax.numpy as jnp
@@ -71,10 +72,7 @@
             ref[g, :, columns] = part
 
 
-def own_kernel(where_ref, q_ref, ok, ov, *outs):
-    refs, where_out = outs[:3], outs[3]
-    for n in range(3):
-        where_out[n] = where_ref[n]
+def own_kernel(where_ref, q_ref, ok, ov, *refs):
     absorb(refs, q_ref, [(ok, ov)], causal=True)
 
 
@@ -167,9 +165,8 @@
         q,
         (),
         (own,),
-        state_specs(rows) + [pl.BlockSpec(memory_space=pltpu.SMEM)],
-        [jax.ShapeDtypeStruct(shape, F32) for shape in state_shapes(4, rows)]
-        + [jax.ShapeDtypeStruct((3,), jnp.int32)],
+        state_specs(rows),
+        [jax.ShapeDtypeStruct(shape, F32) for shape in state_shapes(4, rows)],
         [],
         64,
     )
@@ -206,50 +203,104 @@
     )
 
 
+def device_index(zl, y, c, zh, x):
+    return (((zl * 4 + y) * 2 + c) * 4 + zh) * 4 + x
+
+
+def send(block, move):
+    places = itertools.product(*(range(size) for size in SIZES))
+    moves = [(place, move(*place)) for place in places]
+    return lax.ppermute(
+        block, AXES, [(device_index(*place), device_index(*to)) for place, to in moves if to is not None]
+    )
+
+
+def of_heads(block):
+    width = block.shape[1] // 2
+    return jnp.concatenate(
+        [
+            jnp.concatenate(
+                [block[:, n * 256 : (n + 1) * 256], block[:, width + n * 256 : width + (n + 1) * 256]], 1
+            )
+            for n in range(HEADS_X)
+        ],
+        0,
+    )
+
+
 def local(queries, keys, values):
     zl, y, c, zh, x = (lax.axis_index(name) for name in AXES)
     blk = (zl * SIZES[1] + y) * SIZES[2] + c
     where = jnp.stack([x, zh, blk]).astype(jnp.int32)
-
-    own = exchange(
-        jnp.concatenate(
-            [
-                jnp.concatenate([keys[:, n * 256 : (n + 1) * 256], values[:, n * 256 : (n + 1) * 256]], 1)
-                for n in range(HEADS_X)
-            ],
-            0,
-        ),
-        "x",
-    )
+    always = blk < 32
+    raw = jnp.concatenate([keys, values], 1)
+
+    own = exchange(of_heads(raw), "x")
     rows = own.shape[0]
-
+    quarter = rows // 4
+
+    def onward(n):
+        part = own[n * quarter : (n + 1) * quarter]
+        return (
+            lax.ppermute(part, "zh", [(0, 1), (1, 2), (2, 3)]),
+            lax.ppermute(part, "zh", [(0, 3), (1, 0)]),
+        )
+
+    def step(body, *operands):
+        shapes = jax.eval_shape(body, *operands)
+        return lax.cond(
+            always,
+            body,
+            lambda *_: jax.tree.map(lambda one: jnp.zeros(one.shape, one.dtype), shapes),
+            *operands,
+        )
+
+    part = raw.shape[0] // 4
+    held = raw[:part]
+    for to in range(1, 4):
+        got = send(
+            raw[to * part : (to + 1) * part],
+            lambda zl, y, c, zh, x: (0, to, 0, zh, x) if (zl, y, c) == (0, 0, 0) else None,
+        )
+        held = jnp.where(y == to, got, held)
+
+    def doubled(held, swap):
+        got = send(held, lambda zl, y, c, zh, x: (0, y, 0, swap[zh], x) if (zl, c) == (0, 0) else None)
+        return jnp.concatenate([held, got], 0)
+
+    held, *kv0 = step(lambda held: (doubled(held, (1, 0, 3, 2)), *onward(0)), held)
+
+    def second(held):
+        q = exchange(
+            jnp.concatenate([queries[:, n * 512 : (n + 1) * 512] for n in range(HEADS_X)], 0), "x"
+        )
+        return (doubled(held, (3, 2, 1, 0)), q, *onward(1))
+
+    held, q, *kv1 = step(second, held)
+
+    def third(held):
+        first = lambda zl, c: (zl, c) == (0, 0)
+        two = send(held, lambda zl, y, c, zh, x: (2, y, 0, zh, x) if first(zl, c) else None)
+        one = send(held, lambda zl, y, c, zh, x: (1, y, 0, zh, x) if first(zl, c) else None)
+        three = send(held, lambda zl, y, c, zh, x: (3, y, 0, (zh + 3) % 4, x) if first(zl, c) else None)
+        strip = jnp.where(zl == 0, held, jnp.where(zl == 1, one, jnp.where(zl == 2, two, three)))
+        half = strip.shape[0] // 2
+        moved = lax.ppermute(strip[half:], "c", [(0, 1)])
+        return (jnp.where(c == 0, strip[:half], moved), *onward(2))
+
+    strip, *kv2 = step(third, held)
+    strip, *kv3 = step(lambda strip: (exchange(of_heads(strip), "x"), *onward(3)), strip)
+
+    got_a, got_b = (jnp.concatenate(parts, 0) for parts in zip(kv0, kv1, kv2, kv3))
     half = rows // 2
-    got_a = lax.ppermute(own, "zh", [(0, 1), (1, 2), (2, 3)])
-    got_b = lax.ppermute(own, "zh", [(0, 3), (1, 0)])
-
-    piece, where = lax.cond(
-        blk < 32,
-        lambda: (exchange(own, ("zl", "y", "c"))[: rows // 32], where),
-        lambda: (jnp.zeros((rows // 32, 512), BF), where - 1),
-    )
-    q = exchange(
-        jnp.concatenate([queries[:, n * 512 : (n + 1) * 512] for n in range(HEADS_X)], 0), "x"
-    )
-    *state, where = own_part(where, q, own)
-    strip, where = lax.cond(
-        where[2] < 32,
-        lambda: (gathered(piece, ("zl", "zh"), 16), where),
-        lambda: (jnp.zeros((rows // 2, 512), BF), where - 1),
-    )
-    arrived = where[2] >= 0
-    got_a2 = lax.ppermute(jnp.where(arrived, got_a[:half], own[:half]), "zh", [(1, 2), (2, 3)])
-    got_b2 = lax.ppermute(jnp.where(arrived, got_b[half:], own[half:]), "zh", [(3, 2), (0, 3)])
-
-    def whole_anchor():
+    got_a2 = lax.ppermute(got_a[:half], "zh", [(1, 2), (2, 3)])
+    got_b2 = lax.ppermute(got_b[half:], "zh", [(3, 2), (0, 3)])
+
+    def whole_anchor(strip):
         here = gathered(strip, "y", 4)
-        return here, lax.ppermute(here, "c", [(0, 1), (1, 0)])
-
-    here, there = lax.cond(blk < 32, whole_anchor, lambda: (jnp.zeros((1024, 512), BF),) * 2)
+        return here, lax.ppermute(here, "c", [(0, 1), (1, 0)]), *own_part(where, q, own)
+
+    here, there, *state = step(whole_anchor, strip)
     state = middle(where, q, state, (got_a, got_b, here, there))
     out = exchange(last(where, q, state, (got_a2, got_b2)), "x")
     width = rows // HEADS_X

time: 178 us -> 199 us (1.12)
  the two profiles are of different devices: /device:TPU:416 before, /device:TPU:480 now
where the time goes in v4:
time: 199 us; the launch traced here: 198 us
  waiting for transfers between devices  97.8 us (49%)
  starting transfers between devices  39.6 us (20%)
  blocking collectives  29.9 us (15%)
  Pallas kernels  20 us (10%)
  other arithmetic  8.31 us (4%)
  local copies, waits for them, and re-layouts  2.15 us (1%)
    ppermute x4, waiting for transfers between devices, onward(): lax.ppermute(part, 'zh', [(0, 1), (1, 2), (2, 3)])  69.5 us
    all_to_all x2, blocking collectives, exchange(): return lax.all_to_all(block, axes, split_axis=0, concat_axis=0, tiled=True)  29.9 us
    pallas_call x3, Pallas kernels, attention_call(): pl.pallas_call(body, grid_spec=pltpu.PrefetchScalarGridSpec(num_scalar_pr...  20 us
    ppermute x8, waiting for transfers between devices, send(): lax.ppermute(block, AXES, [(device_index(*place), device_index(*to)) for...  17.6 us
    all_to_all x3, starting transfers between devices, exchange(): return lax.all_to_all(block, axes, split_axis=0, concat_axis=0, tiled=True)  12.6 us
    all_to_all x3, waiting for transfers between devices, exchange(): return lax.all_to_all(block, axes, split_axis=0, concat_axis=0, tiled=True)  7.17 us
    ppermute x8, starting transfers between devices, send(): lax.ppermute(block, AXES, [(device_index(*place), device_index(*to)) for...  6.14 us
    ppermute x1, starting transfers between devices, local(): got_b2 = lax.ppermute(got_b[half:], 'zh', [(3, 2), (0, 3)])  5.99 us
  transfers between devices with their start and end apart: 23, of which 8 were waited for; matrix products, arithmetic and copies ran while one was open for 3% of the time, Pallas kernels for 8%

profile of v4, /device:TPU:480, one launch (start us, length us, event | category | flops | bytes accessed | tf_op | source)
XLA Modules:
  0.0 198.3 jit_solution(339628118419923834)
XLA Ops:
  2.8 4.4 %all-to-all-start.3 = ((bf16[4,128,512]{2,1,0:T(8,128)(2,1)}), bf16[4,128,512]{2,1,0:T(8,128)(2,1)S(1)}, u32[]{:S(2)}, u32[]{:S(2)}) async-start(bf16[4,128,512]{2,1,0:T(8,128)(2,1)} %bitcast.9), calls=%async_computation.3 | async-start | bytes 1048576 | tf_op jit(solution)/shard_map/all_to_all | solution.py:23
  9.5 7.2 %all-to-all-done.3 = bf16[4,128,512]{2,1,0:T(8,128)(2,1)S(1)} async-done(((bf16[4,128,512]{2,1,0:T(8,128)(2,1)}), bf16[4,128,512]{2,1,0:T(8,128)(2,1)S(1)}, u32[]{:S(2)}, u32[]{:S(2)}) %all-to-all-start.3) | async-done | bytes 524320 | tf_op jit(solution)/shard_map/all_to_all | solution.py:23
  16.7 18.9 %conditional.5 = (bf16[64,2048]{1,0:T(8,128)(2,1)S(1)}, bf16[128,512]{1,0:T(8,128)(2,1)}, bf16[128,512]{1,0:T(8,128)(2,1)}) conditional(s32[]{:T(128)} %convert_element_type.2, () %tuple.53, (s32[]{:T(128)}, bf16[128,2048]{1,0:T(8,128)(2,1)S(1)}, bf16[32,2048]{1,0:T(8,128)(2,1)S(1)}, bf16[32,2048]{1,0:T(8,128)(2,1)S(1)}, ...), branch_computations={%region_0.1_spmd, %region_1.2_spmd} | conditional | flops 720899 | bytes 3014830 | solution.py:251
  17.4 1.3 collective-permute-start.1
  18.7 1.3 collective-permute-start.2
  20.0 15.5 %collective-permute-done.1 = bf16[128,512]{1,0:T(8,128)(2,1)} collective-permute-done((bf16[128,512]{1,0:T(8,128)(2,1)S(1)}, bf16[128,512]{1,0:T(8,128)(2,1)}, u32[]{:S(2)}, u32[]{:S(2)}) %collective-permute-start.1) | collective-permute-done | bytes 131104 | tf_op jit(solution)/shard_map/cond/branch_1_fun/ppermute | solution.py:245
  35.5 22.5 %conditional.6 = (bf16[128,2048]{1,0:T(8,128)(2,1)S(1)}, bf16[512,512]{1,0:T(8,128)(2,1)}, bf16[128,512]{1,0:T(8,128)(2,1)}, bf16[128,512]{1,0:T(8,128)(2,1)}) conditional(s32[]{:T(128)} %convert_element_type.2, () %tuple.52, (bf16[64,2048]{1,0:T(8,128)(2,1)S(1)}, bf16[128,2048]{1,0:T(8,128)(2,1)S(1)}, bf16[512,512]{1,0:T(8,128)(2,1)S(1)}) %tuple.99), branch_computations={%region_2.3_spmd, %region_3.4_spmd} | conditional | flops 3145728 | bytes 7078072 | solution.py:251
  37.1 4.1 %all-to-all-start.1 = ((bf16[4,128,512]{2,1,0:T(8,128)(2,1)}), bf16[4,128,512]{2,1,0:T(8,128)(2,1)}, u32[]{:S(2)}, u32[]{:S(2)}) async-start(bf16[4,128,512]{2,1,0:T(8,128)(2,1)} %bitcast), calls=%async_computation.1 | async-start | bytes 1048576 | tf_op jit(solution)/shard_map/cond/branch_1_fun/all_to_all | solution.py:23
  41.3 1.3 collective-permute-start.11
  42.6 1.3 collective-permute-start.12
  43.9 12.5 %collective-permute-done.11 = bf16[128,512]{1,0:T(8,128)(2,1)} collective-permute-done((bf16[128,512]{1,0:T(8,128)(2,1)S(1)}, bf16[128,512]{1,0:T(8,128)(2,1)}, u32[]{:S(2)}, u32[]{:S(2)}) %collective-permute-start.11) | collective-permute-done | bytes 131104 | tf_op jit(solution)/shard_map/cond/branch_1_fun/ppermute | solution.py:245
  56.4 1.7 collective-permute-done.12
  58.1 57.1 %conditional.7 = (bf16[64,2048]{1,0:T(8,128)(2,1)S(1)}, bf16[128,512]{1,0:T(8,128)(2,1)}, bf16[128,512]{1,0:T(8,128)(2,1)}) conditional(s32[]{:T(128)} %convert_element_type.2, () %tuple.58, (s32[]{:T(128)}, s32[]{:T(128)}, bf16[128,2048]{1,0:T(8,128)(2,1)S(1)}, bf16[512,512]{1,0:T(8,128)(2,1)S(1)}) %tuple.96), branch_computations={%region_4.5_spmd, %region_5.6_spmd} | conditional | flops 917508 | bytes 12583216 | solution.py:251
  59.5 1.3 collective-permute-start.5
  60.8 17.6 %collective-permute-done.5 = bf16[128,2048]{1,0:T(8,128)(2,1)S(1)} collective-permute-done((bf16[128,2048]{1,0:T(8,128)(2,1)S(1)}, bf16[128,2048]{1,0:T(8,128)(2,1)S(1)}, u32[]{:S(2)}, u32[]{:S(2)}) %collective-permute-start.5) | collective-permute-done | bytes 524320 | tf_op jit(solution)/shard_map/cond/branch_1_fun/ppermute | solution.py:213
  78.5 1.3 collective-permute-start.6
  79.9 1.3 collective-permute-start.7
  82.5 32.6 %collective-permute-done.7 = bf16[128,512]{1,0:T(8,128)(2,1)} collective-permute-done((bf16[128,512]{1,0:T(8,128)(2,1)S(1)}, bf16[128,512]{1,0:T(8,128)(2,1)}, u32[]{:S(2)}, u32[]{:S(2)}) %collective-permute-start.7) | collective-permute-done | bytes 131104 | tf_op jit(solution)/shard_map/cond/branch_1_fun/ppermute | solution.py:245
  117.4 18.2 %conditional.8 = (bf16[256,512]{1,0:T(8,128)(2,1)}, bf16[128,512]{1,0:T(8,128)(2,1)}, bf16[128,512]{1,0:T(8,128)(2,1)}) conditional(s32[]{:T(128)} %convert_element_type.2, () %tuple.57, (bf16[64,2048]{1,0:T(8,128)(2,1)S(1)}, bf16[512,512]{1,0:T(8,128)(2,1)S(1)}) %tuple.97), branch_computations={%region_6.7_spmd, %region_7.8_spmd} | conditional | flops 2097152 | bytes 3145864 | solution.py:251
  118.2 4.0 %all-to-all-start.2 = ((bf16[4,64,512]{2,1,0:T(8,128)(2,1)}), bf16[4,64,512]{2,1,0:T(8,128)(2,1)}, u32[]{:S(2)}, u32[]{:S(2)}) async-start(bf16[4,64,512]{2,1,0:T(8,128)(2,1)} %bitcast.2), calls=%async_computation.2 | async-start | bytes 524288 | tf_op jit(solution)/shard_map/cond/branch_1_fun/all_to_all | solution.py:23
  124.9 8.9 %collective-permute-done.13 = bf16[128,512]{1,0:T(8,128)(2,1)} collective-permute-done((bf16[128,512]{1,0:T(8,128)(2,1)S(1)}, bf16[128,512]{1,0:T(8,128)(2,1)}, u32[]{:S(2)}, u32[]{:S(2)}) %collective-permute-start.13) | collective-permute-done | bytes 131104 | tf_op jit(solution)/shard_map/cond/branch_1_fun/ppermute | solution.py:245
  133.8 1.8 collective-permute-done.14
  136.6 6.0 %collective-permute-start.19 = (bf16[256,512]{1,0:T(8,128)(2,1)S(1)}, bf16[256,512]{1,0:T(8,128)(2,1)S(1)}, u32[]{:S(2)}, u32[]{:S(2)}) collective-permute-start(bf16[256,512]{1,0:T(8,128)(2,1)S(1)} %pad_maximum_fusion.8), channel_id=1, source_target_pairs={{12,8},{0,12},{13,9},{1,13},{14,10},{2,14},{15,11},{3,15},{28,24},... | collective-permute-start | bytes 786440 | tf_op jit(solution)/shard_map/ppermute | solution.py:297
  142.7 22.0 %conditional.9 = (bf16[1024,512]{1,0:T(8,128)(2,1)}, bf16[1024,512]{1,0:T(8,128)(2,1)}, f32[4,1,512]{2,1,0:T(1,128)S(1)}, f32[4,1,512]{2,1,0:T(1,128)S(1)}, f32[4,128,512]{2,1,0:T(8,128)S(1)}) conditional(s32[]{:T(128)} %convert_element_type.2, () %tuple.56, (bf16[256,512]{1,0:T(8,128)(2,1)}, s32[3]{0:T(128)S(1)}, bf16[512,512]{1,0:T(8,128)(2,1)}, ...), branch_computations={%region_8.9_spmd, %region_9.10_spmd} | conditional | flops 12582912 | bytes 7733328 | solution.py:251
  142.7 1.5 pad_maximum_fusion.3
  144.1 15.2 %all_to_all.48 = bf16[4,256,512]{2,1,0:T(8,128)(2,1)} all-to-all(bf16[4,256,512]{2,1,0:T(8,128)(2,1)S(1)} %bitcast.26), channel_id=1, replica_groups=mesh['zl'=4,'y'=4,'c'=2,'zh'=4,'x'=4] {'y'}, dimensions={0} | all-to-all | bytes 2097152 | tf_op jit(solution)/shard_map/cond/branch_1_fun/all_to_all | solution.py:23
  159.4 1.9 collective-permute-start.9
  161.3 3.3 %own_attention.1 = (f32[4,1,512]{2,1,0:T(1,128)S(1)}, f32[4,1,512]{2,1,0:T(1,128)S(1)}, f32[4,128,512]{2,1,0:T(8,128)S(1)}) custom-call(s32[3]{0:T(128)S(1)} %get-tuple-element.74.where_ref, bf16[512,512]{1,0:T(8,128)(2,1)} %get-tuple-element.75.q_ref, bf16[512,512]{1,0:T(8,128)(2,1)S(1)} %get-tuple-element.76.ok.ov, ...), custom_call_target="tpu_custom_call" | custom-call | flops 8388608 | bytes 131072 | tf_op jit(solution)/shard_map/cond/branch_1_fun/own_attention/pallas_call | solution.py:141
  164.6 1.4 pad_maximum_fusion.4
  166.0 12.5 %middle_attention.1 = (f32[4,1,512]{2,1,0:T(1,128)S(1)}, f32[4,1,512]{2,1,0:T(1,128)S(1)}, f32[4,128,512]{2,1,0:T(8,128)S(1)}) custom-call(s32[3]{0:T(128)S(1)} %pad_add_fusion.where_ref, bf16[512,512]{1,0:T(8,128)(2,1)} %get-tuple-element.102.q_ref, f32[4,1,512]{2,1,0:T(1,128)S(1)} %get-tuple-element.106.p_ref, f32[4,1,512]{2,1,0:T(1,128)S(1)} %get-tuple-element.107.t_ref, ...), custom_call_target="tpu_custom_call" | custom-call | flops 3221 | bytes 8 | tf_op jit(solution)/shard_map/middle_attention/pallas_call | solution.py:141
  178.5 4.2 %last_attention.1 = bf16[512,512]{1,0:T(8,128)(2,1)S(1)} custom-call(s32[3]{0:T(128)S(1)} %pad_add_fusion.where_ref, bf16[512,512]{1,0:T(8,128)(2,1)} %get-tuple-element.102.q_ref, f32[4,1,512]{2,1,0:T(1,128)S(1)} %get-tuple-element.119.peak_ref, f32[4,1,512]{2,1,0:T(1,128)S(1)} %get-tuple-element.120.total_ref, ...), custom_call_target="tpu_custom_call" | custom-call | flops 536870912 | bytes 8388608 | tf_op jit(solution)/shard_map/last_attention/pallas_call | solution.py:141
  182.7 14.7 %all_to_all.49 = bf16[4,128,512]{2,1,0:T(8,128)(2,1)S(1)} all-to-all(bf16[4,128,512]{2,1,0:T(8,128)(2,1)S(1)} %bitcast.20), channel_id=1, replica_groups=mesh['zl'=4,'y'=4,'c'=2,'zh'=4,'x'=4] {'x'}, dimensions={0} | all-to-all | bytes 1048576 | tf_op jit(solution)/shard_map/all_to_all | solution.py:23
  (57 shorter events, 17.7 us)
Async XLA Ops:
  1.9 5.3 %copy-start = (bf16[128,1024]{1,0:T(8,128)(2,1)S(1)}, bf16[128,1024]{1,0:T(8,128)(2,1)}, u32[]{:S(2)}) copy-start(bf16[128,1024]{1,0:T(8,128)(2,1)} %param.14) | copy-start | bytes 786436
  2.8 4.5 %copy-start.1 = (bf16[128,1024]{1,0:T(8,128)(2,1)S(1)}, bf16[128,1024]{1,0:T(8,128)(2,1)}, u32[]{:S(2)}) copy-start(bf16[128,1024]{1,0:T(8,128)(2,1)} %param.15) | copy-start | bytes 786436
  2.8 13.9 %all-to-all-start.3 = ((bf16[4,128,512]{2,1,0:T(8,128)(2,1)}), bf16[4,128,512]{2,1,0:T(8,128)(2,1)S(1)}, u32[]{:S(2)}, u32[]{:S(2)}) async-start(bf16[4,128,512]{2,1,0:T(8,128)(2,1)} %bitcast.9), calls=%async_computation.3 | async-start | bytes 1048576 | tf_op jit(solution)/shard_map/all_to_all | solution.py:23
  7.3 28.3 %copy-start.2 = (bf16[128,2048]{1,0:T(8,128)(2,1)S(1)}, bf16[128,2048]{1,0:T(8,128)(2,1)}, u32[]{:S(2)}) copy-start(bf16[128,2048]{1,0:T(8,128)(2,1)} %param.13) | copy-start | bytes 1572868
  7.3 2.2 %collective-permute-start.15 = (bf16[32,2048]{1,0:T(8,128)(2,1)S(1)}, bf16[32,2048]{1,0:T(8,128)(2,1)S(1)}, u32[]{:S(2)}, u32[]{:S(2)}) collective-permute-start(bf16[32,2048]{1,0:T(8,128)(2,1)S(1)} %get-tuple-element.142), channel_id=1, source_target_pairs={{0,32},{1,33},{2,34},{3,35},{4,36},{5,37},{6,38},{7,39},{8,40},{9,... | collective-permute-start | bytes 393224 | tf_op jit(solution)/shard_map/ppermute | solution.py:213
  8.1 1.4 collective-permute-start.16
  8.8 0.7 collective-permute-start.17
  16.7 3.3 %collective-permute-start = (bf16[32,2048]{1,0:T(8,128)(2,1)S(1)}, bf16[32,2048]{1,0:T(8,128)(2,1)S(1)}, u32[]{:S(2)}, u32[]{:S(2)}) collective-permute-start(bf16[32,2048]{1,0:T(8,128)(2,1)S(1)} %select_select_fusion), channel_id=1, source_target_pairs={{0,4},{1,5},{2,6},{3,7},{4,0},{5,1},{6,2},{7,3},{8,12},{9,13},{10,... | collective-permute-start | bytes 393224 | tf_op jit(solution)/shard_map/cond/branch_1_fun/ppermute | solution.py:213
  17.4 18.1 %collective-permute-start.1 = (bf16[128,512]{1,0:T(8,128)(2,1)S(1)}, bf16[128,512]{1,0:T(8,128)(2,1)}, u32[]{:S(2)}, u32[]{:S(2)}) collective-permute-start(bf16[128,512]{1,0:T(8,128)(2,1)S(1)} %slice.82), channel_id=1, source_target_pairs={{0,4},{4,8},{8,12},{1,5},{5,9},{9,13},{2,6},{6,10},{10,14},{3,7},{... | collective-permute-start | bytes 393224 | tf_op jit(solution)/shard_map/cond/branch_1_fun/ppermute | solution.py:245
  18.7 16.8 %collective-permute-start.2 = (bf16[128,512]{1,0:T(8,128)(2,1)S(1)}, bf16[128,512]{1,0:T(8,128)(2,1)}, u32[]{:S(2)}, u32[]{:S(2)}) collective-permute-start(bf16[128,512]{1,0:T(8,128)(2,1)S(1)} %slice.82), channel_id=1, source_target_pairs={{0,12},{4,0},{1,13},{5,1},{2,14},{6,2},{3,15},{7,3},{16,28},{20,16... | collective-permute-start | bytes 393224 | tf_op jit(solution)/shard_map/cond/branch_1_fun/ppermute | solution.py:246
  35.5 8.3 %collective-permute-start.10 = (bf16[64,2048]{1,0:T(8,128)(2,1)S(1)}, bf16[64,2048]{1,0:T(8,128)(2,1)S(1)}, u32[]{:S(2)}, u32[]{:S(2)}) collective-permute-start(bf16[64,2048]{1,0:T(8,128)(2,1)S(1)} %get-tuple-element.64), channel_id=1, source_target_pairs={{0,12},{1,13},{2,14},{3,15},{4,8},{5,9},{6,10},{7,11},{8,4},{9,5},... | collective-permute-start | bytes 786440 | tf_op jit(solution)/shard_map/cond/branch_1_fun/ppermute | solution.py:213
  37.1 21.0 %all-to-all-start.1 = ((bf16[4,128,512]{2,1,0:T(8,128)(2,1)}), bf16[4,128,512]{2,1,0:T(8,128)(2,1)}, u32[]{:S(2)}, u32[]{:S(2)}) async-start(bf16[4,128,512]{2,1,0:T(8,128)(2,1)} %bitcast), calls=%async_computation.1 | async-start | bytes 1048576 | tf_op jit(solution)/shard_map/cond/branch_1_fun/all_to_all | solution.py:23
  41.3 15.2 %collective-permute-start.11 = (bf16[128,512]{1,0:T(8,128)(2,1)S(1)}, bf16[128,512]{1,0:T(8,128)(2,1)}, u32[]{:S(2)}, u32[]{:S(2)}) collective-permute-start(bf16[128,512]{1,0:T(8,128)(2,1)S(1)} %slice.87), channel_id=1, source_target_pairs={{0,4},{4,8},{8,12},{1,5},{5,9},{9,13},{2,6},{6,10},{10,14},{3,7},{... | collective-permute-start | bytes 393224 | tf_op jit(solution)/shard_map/cond/branch_1_fun/ppermute | solution.py:245
  42.6 15.5 %collective-permute-start.12 = (bf16[128,512]{1,0:T(8,128)(2,1)S(1)}, bf16[128,512]{1,0:T(8,128)(2,1)}, u32[]{:S(2)}, u32[]{:S(2)}) collective-permute-start(bf16[128,512]{1,0:T(8,128)(2,1)S(1)} %slice.87), channel_id=1, source_target_pairs={{0,12},{4,0},{1,13},{5,1},{2,14},{6,2},{3,15},{7,3},{16,28},{20,16... | collective-permute-start | bytes 393224 | tf_op jit(solution)/shard_map/cond/branch_1_fun/ppermute | solution.py:246
  58.1 2.7 %collective-permute-start.3 = (bf16[128,2048]{1,0:T(8,128)(2,1)S(1)}, bf16[128,2048]{1,0:T(8,128)(2,1)S(1)}, u32[]{:S(2)}, u32[]{:S(2)}) collective-permute-start(bf16[128,2048]{1,0:T(8,128)(2,1)S(1)} %get-tuple-element.69), channel_id=1, source_target_pairs={{0,128},{1,129},{2,130},{3,131},{4,132},{5,133},{6,134},{7,135},{8... | collective-permute-start | bytes 1572872 | tf_op jit(solution)/shard_map/cond/branch_1_fun/ppermute | solution.py:213
  58.8 2.0 %collective-permute-start.4 = (bf16[128,2048]{1,0:T(8,128)(2,1)S(1)}, bf16[128,2048]{1,0:T(8,128)(2,1)S(1)}, u32[]{:S(2)}, u32[]{:S(2)}) collective-permute-start(bf16[128,2048]{1,0:T(8,128)(2,1)S(1)} %get-tuple-element.69), channel_id=1, source_target_pairs={{0,256},{1,257},{2,258},{3,259},{4,260},{5,261},{6,262},{7,263},{8... | collective-permute-start | bytes 1572872 | tf_op jit(solution)/shard_map/cond/branch_1_fun/ppermute | solution.py:213
  59.5 18.9 %collective-permute-start.5 = (bf16[128,2048]{1,0:T(8,128)(2,1)S(1)}, bf16[128,2048]{1,0:T(8,128)(2,1)S(1)}, u32[]{:S(2)}, u32[]{:S(2)}) collective-permute-start(bf16[128,2048]{1,0:T(8,128)(2,1)S(1)} %get-tuple-element.69), channel_id=1, source_target_pairs={{0,396},{1,397},{2,398},{3,399},{4,384},{5,385},{6,386},{7,387},{8... | collective-permute-start | bytes 1572872 | tf_op jit(solution)/shard_map/cond/branch_1_fun/ppermute | solution.py:213
  78.5 3.9 %collective-permute-start.6 = (bf16[64,2048]{1,0:T(8,128)(2,1)S(1)}, bf16[64,2048]{1,0:T(8,128)(2,1)S(1)}, u32[]{:S(2)}, u32[]{:S(2)}) collective-permute-start(bf16[64,2048]{1,0:T(8,128)(2,1)S(1)} %slice.139), channel_id=1, source_target_pairs={{0,16},{1,17},{2,18},{3,19},{4,20},{5,21},{6,22},{7,23},{8,24},{9,... | collective-permute-start | bytes 786440 | tf_op jit(solution)/shard_map/cond/branch_1_fun/ppermute | solution.py:288
  79.9 35.3 %collective-permute-start.7 = (bf16[128,512]{1,0:T(8,128)(2,1)S(1)}, bf16[128,512]{1,0:T(8,128)(2,1)}, u32[]{:S(2)}, u32[]{:S(2)}) collective-permute-start(bf16[128,512]{1,0:T(8,128)(2,1)S(1)} %slice.90), channel_id=1, source_target_pairs={{0,4},{4,8},{8,12},{1,5},{5,9},{9,13},{2,6},{6,10},{10,14},{3,7},{... | collective-permute-start | bytes 393224 | tf_op jit(solution)/shard_map/cond/branch_1_fun/ppermute | solution.py:245
  81.2 34.0 %collective-permute-start.8 = (bf16[128,512]{1,0:T(8,128)(2,1)S(1)}, bf16[128,512]{1,0:T(8,128)(2,1)}, u32[]{:S(2)}, u32[]{:S(2)}) collective-permute-start(bf16[128,512]{1,0:T(8,128)(2,1)S(1)} %slice.90), channel_id=1, source_target_pairs={{0,12},{4,0},{1,13},{5,1},{2,14},{6,2},{3,15},{7,3},{16,28},{20,16... | collective-permute-start | bytes 393224 | tf_op jit(solution)/shard_map/cond/branch_1_fun/ppermute | solution.py:246
  116.1 62.4 %collective-permute-start.18 = (bf16[256,512]{1,0:T(8,128)(2,1)S(1)}, bf16[256,512]{1,0:T(8,128)(2,1)S(1)}, u32[]{:S(2)}, u32[]{:S(2)}) collective-permute-start(bf16[256,512]{1,0:T(8,128)(2,1)S(1)} %pad_maximum_fusion.7), channel_id=1, source_target_pairs={{4,8},{8,12},{5,9},{9,13},{6,10},{10,14},{7,11},{11,15},{20,24},{2... | collective-permute-start | bytes 786440 | tf_op jit(solution)/shard_map/ppermute | solution.py:296
  118.2 17.4 %all-to-all-start.2 = ((bf16[4,64,512]{2,1,0:T(8,128)(2,1)}), bf16[4,64,512]{2,1,0:T(8,128)(2,1)}, u32[]{:S(2)}, u32[]{:S(2)}) async-start(bf16[4,64,512]{2,1,0:T(8,128)(2,1)} %bitcast.2), calls=%async_computation.2 | async-start | bytes 524288 | tf_op jit(solution)/shard_map/cond/branch_1_fun/all_to_all | solution.py:23
  122.3 11.5 %collective-permute-start.13 = (bf16[128,512]{1,0:T(8,128)(2,1)S(1)}, bf16[128,512]{1,0:T(8,128)(2,1)}, u32[]{:S(2)}, u32[]{:S(2)}) collective-permute-start(bf16[128,512]{1,0:T(8,128)(2,1)S(1)} %slice.99), channel_id=1, source_target_pairs={{0,4},{4,8},{8,12},{1,5},{5,9},{9,13},{2,6},{6,10},{10,14},{3,7},{... | collective-permute-start | bytes 393224 | tf_op jit(solution)/shard_map/cond/branch_1_fun/ppermute | solution.py:245
  123.6 12.1 %collective-permute-start.14 = (bf16[128,512]{1,0:T(8,128)(2,1)S(1)}, bf16[128,512]{1,0:T(8,128)(2,1)}, u32[]{:S(2)}, u32[]{:S(2)}) collective-permute-start(bf16[128,512]{1,0:T(8,128)(2,1)S(1)} %slice.99), channel_id=1, source_target_pairs={{0,12},{4,0},{1,13},{5,1},{2,14},{6,2},{3,15},{7,3},{16,28},{20,16... | collective-permute-start | bytes 393224 | tf_op jit(solution)/shard_map/cond/branch_1_fun/ppermute | solution.py:246
  136.6 41.9 %collective-permute-start.19 = (bf16[256,512]{1,0:T(8,128)(2,1)S(1)}, bf16[256,512]{1,0:T(8,128)(2,1)S(1)}, u32[]{:S(2)}, u32[]{:S(2)}) collective-permute-start(bf16[256,512]{1,0:T(8,128)(2,1)S(1)} %pad_maximum_fusion.8), channel_id=1, source_target_pairs={{12,8},{0,12},{13,9},{1,13},{14,10},{2,14},{15,11},{3,15},{28,24},... | collective-permute-start | bytes 786440 | tf_op jit(solution)/shard_map/ppermute | solution.py:297
  159.4 5.3 %collective-permute-start.9 = (bf16[1024,512]{1,0:T(8,128)(2,1)}, bf16[1024,512]{1,0:T(8,128)(2,1)}, u32[]{:S(2)}, u32[]{:S(2)}) collective-permute-start(bf16[1024,512]{1,0:T(8,128)(2,1)} %bitcast.5), channel_id=1, source_target_pairs={{0,16},{16,0},{1,17},{17,1},{2,18},{18,2},{3,19},{19,3},{4,20},{20... | collective-permute-start | bytes 3145736 | tf_op jit(solution)/shard_map/cond/branch_1_fun/ppermute | solution.py:301

commit v5 on v4

--- a/solution.py
+++ b/solution.py
@@ -72,7 +72,10 @@
             ref[g, :, columns] = part
 
 
-def own_kernel(where_ref, q_ref, ok, ov, *refs):
+def own_kernel(where_ref, q_ref, ok, ov, *outs):
+    refs, where_out = outs[:3], outs[3]
+    for n in range(3):
+        where_out[n] = where_ref[n]
     absorb(refs, q_ref, [(ok, ov)], causal=True)
 
 
@@ -165,8 +168,9 @@
         q,
         (),
         (own,),
-        state_specs(rows),
-        [jax.ShapeDtypeStruct(shape, F32) for shape in state_shapes(4, rows)],
+        state_specs(rows) + [pl.BlockSpec(memory_space=pltpu.SMEM)],
+        [jax.ShapeDtypeStruct(shape, F32) for shape in state_shapes(4, rows)]
+        + [jax.ShapeDtypeStruct((3,), jnp.int32)],
         [],
         64,
     )
@@ -184,7 +188,6 @@
         state_specs(rows),
         [jax.ShapeDtypeStruct(shape, F32) for shape in state_shapes(4, rows)],
         [],
-        10**6,
     )
 
 
@@ -237,15 +240,6 @@
 
     own = exchange(of_heads(raw), "x")
     rows = own.shape[0]
-    quarter = rows // 4
-
-    def onward(n):
-        part = own[n * quarter : (n + 1) * quarter]
-        return (
-            lax.ppermute(part, "zh", [(0, 1), (1, 2), (2, 3)]),
-            lax.ppermute(part, "zh", [(0, 3), (1, 0)]),
-        )
-
     def step(body, *operands):
         shapes = jax.eval_shape(body, *operands)
         return lax.cond(
@@ -268,17 +262,8 @@
         got = send(held, lambda zl, y, c, zh, x: (0, y, 0, swap[zh], x) if (zl, c) == (0, 0) else None)
         return jnp.concatenate([held, got], 0)
 
-    held, *kv0 = step(lambda held: (doubled(held, (1, 0, 3, 2)), *onward(0)), held)
-
-    def second(held):
-        q = exchange(
-            jnp.concatenate([queries[:, n * 512 : (n + 1) * 512] for n in range(HEADS_X)], 0), "x"
-        )
-        return (doubled(held, (3, 2, 1, 0)), q, *onward(1))
-
-    held, q, *kv1 = step(second, held)
-
-    def third(held):
+    def over_z(held, own):
+        held = doubled(doubled(held, (1, 0, 3, 2)), (3, 2, 1, 0))
         first = lambda zl, c: (zl, c) == (0, 0)
         two = send(held, lambda zl, y, c, zh, x: (2, y, 0, zh, x) if first(zl, c) else None)
         one = send(held, lambda zl, y, c, zh, x: (1, y, 0, zh, x) if first(zl, c) else None)
@@ -286,21 +271,26 @@
         strip = jnp.where(zl == 0, held, jnp.where(zl == 1, one, jnp.where(zl == 2, two, three)))
         half = strip.shape[0] // 2
         moved = lax.ppermute(strip[half:], "c", [(0, 1)])
-        return (jnp.where(c == 0, strip[:half], moved), *onward(2))
-
-    strip, *kv2 = step(third, held)
-    strip, *kv3 = step(lambda strip: (exchange(of_heads(strip), "x"), *onward(3)), strip)
-
-    got_a, got_b = (jnp.concatenate(parts, 0) for parts in zip(kv0, kv1, kv2, kv3))
+        return jnp.where(c == 0, strip[:half], moved), own
+
+    strip, own = step(over_z, held, own)
+
     half = rows // 2
-    got_a2 = lax.ppermute(got_a[:half], "zh", [(1, 2), (2, 3)])
-    got_b2 = lax.ppermute(got_b[half:], "zh", [(3, 2), (0, 3)])
-
-    def whole_anchor(strip):
-        here = gathered(strip, "y", 4)
-        return here, lax.ppermute(here, "c", [(0, 1), (1, 0)]), *own_part(where, q, own)
-
-    here, there, *state = step(whole_anchor, strip)
+    got_b = lax.ppermute(own, "zh", [(0, 3), (1, 0)])
+    got_a = lax.ppermute(own, "zh", [(0, 1), (1, 2), (2, 3)])
+
+    def whole_anchor(strip, where):
+        here = gathered(exchange(of_heads(strip), "x"), "y", 4)
+        return here, lax.ppermute(here, "c", [(0, 1), (1, 0)]), where
+
+    here, there, where = step(whole_anchor, strip, where)
+    q = exchange(
+        jnp.concatenate([queries[:, n * 512 : (n + 1) * 512] for n in range(HEADS_X)], 0), "x"
+    )
+    *state, where = own_part(where, q, own)
+    arrived = where[2] >= 0
+    got_a2 = lax.ppermute(jnp.where(arrived, got_a[:half], own[:half]), "zh", [(1, 2), (2, 3)])
+    got_b2 = lax.ppermute(jnp.where(arrived, got_b[half:], own[half:]), "zh", [(3, 2), (0, 3)])
     state = middle(where, q, state, (got_a, got_b, here, there))
     out = exchange(last(where, q, state, (got_a2, got_b2)), "x")
     width = rows // HEADS_X

time: 199 us -> 160 us (0.80)
  the two profiles are of different devices: /device:TPU:480 before, /device:TPU:1 now
where the time goes in v5:
time: 160 us
  waiting for transfers between devices  59.4 us (37%)
  blocking collectives  51.3 us (32%)
  starting transfers between devices  28.3 us (18%)
  Pallas kernels  13 us (8%)
  local copies, waits for them, and re-layouts  3.39 us (2%)
  other arithmetic  3.31 us (2%)
    all_to_all x4, blocking collectives, exchange(): return lax.all_to_all(block, axes, split_axis=0, concat_axis=0, tiled=True)  51.3 us
    ppermute x1, waiting for transfers between devices, over_z(): moved = lax.ppermute(strip[half:], 'c', [(0, 1)])  42.7 us
    pallas_call x3, Pallas kernels, attention_call(): pl.pallas_call(body, grid_spec=pltpu.PrefetchScalarGridSpec(num_scalar_pr...  13 us
    ppermute x1, waiting for transfers between devices, local(): lax.ppermute(jnp.where(arrived, got_b[half:], own[half:]), 'zh', [(3, 2),...  10.1 us
    ppermute x8, starting transfers between devices, send(): lax.ppermute(block, AXES, [(device_index(*place), device_index(*to)) for...  5.57 us
    ppermute x1, starting transfers between devices, local(): got_a = lax.ppermute(own, 'zh', [(0, 1), (1, 2), (2, 3)])  5.21 us
    all_to_all x1, starting transfers between devices, exchange(): return lax.all_to_all(block, axes, split_axis=0, concat_axis=0, tiled=True)  4.97 us
    ppermute x1, starting transfers between devices, whole_anchor(): return (here, lax.ppermute(here, 'c', [(0, 1), (1, 0)]), where)  4.69 us
  transfers between devices with their start and end apart: 15, of which 4 were waited for; matrix products, arithmetic and copies ran while one was open for 2% of the time, Pallas kernels for 7%

profile of v5, /device:TPU:1, one launch (start us, length us, event | category | flops | bytes accessed | tf_op | source)
XLA Modules:
  0.0 159.7 jit_solution(8696083050493195360)
XLA Ops:
  0.0 1.0 fusion.4
  1.0 1.0 fusion.3
  1.9 0.8 maximum_maximum_fusion.1
  2.8 5.0 %all-to-all-start.2 = ((bf16[4,128,512]{2,1,0:T(8,128)(2,1)}), bf16[4,128,512]{2,1,0:T(8,128)(2,1)S(1)}, u32[]{:S(2)}, u32[]{:S(2)}) async-start(bf16[4,128,512]{2,1,0:T(8,128)(2,1)} %bitcast.5), calls=%async_computation.2 | async-start | bytes 1048576 | tf_op jit(solution)/shard_map/all_to_all | solution.py:23
  7.8 0.8 collective-permute-start.7
  8.7 0.7 collective-permute-start.8
  10.0 0.7 fusion.1
  10.7 3.9 %all-to-all-done.2 = bf16[4,128,512]{2,1,0:T(8,128)(2,1)S(1)} async-done(((bf16[4,128,512]{2,1,0:T(8,128)(2,1)}), bf16[4,128,512]{2,1,0:T(8,128)(2,1)S(1)}, u32[]{:S(2)}, u32[]{:S(2)}) %all-to-all-start.2) | async-done | bytes 524320 | tf_op jit(solution)/shard_map/all_to_all | solution.py:23
  14.7 48.1 %conditional.2 = (bf16[64,2048]{1,0:T(8,128)(2,1)S(1)}, bf16[512,512]{1,0:T(8,128)(2,1)S(1)}) conditional(s32[]{:T(128)} %convert_element_type.4, () %tuple.29, (s32[]{:T(128)}, s32[]{:T(128)}, s32[]{:T(128)}, bf16[128,2048]{1,0:T(8,128)(2,1)S(1)}, bf16[32,2048]{1,0:T(8,128)(2,1)S(1)}, /*index=5*/bf16[32,2048]{1,0:T(8,128)(2,1)S(1)}, ...), branch_computations={%region_0.1_spmd, %region_1.2_spmd} | conditional | flops 4784135 | bytes 16122182 | solution.py:245
  15.4 0.7 collective-permute-start.1
  16.2 0.7 collective-permute-start.2
  16.9 0.7 collective-permute-start.3
  17.6 0.7 collective-permute-start.4
  18.7 1.3 collective-permute-start.5
  20.0 42.7 %collective-permute-done.5 = bf16[64,2048]{1,0:T(8,128)(2,1)S(1)} collective-permute-done((bf16[64,2048]{1,0:T(8,128)(2,1)S(1)}, bf16[64,2048]{1,0:T(8,128)(2,1)S(1)}, u32[]{:S(2)}, u32[]{:S(2)}) %collective-permute-start.5) | collective-permute-done | bytes 262176 | tf_op jit(solution)/shard_map/cond/branch_1_fun/ppermute | solution.py:273
  62.8 5.2 %collective-permute-start.10 = (bf16[512,512]{1,0:T(8,128)(2,1)S(1)}, bf16[512,512]{1,0:T(8,128)(2,1)S(1)}, u32[]{:S(2)}, u32[]{:S(2)}) collective-permute-start(bf16[512,512]{1,0:T(8,128)(2,1)S(1)} %get-tuple-element.65.ok.ov), channel_id=1, source_target_pairs={{0,4},{4,8},{8,12},{1,5},{5,9},{9,13},{2,6},{6,10},{10,14},{3,7},{... | collective-permute-start | bytes 1572872 | tf_op jit(solution)/shard_map/ppermute | solution.py:280
  68.0 3.6 %collective-permute-start.11 = (bf16[512,512]{1,0:T(8,128)(2,1)S(1)}, bf16[512,512]{1,0:T(8,128)(2,1)S(1)}, u32[]{:S(2)}, u32[]{:S(2)}) collective-permute-start(bf16[512,512]{1,0:T(8,128)(2,1)S(1)} %get-tuple-element.65.ok.ov), channel_id=1, source_target_pairs={{0,12},{4,0},{1,13},{5,1},{2,14},{6,2},{3,15},{7,3},{16,28},{20,16... | collective-permute-start | bytes 1572872 | tf_op jit(solution)/shard_map/ppermute | solution.py:279
  71.7 0.9 pad_maximum_fusion.3
  72.7 35.6 %conditional.3 = (bf16[1024,512]{1,0:T(8,128)(2,1)}, bf16[1024,512]{1,0:T(8,128)(2,1)}, s32[3]{0:T(128)S(1)}) conditional(s32[]{:T(128)} %convert_element_type.4, () %tuple.28, (bf16[64,2048]{1,0:T(8,128)(2,1)S(1)}, s32[3]{0:T(128)S(1)}) %tuple.31), branch_computations={%region_2.3_spmd, %region_3.4_spmd} | conditional | flops 6291456 | bytes 9175104 | solution.py:245
  72.7 10.4 %all_to_all.49 = bf16[4,64,512]{2,1,0:T(8,128)(2,1)S(1)} all-to-all(bf16[4,64,512]{2,1,0:T(8,128)(2,1)S(1)} %bitcast.29), channel_id=1, replica_groups=mesh['zl'=4,'y'=4,'c'=2,'zh'=4,'x'=4] {'x'}, dimensions={0} | all-to-all | bytes 524288 | tf_op jit(solution)/shard_map/cond/branch_1_fun/all_to_all | solution.py:23
  83.2 17.8 %all_to_all.50 = bf16[4,256,512]{2,1,0:T(8,128)(2,1)} all-to-all(bf16[4,256,512]{2,1,0:T(8,128)(2,1)S(1)} %bitcast.25), channel_id=1, replica_groups=mesh['zl'=4,'y'=4,'c'=2,'zh'=4,'x'=4] {'y'}, dimensions={0} | all-to-all | bytes 2097152 | tf_op jit(solution)/shard_map/cond/branch_1_fun/all_to_all | solution.py:23
  101.0 4.7 %collective-permute-start.6 = (bf16[1024,512]{1,0:T(8,128)(2,1)}, bf16[1024,512]{1,0:T(8,128)(2,1)}, u32[]{:S(2)}, u32[]{:S(2)}) collective-permute-start(bf16[1024,512]{1,0:T(8,128)(2,1)} %bitcast.4), channel_id=1, source_target_pairs={{0,16},{16,0},{1,17},{17,1},{2,18},{18,2},{3,19},{19,3},{4,20},{20... | collective-permute-start | bytes 3145736 | tf_op jit(solution)/shard_map/cond/branch_1_fun/ppermute | solution.py:284
  105.7 2.6 %collective-permute-done.6 = bf16[1024,512]{1,0:T(8,128)(2,1)} collective-permute-done((bf16[1024,512]{1,0:T(8,128)(2,1)}, bf16[1024,512]{1,0:T(8,128)(2,1)}, u32[]{:S(2)}, u32[]{:S(2)}) %collective-permute-start.6) | collective-permute-done | bytes 1048608 | tf_op jit(solution)/shard_map/cond/branch_1_fun/ppermute | solution.py:284
  108.3 11.6 %all_to_all.51 = bf16[4,128,512]{2,1,0:T(8,128)(2,1)S(1)} all-to-all(bf16[4,128,512]{2,1,0:T(8,128)(2,1)S(1)} %bitcast.27), channel_id=1, replica_groups=mesh['zl'=4,'y'=4,'c'=2,'zh'=4,'x'=4] {'x'}, dimensions={0} | all-to-all | bytes 1048576 | tf_op jit(solution)/shard_map/all_to_all | solution.py:23
  119.9 2.8 %own_attention.1 = (f32[4,1,512]{2,1,0:T(1,128)S(1)}, f32[4,1,512]{2,1,0:T(1,128)S(1)}, f32[4,128,512]{2,1,0:T(8,128)S(1)}, s32[3]{0:T(128)S(1)}) custom-call(s32[3]{0:T(128)S(1)} %get-tuple-element.64.where_ref, bf16[512,512]{1,0:T(8,128)(2,1)S(1)} %bitcast.21, bf16[512,512]{1,0:T(8,128)(2,1)S(1)} %get-tuple-element.65.ok.ov, ...), custom_call_target="tpu_custom_call" | custom-call | flops 8388608 | bytes 131072 | tf_op jit(solution)/shard_map/own_attention/pallas_call | solution.py:144
  124.0 0.7 collective-permute-start.12
  124.7 2.2 %collective-permute-start.13 = (bf16[256,512]{1,0:T(8,128)(2,1)S(1)}, bf16[256,512]{1,0:T(8,128)(2,1)S(1)}, u32[]{:S(2)}, u32[]{:S(2)}) collective-permute-start(bf16[256,512]{1,0:T(8,128)(2,1)S(1)} %get-tuple-element.87), channel_id=1, source_target_pairs={{12,8},{0,12},{13,9},{1,13},{14,10},{2,14},{15,11},{3,15},{28,24},... | collective-permute-start | bytes 786440 | tf_op jit(solution)/shard_map/ppermute | solution.py:293
  126.9 9.0 %middle_attention.1 = (f32[4,1,512]{2,1,0:T(1,128)S(1)}, f32[4,1,512]{2,1,0:T(1,128)S(1)}, f32[4,128,512]{2,1,0:T(8,128)S(1)}) custom-call(s32[3]{0:T(128)S(1)} %get-tuple-element.66.where_ref, bf16[512,512]{1,0:T(8,128)(2,1)S(1)} %bitcast.22, f32[4,1,512]{2,1,0:T(1,128)S(1)} %get-tuple-element.67.p_ref, f32[4,1,512]{2,1,0:T(1,128)S(1)} %get-tuple-element.68.t_ref, ...), custom_call_target="tpu_custom_call" | custom-call | flops 3221225472 | bytes 8388608 | tf_op jit(solution)/shard_map/middle_attention/pallas_call | solution.py:144
  136.0 10.1 %collective-permute-done.13.bk.bv = bf16[256,512]{1,0:T(8,128)(2,1)S(1)} collective-permute-done((bf16[256,512]{1,0:T(8,128)(2,1)S(1)}, bf16[256,512]{1,0:T(8,128)(2,1)S(1)}, u32[]{:S(2)}, u32[]{:S(2)}) %collective-permute-start.13) | collective-permute-done | bytes 262176 | tf_op jit(solution)/shard_map/ppermute | solution.py:293
  146.1 1.2 last_attention.1
  147.3 11.5 %all_to_all.52 = bf16[4,128,512]{2,1,0:T(8,128)(2,1)S(1)} all-to-all(bf16[4,128,512]{2,1,0:T(8,128)(2,1)S(1)} %bitcast.24), channel_id=1, replica_groups=mesh['zl'=4,'y'=4,'c'=2,'zh'=4,'x'=4] {'x'}, dimensions={0} | all-to-all | bytes 1048576 | tf_op jit(solution)/shard_map/all_to_all | solution.py:23
  158.8 0.8 pad_maximum_fusion.4
  (36 shorter events, 2.8 us)
Async XLA Ops:
  1.9 5.8 %copy-start = (bf16[128,1024]{1,0:T(8,128)(2,1)S(1)}, bf16[128,1024]{1,0:T(8,128)(2,1)}, u32[]{:S(2)}) copy-start(bf16[128,1024]{1,0:T(8,128)(2,1)} %param.8) | copy-start | bytes 786436
  2.8 5.0 %copy-start.1 = (bf16[128,1024]{1,0:T(8,128)(2,1)S(1)}, bf16[128,1024]{1,0:T(8,128)(2,1)}, u32[]{:S(2)}) copy-start(bf16[128,1024]{1,0:T(8,128)(2,1)} %param.9) | copy-start | bytes 786436
  2.8 11.9 %all-to-all-start.2 = ((bf16[4,128,512]{2,1,0:T(8,128)(2,1)}), bf16[4,128,512]{2,1,0:T(8,128)(2,1)S(1)}, u32[]{:S(2)}, u32[]{:S(2)}) async-start(bf16[4,128,512]{2,1,0:T(8,128)(2,1)} %bitcast.5), calls=%async_computation.2 | async-start | bytes 1048576 | tf_op jit(solution)/shard_map/all_to_all | solution.py:23
  7.7 2.3 %copy-start.2 = (bf16[128,2048]{1,0:T(8,128)(2,1)S(1)}, bf16[128,2048]{1,0:T(8,128)(2,1)}, u32[]{:S(2)}) copy-start(bf16[128,2048]{1,0:T(8,128)(2,1)} %param.7) | copy-start | bytes 1572868
  7.8 2.9 %collective-permute-start.7 = (bf16[32,2048]{1,0:T(8,128)(2,1)S(1)}, bf16[32,2048]{1,0:T(8,128)(2,1)S(1)}, u32[]{:S(2)}, u32[]{:S(2)}) collective-permute-start(bf16[32,2048]{1,0:T(8,128)(2,1)S(1)} %get-tuple-element.95), channel_id=1, source_target_pairs={{0,32},{1,33},{2,34},{3,35},{4,36},{5,37},{6,38},{7,39},{8,40},{9,... | collective-permute-start | bytes 393224 | tf_op jit(solution)/shard_map/ppermute | solution.py:216
  8.7 2.1 %collective-permute-start.8 = (bf16[32,2048]{1,0:T(8,128)(2,1)S(1)}, bf16[32,2048]{1,0:T(8,128)(2,1)S(1)}, u32[]{:S(2)}, u32[]{:S(2)}) collective-permute-start(bf16[32,2048]{1,0:T(8,128)(2,1)S(1)} %get-tuple-element.94), channel_id=1, source_target_pairs={{0,64},{1,65},{2,66},{3,67},{4,68},{5,69},{6,70},{7,71},{8,72},{9,... | collective-permute-start | bytes 393224 | tf_op jit(solution)/shard_map/ppermute | solution.py:216
  9.3 1.4 collective-permute-start.9
  14.7 0.7 collective-permute-start
  15.4 0.7 collective-permute-start.1
  16.2 2.1 %collective-permute-start.2 = (bf16[128,2048]{1,0:T(8,128)(2,1)S(1)}, bf16[128,2048]{1,0:T(8,128)(2,1)S(1)}, u32[]{:S(2)}, u32[]{:S(2)}) collective-permute-start(bf16[128,2048]{1,0:T(8,128)(2,1)S(1)} %pad_maximum_fusion), channel_id=1, source_target_pairs={{0,128},{1,129},{2,130},{3,131},{4,132},{5,133},{6,134},{7,135},{8... | collective-permute-start | bytes 1572872 | tf_op jit(solution)/shard_map/cond/branch_1_fun/ppermute | solution.py:216
  16.9 1.4 collective-permute-start.3
  17.6 0.7 collective-permute-start.4
  18.7 44.1 %collective-permute-start.5 = (bf16[64,2048]{1,0:T(8,128)(2,1)S(1)}, bf16[64,2048]{1,0:T(8,128)(2,1)S(1)}, u32[]{:S(2)}, u32[]{:S(2)}) collective-permute-start(bf16[64,2048]{1,0:T(8,128)(2,1)S(1)} %slice.147), channel_id=1, source_target_pairs={{0,16},{1,17},{2,18},{3,19},{4,20},{5,21},{6,22},{7,23},{8,24},{9,... | collective-permute-start | bytes 786440 | tf_op jit(solution)/shard_map/cond/branch_1_fun/ppermute | solution.py:273
  62.8 61.2 %collective-permute-start.10 = (bf16[512,512]{1,0:T(8,128)(2,1)S(1)}, bf16[512,512]{1,0:T(8,128)(2,1)S(1)}, u32[]{:S(2)}, u32[]{:S(2)}) collective-permute-start(bf16[512,512]{1,0:T(8,128)(2,1)S(1)} %get-tuple-element.65.ok.ov), channel_id=1, source_target_pairs={{0,4},{4,8},{8,12},{1,5},{5,9},{9,13},{2,6},{6,10},{10,14},{3,7},{... | collective-permute-start | bytes 1572872 | tf_op jit(solution)/shard_map/ppermute | solution.py:280
  68.0 55.9 %collective-permute-start.11 = (bf16[512,512]{1,0:T(8,128)(2,1)S(1)}, bf16[512,512]{1,0:T(8,128)(2,1)S(1)}, u32[]{:S(2)}, u32[]{:S(2)}) collective-permute-start(bf16[512,512]{1,0:T(8,128)(2,1)S(1)} %get-tuple-element.65.ok.ov), channel_id=1, source_target_pairs={{0,12},{4,0},{1,13},{5,1},{2,14},{6,2},{3,15},{7,3},{16,28},{20,16... | collective-permute-start | bytes 1572872 | tf_op jit(solution)/shard_map/ppermute | solution.py:279
  101.0 7.3 %collective-permute-start.6 = (bf16[1024,512]{1,0:T(8,128)(2,1)}, bf16[1024,512]{1,0:T(8,128)(2,1)}, u32[]{:S(2)}, u32[]{:S(2)}) collective-permute-start(bf16[1024,512]{1,0:T(8,128)(2,1)} %bitcast.4), channel_id=1, source_target_pairs={{0,16},{16,0},{1,17},{17,1},{2,18},{18,2},{3,19},{19,3},{4,20},{20... | collective-permute-start | bytes 3145736 | tf_op jit(solution)/shard_map/cond/branch_1_fun/ppermute | solution.py:284
  124.0 12.0 %collective-permute-start.12 = (bf16[256,512]{1,0:T(8,128)(2,1)S(1)}, bf16[256,512]{1,0:T(8,128)(2,1)S(1)}, u32[]{:S(2)}, u32[]{:S(2)}) collective-permute-start(bf16[256,512]{1,0:T(8,128)(2,1)S(1)} %get-tuple-element.88), channel_id=1, source_target_pairs={{4,8},{8,12},{5,9},{9,13},{6,10},{10,14},{7,11},{11,15},{20,24},{2... | collective-permute-start | bytes 786440 | tf_op jit(solution)/shard_map/ppermute | solution.py:292
  124.7 21.4 %collective-permute-start.13 = (bf16[256,512]{1,0:T(8,128)(2,1)S(1)}, bf16[256,512]{1,0:T(8,128)(2,1)S(1)}, u32[]{:S(2)}, u32[]{:S(2)}) collective-permute-start(bf16[256,512]{1,0:T(8,128)(2,1)S(1)} %get-tuple-element.87), channel_id=1, source_target_pairs={{12,8},{0,12},{13,9},{1,13},{14,10},{2,14},{15,11},{3,15},{28,24},... | collective-permute-start | bytes 786440 | tf_op jit(solution)/shard_map/ppermute | solution.py:293

commit v6 on v5

--- a/solution.py
+++ b/solution.py
@@ -262,8 +262,14 @@
         got = send(held, lambda zl, y, c, zh, x: (0, y, 0, swap[zh], x) if (zl, c) == (0, 0) else None)
         return jnp.concatenate([held, got], 0)
 
+    def pair_and_queries(held):
+        q = exchange(
+            jnp.concatenate([queries[:, n * 512 : (n + 1) * 512] for n in range(HEADS_X)], 0), "x"
+        )
+        return doubled(held, (1, 0, 3, 2)), q
+
     def over_z(held, own):
-        held = doubled(doubled(held, (1, 0, 3, 2)), (3, 2, 1, 0))
+        held = doubled(held, (3, 2, 1, 0))
         first = lambda zl, c: (zl, c) == (0, 0)
         two = send(held, lambda zl, y, c, zh, x: (2, y, 0, zh, x) if first(zl, c) else None)
         one = send(held, lambda zl, y, c, zh, x: (1, y, 0, zh, x) if first(zl, c) else None)
@@ -273,6 +279,7 @@
         moved = lax.ppermute(strip[half:], "c", [(0, 1)])
         return jnp.where(c == 0, strip[:half], moved), own
 
+    held, q = step(pair_and_queries, held)
     strip, own = step(over_z, held, own)
 
     half = rows // 2
@@ -284,9 +291,6 @@
         return here, lax.ppermute(here, "c", [(0, 1), (1, 0)]), where
 
     here, there, where = step(whole_anchor, strip, where)
-    q = exchange(
-        jnp.concatenate([queries[:, n * 512 : (n + 1) * 512] for n in range(HEADS_X)], 0), "x"
-    )
     *state, where = own_part(where, q, own)
     arrived = where[2] >= 0
     got_a2 = lax.ppermute(jnp.where(arrived, got_a[:half], own[:half]), "zh", [(1, 2), (2, 3)])

time: 160 us -> 173 us (1.081)
  the two profiles are of different devices: /device:TPU:1 before, /device:TPU:328 now
where the time goes in v6:
time: 173 us
  waiting for transfers between devices  83.1 us (48%)
  blocking collectives  38.2 us (22%)
  starting transfers between devices  25.3 us (15%)
  Pallas kernels  19.1 us (11%)
  local copies, waits for them, and re-layouts  2.92 us (2%)
  other arithmetic  2.9 us (2%)
    all_to_all x3, blocking collectives, exchange(): return lax.all_to_all(block, axes, split_axis=0, concat_axis=0, tiled=True)  38.2 us
    ppermute x8, waiting for transfers between devices, send(): lax.ppermute(block, AXES, [(device_index(*place), device_index(*to)) for...  34.1 us
    pallas_call x3, Pallas kernels, attention_call(): pl.pallas_call(body, grid_spec=pltpu.PrefetchScalarGridSpec(num_scalar_pr...  19.1 us
    all_to_all x2, waiting for transfers between devices, exchange(): return lax.all_to_all(block, axes, split_axis=0, concat_axis=0, tiled=True)  17.5 us
    ppermute x1, waiting for transfers between devices, local(): got_a = lax.ppermute(own, 'zh', [(0, 1), (1, 2), (2, 3)])  16.3 us
    ppermute x1, waiting for transfers between devices, local(): lax.ppermute(jnp.where(arrived, got_b[half:], own[half:]), 'zh', [(3, 2),...  11 us
    all_to_all x2, starting transfers between devices, exchange(): return lax.all_to_all(block, axes, split_axis=0, concat_axis=0, tiled=True)  7.76 us
    ppermute x8, starting transfers between devices, send(): lax.ppermute(block, AXES, [(device_index(*place), device_index(*to)) for...  6.15 us
  transfers between devices with their start and end apart: 16, of which 7 were waited for; matrix products, arithmetic and copies ran while one was open for 1% of the time, Pallas kernels for 9%

profile of v6, /device:TPU:328, one launch (start us, length us, event | category | flops | bytes accessed | tf_op | source)
XLA Modules:
  0.0 172.5 jit_solution(17367306181580695834)
XLA Ops:
  0.0 1.0 constant_dynamic-update-slice_fusion.3
  1.1 1.0 constant_dynamic-update-slice_fusion.2
  3.5 0.8 collective-permute-start.9
  4.4 0.8 maximum_maximum_fusion.1
  5.2 14.8 %conditional.3 = (bf16[64,2048]{1,0:T(8,128)(2,1)S(1)}, bf16[512,512]{1,0:T(8,128)(2,1)}) conditional(s32[]{:T(128)} %convert_element_type.2, () %tuple.31, (s32[]{:T(128)}, bf16[128,2048]{1,0:T(8,128)(2,1)S(1)}, bf16[32,2048]{1,0:T(8,128)(2,1)S(1)}, s32[]{:T(128)}, bf16[32,2048]{1,0:T(8,128)(2,1)S(1)}, /*index=5*/s32[]{:T(128)}, (), ...), branch_computations={%region_0.1_spmd, %region_1.2_spmd} | conditional | flops 2818051 | bytes 5374070 | solution.py:245
  5.3 0.8 pad_maximum_fusion
  6.1 4.3 %all-to-all-start = ((bf16[4,128,512]{2,1,0:T(8,128)(2,1)}), bf16[4,128,512]{2,1,0:T(8,128)(2,1)}, u32[]{:S(2)}, u32[]{:S(2)}) async-start(bf16[4,128,512]{2,1,0:T(8,128)(2,1)} %bitcast), calls=%async_computation | async-start | bytes 1048576 | tf_op jit(solution)/shard_map/cond/branch_1_fun/all_to_all | solution.py:23
  11.2 8.9 %all-to-all-done = bf16[4,128,512]{2,1,0:T(8,128)(2,1)} async-done(((bf16[4,128,512]{2,1,0:T(8,128)(2,1)}), bf16[4,128,512]{2,1,0:T(8,128)(2,1)}, u32[]{:S(2)}, u32[]{:S(2)}) %all-to-all-start) | async-done | bytes 524320 | tf_op jit(solution)/shard_map/cond/branch_1_fun/all_to_all | solution.py:23
  20.1 3.5 %all-to-all-start.3 = ((bf16[4,128,512]{2,1,0:T(8,128)(2,1)}), bf16[4,128,512]{2,1,0:T(8,128)(2,1)S(1)}, u32[]{:S(2)}, u32[]{:S(2)}) async-start(bf16[4,128,512]{2,1,0:T(8,128)(2,1)} %bitcast.7), calls=%async_computation.3 | async-start | bytes 1048576 | tf_op jit(solution)/shard_map/all_to_all | solution.py:23
  23.6 8.6 %all-to-all-done.3 = bf16[4,128,512]{2,1,0:T(8,128)(2,1)S(1)} async-done(((bf16[4,128,512]{2,1,0:T(8,128)(2,1)}), bf16[4,128,512]{2,1,0:T(8,128)(2,1)S(1)}, u32[]{:S(2)}, u32[]{:S(2)}) %all-to-all-start.3) | async-done | bytes 524320 | tf_op jit(solution)/shard_map/all_to_all | solution.py:23
  32.2 40.2 %conditional.4 = (bf16[64,2048]{1,0:T(8,128)(2,1)S(1)}, bf16[512,512]{1,0:T(8,128)(2,1)S(1)}) conditional(s32[]{:T(128)} %convert_element_type.2, () %tuple.30, (s32[]{:T(128)}, s32[]{:T(128)}, bf16[64,2048]{1,0:T(8,128)(2,1)S(1)}, bf16[4,128,512]{2,1,0:T(8,128)(2,1)S(1)}) %tuple.33), branch_computations={%region_2.3_spmd, %region_3.4_spmd} | conditional | flops 917508 | bytes 14418176 | solution.py:245
  33.6 1.3 collective-permute-start.2
  34.9 0.7 collective-permute-start.3
  35.6 34.1 %collective-permute-done.2 = bf16[128,2048]{1,0:T(8,128)(2,1)S(1)} collective-permute-done((bf16[128,2048]{1,0:T(8,128)(2,1)S(1)}, bf16[128,2048]{1,0:T(8,128)(2,1)S(1)}, u32[]{:S(2)}, u32[]{:S(2)}) %collective-permute-start.2) | collective-permute-done | bytes 524320 | tf_op jit(solution)/shard_map/cond/branch_1_fun/ppermute | solution.py:216
  69.9 1.3 collective-permute-start.4
  71.2 1.1 collective-permute-done.4
  72.4 4.3 %collective-permute-start.10 = (bf16[512,512]{1,0:T(8,128)(2,1)S(1)}, bf16[512,512]{1,0:T(8,128)(2,1)S(1)}, u32[]{:S(2)}, u32[]{:S(2)}) collective-permute-start(bf16[512,512]{1,0:T(8,128)(2,1)S(1)} %get-tuple-element.48.ok.ov), channel_id=1, source_target_pairs={{0,4},{4,8},{8,12},{1,5},{5,9},{9,13},{2,6},{6,10},{10,14},{3,7},{... | collective-permute-start | bytes 1572872 | tf_op jit(solution)/shard_map/ppermute | solution.py:287
  76.7 0.7 collective-permute-start.11
  77.5 30.9 %conditional.5 = (bf16[1024,512]{1,0:T(8,128)(2,1)}, bf16[1024,512]{1,0:T(8,128)(2,1)}, s32[3]{0:T(128)S(1)}) conditional(s32[]{:T(128)} %convert_element_type.2, () %tuple.29, (bf16[64,2048]{1,0:T(8,128)(2,1)S(1)}, s32[3]{0:T(128)S(1)}) %tuple.34), branch_computations={%region_4.5_spmd, %region_5.6_spmd} | conditional | flops 6291456 | bytes 9175104 | solution.py:245
  77.5 9.6 %all_to_all.47 = bf16[4,64,512]{2,1,0:T(8,128)(2,1)S(1)} all-to-all(bf16[4,64,512]{2,1,0:T(8,128)(2,1)S(1)} %bitcast.25), channel_id=1, replica_groups=mesh['zl'=4,'y'=4,'c'=2,'zh'=4,'x'=4] {'x'}, dimensions={0} | all-to-all | bytes 524288 | tf_op jit(solution)/shard_map/cond/branch_1_fun/all_to_all | solution.py:23
  87.2 16.3 %all_to_all.48 = bf16[4,256,512]{2,1,0:T(8,128)(2,1)} all-to-all(bf16[4,256,512]{2,1,0:T(8,128)(2,1)S(1)} %bitcast.22), channel_id=1, replica_groups=mesh['zl'=4,'y'=4,'c'=2,'zh'=4,'x'=4] {'y'}, dimensions={0} | all-to-all | bytes 2097152 | tf_op jit(solution)/shard_map/cond/branch_1_fun/all_to_all | solution.py:23
  103.5 1.9 %collective-permute-start.6 = (bf16[1024,512]{1,0:T(8,128)(2,1)}, bf16[1024,512]{1,0:T(8,128)(2,1)}, u32[]{:S(2)}, u32[]{:S(2)}) collective-permute-start(bf16[1024,512]{1,0:T(8,128)(2,1)} %bitcast.6), channel_id=1, source_target_pairs={{0,16},{16,0},{1,17},{17,1},{2,18},{18,2},{3,19},{19,3},{4,20},{20... | collective-permute-start | bytes 3145736 | tf_op jit(solution)/shard_map/cond/branch_1_fun/ppermute | solution.py:291
  105.4 3.0 %collective-permute-done.6 = bf16[1024,512]{1,0:T(8,128)(2,1)} collective-permute-done((bf16[1024,512]{1,0:T(8,128)(2,1)}, bf16[1024,512]{1,0:T(8,128)(2,1)}, u32[]{:S(2)}, u32[]{:S(2)}) %collective-permute-start.6) | collective-permute-done | bytes 1048608 | tf_op jit(solution)/shard_map/cond/branch_1_fun/ppermute | solution.py:291
  108.4 3.4 %own_attention.1 = (f32[4,1,512]{2,1,0:T(1,128)S(1)}, f32[4,1,512]{2,1,0:T(1,128)S(1)}, f32[4,128,512]{2,1,0:T(8,128)S(1)}, s32[3]{0:T(128)S(1)}) custom-call(s32[3]{0:T(128)S(1)} %get-tuple-element.46.where_ref, bf16[512,512]{1,0:T(8,128)(2,1)} %get-tuple-element.47.q_ref, bf16[512,512]{1,0:T(8,128)(2,1)S(1)} %get-tuple-element.48.ok.ov, ...), custom_call_target="tpu_custom_call" | custom-call | flops 8388608 | bytes 131072 | tf_op jit(solution)/shard_map/own_attention/pallas_call | solution.py:144
  113.0 16.3 %collective-permute-done.10.ak.av = bf16[512,512]{1,0:T(8,128)(2,1)S(1)} collective-permute-done((bf16[512,512]{1,0:T(8,128)(2,1)S(1)}, bf16[512,512]{1,0:T(8,128)(2,1)S(1)}, u32[]{:S(2)}, u32[]{:S(2)}) %collective-permute-start.10) | collective-permute-done | bytes 524320 | tf_op jit(solution)/shard_map/ppermute | solution.py:287
  129.4 1.9 %collective-permute-start.12 = (bf16[256,512]{1,0:T(8,128)(2,1)S(1)}, bf16[256,512]{1,0:T(8,128)(2,1)S(1)}, u32[]{:S(2)}, u32[]{:S(2)}) collective-permute-start(bf16[256,512]{1,0:T(8,128)(2,1)S(1)} %get-tuple-element.96), channel_id=1, source_target_pairs={{4,8},{8,12},{5,9},{9,13},{6,10},{10,14},{7,11},{11,15},{20,24},{2... | collective-permute-start | bytes 786440 | tf_op jit(solution)/shard_map/ppermute | solution.py:296
  131.3 1.3 collective-permute-start.13
  132.6 11.5 %middle_attention.1 = (f32[4,1,512]{2,1,0:T(1,128)S(1)}, f32[4,1,512]{2,1,0:T(1,128)S(1)}, f32[4,128,512]{2,1,0:T(8,128)S(1)}) custom-call(s32[3]{0:T(128)S(1)} %get-tuple-element.49.where_ref, bf16[512,512]{1,0:T(8,128)(2,1)} %get-tuple-element.47.q_ref, f32[4,1,512]{2,1,0:T(1,128)S(1)} %get-tuple-element.50.p_ref, ...), custom_call_target="tpu_custom_call" | custom-call | flops 3221225472 | bytes 8388608 | tf_op jit(solution)/shard_map/middle_attention/pallas_call | solution.py:144
  144.1 11.0 %collective-permute-done.13.bk.bv = bf16[256,512]{1,0:T(8,128)(2,1)S(1)} collective-permute-done((bf16[256,512]{1,0:T(8,128)(2,1)S(1)}, bf16[256,512]{1,0:T(8,128)(2,1)S(1)}, u32[]{:S(2)}, u32[]{:S(2)}) %collective-permute-start.13) | collective-permute-done | bytes 262176 | tf_op jit(solution)/shard_map/ppermute | solution.py:297
  155.2 4.2 %last_attention.1 = bf16[512,512]{1,0:T(8,128)(2,1)S(1)} custom-call(s32[3]{0:T(128)S(1)} %get-tuple-element.49.where_ref, bf16[512,512]{1,0:T(8,128)(2,1)} %get-tuple-element.47.q_ref, f32[4,1,512]{2,1,0:T(1,128)S(1)} %get-tuple-element.55.peak_ref, f32[4,1,512]{2,1,0:T(1,128)S(1)} %get-tuple-element.56.total_ref, ...), custom_call_target="tpu_custom_call" | custom-call | flops 536870912 | bytes 8388608 | tf_op jit(solution)/shard_map/last_attention/pallas_call | solution.py:144
  159.3 12.3 %all_to_all.49 = bf16[4,128,512]{2,1,0:T(8,128)(2,1)S(1)} all-to-all(bf16[4,128,512]{2,1,0:T(8,128)(2,1)S(1)} %bitcast.21), channel_id=1, replica_groups=mesh['zl'=4,'y'=4,'c'=2,'zh'=4,'x'=4] {'x'}, dimensions={0} | all-to-all | bytes 1048576 | tf_op jit(solution)/shard_map/all_to_all | solution.py:23
  171.7 0.8 pad_maximum_fusion.3
  (39 shorter events, 4.6 us)
Async XLA Ops:
  0.0 4.3 %copy-start = (bf16[128,1024]{1,0:T(8,128)(2,1)S(1)}, bf16[128,1024]{1,0:T(8,128)(2,1)}, u32[]{:S(2)}) copy-start(bf16[128,1024]{1,0:T(8,128)(2,1)} %param.10) | copy-start | bytes 786436
  1.0 3.3 %copy-start.1 = (bf16[128,1024]{1,0:T(8,128)(2,1)S(1)}, bf16[128,1024]{1,0:T(8,128)(2,1)}, u32[]{:S(2)}) copy-start(bf16[128,1024]{1,0:T(8,128)(2,1)} %param.11) | copy-start | bytes 786436
  2.1 3.1 %collective-permute-start.7 = (bf16[32,2048]{1,0:T(8,128)(2,1)S(1)}, bf16[32,2048]{1,0:T(8,128)(2,1)S(1)}, u32[]{:S(2)}, u32[]{:S(2)}) collective-permute-start(bf16[32,2048]{1,0:T(8,128)(2,1)S(1)} %get-tuple-element.99), channel_id=1, source_target_pairs={{0,96},{1,97},{2,98},{3,99},{4,100},{5,101},{6,102},{7,103},{8,104... | collective-permute-start | bytes 393224 | tf_op jit(solution)/shard_map/ppermute | solution.py:216
  2.8 2.4 %collective-permute-start.8 = (bf16[32,2048]{1,0:T(8,128)(2,1)S(1)}, bf16[32,2048]{1,0:T(8,128)(2,1)S(1)}, u32[]{:S(2)}, u32[]{:S(2)}) collective-permute-start(bf16[32,2048]{1,0:T(8,128)(2,1)S(1)} %get-tuple-element.98), channel_id=1, source_target_pairs={{0,64},{1,65},{2,66},{3,67},{4,68},{5,69},{6,70},{7,71},{8,72},{9,... | collective-permute-start | bytes 393224 | tf_op jit(solution)/shard_map/ppermute | solution.py:216
  3.5 1.8 %copy-start.2 = (bf16[128,2048]{1,0:T(8,128)(2,1)S(1)}, bf16[128,2048]{1,0:T(8,128)(2,1)}, u32[]{:S(2)}) copy-start(bf16[128,2048]{1,0:T(8,128)(2,1)} %param.9) | copy-start | bytes 1572868
  3.5 1.7 %collective-permute-start.9 = (bf16[32,2048]{1,0:T(8,128)(2,1)S(1)}, bf16[32,2048]{1,0:T(8,128)(2,1)S(1)}, u32[]{:S(2)}, u32[]{:S(2)}) collective-permute-start(bf16[32,2048]{1,0:T(8,128)(2,1)S(1)} %get-tuple-element.97), channel_id=1, source_target_pairs={{0,32},{1,33},{2,34},{3,35},{4,36},{5,37},{6,38},{7,39},{8,40},{9,... | collective-permute-start | bytes 393224 | tf_op jit(solution)/shard_map/ppermute | solution.py:216
  6.1 14.0 %all-to-all-start = ((bf16[4,128,512]{2,1,0:T(8,128)(2,1)}), bf16[4,128,512]{2,1,0:T(8,128)(2,1)}, u32[]{:S(2)}, u32[]{:S(2)}) async-start(bf16[4,128,512]{2,1,0:T(8,128)(2,1)} %bitcast), calls=%async_computation | async-start | bytes 1048576 | tf_op jit(solution)/shard_map/cond/branch_1_fun/all_to_all | solution.py:23
  10.4 0.7 collective-permute-start.5
  20.1 12.1 %all-to-all-start.3 = ((bf16[4,128,512]{2,1,0:T(8,128)(2,1)}), bf16[4,128,512]{2,1,0:T(8,128)(2,1)S(1)}, u32[]{:S(2)}, u32[]{:S(2)}) async-start(bf16[4,128,512]{2,1,0:T(8,128)(2,1)} %bitcast.7), calls=%async_computation.3 | async-start | bytes 1048576 | tf_op jit(solution)/shard_map/all_to_all | solution.py:23
  32.2 0.7 collective-permute-start
  32.9 2.7 %collective-permute-start.1 = (bf16[128,2048]{1,0:T(8,128)(2,1)S(1)}, bf16[128,2048]{1,0:T(8,128)(2,1)S(1)}, u32[]{:S(2)}, u32[]{:S(2)}) collective-permute-start(bf16[128,2048]{1,0:T(8,128)(2,1)S(1)} %constant_dynamic-update-slice_fusion), channel_id=1, source_target_pairs={{0,128},{1,129},{2,130},{3,131},{4,132},{5,133},{6,134},{7,135},{8... | collective-permute-start | bytes 1572872 | tf_op jit(solution)/shard_map/cond/branch_1_fun/ppermute | solution.py:216
  33.6 36.1 %collective-permute-start.2 = (bf16[128,2048]{1,0:T(8,128)(2,1)S(1)}, bf16[128,2048]{1,0:T(8,128)(2,1)S(1)}, u32[]{:S(2)}, u32[]{:S(2)}) collective-permute-start(bf16[128,2048]{1,0:T(8,128)(2,1)S(1)} %constant_dynamic-update-slice_fusion), channel_id=1, source_target_pairs={{0,256},{1,257},{2,258},{3,259},{4,260},{5,261},{6,262},{7,263},{8... | collective-permute-start | bytes 1572872 | tf_op jit(solution)/shard_map/cond/branch_1_fun/ppermute | solution.py:216
  34.9 34.8 %collective-permute-start.3 = (bf16[128,2048]{1,0:T(8,128)(2,1)S(1)}, bf16[128,2048]{1,0:T(8,128)(2,1)S(1)}, u32[]{:S(2)}, u32[]{:S(2)}) collective-permute-start(bf16[128,2048]{1,0:T(8,128)(2,1)S(1)} %constant_dynamic-update-slice_fusion), channel_id=1, source_target_pairs={{0,396},{1,397},{2,398},{3,399},{4,384},{5,385},{6,386},{7,387},{8... | collective-permute-start | bytes 1572872 | tf_op jit(solution)/shard_map/cond/branch_1_fun/ppermute | solution.py:216
  69.9 2.4 %collective-permute-start.4 = (bf16[64,2048]{1,0:T(8,128)(2,1)S(1)}, bf16[64,2048]{1,0:T(8,128)(2,1)S(1)}, u32[]{:S(2)}, u32[]{:S(2)}) collective-permute-start(bf16[64,2048]{1,0:T(8,128)(2,1)S(1)} %slice.144), channel_id=1, source_target_pairs={{0,16},{1,17},{2,18},{3,19},{4,20},{5,21},{6,22},{7,23},{8,24},{9,... | collective-permute-start | bytes 786440 | tf_op jit(solution)/shard_map/cond/branch_1_fun/ppermute | solution.py:279
  72.4 57.0 %collective-permute-start.10 = (bf16[512,512]{1,0:T(8,128)(2,1)S(1)}, bf16[512,512]{1,0:T(8,128)(2,1)S(1)}, u32[]{:S(2)}, u32[]{:S(2)}) collective-permute-start(bf16[512,512]{1,0:T(8,128)(2,1)S(1)} %get-tuple-element.48.ok.ov), channel_id=1, source_target_pairs={{0,4},{4,8},{8,12},{1,5},{5,9},{9,13},{2,6},{6,10},{10,14},{3,7},{... | collective-permute-start | bytes 1572872 | tf_op jit(solution)/shard_map/ppermute | solution.py:287
  76.7 52.7 %collective-permute-start.11 = (bf16[512,512]{1,0:T(8,128)(2,1)S(1)}, bf16[512,512]{1,0:T(8,128)(2,1)S(1)}, u32[]{:S(2)}, u32[]{:S(2)}) collective-permute-start(bf16[512,512]{1,0:T(8,128)(2,1)S(1)} %get-tuple-element.48.ok.ov), channel_id=1, source_target_pairs={{0,12},{4,0},{1,13},{5,1},{2,14},{6,2},{3,15},{7,3},{16,28},{20,16... | collective-permute-start | bytes 1572872 | tf_op jit(solution)/shard_map/ppermute | solution.py:286
  103.5 4.9 %collective-permute-start.6 = (bf16[1024,512]{1,0:T(8,128)(2,1)}, bf16[1024,512]{1,0:T(8,128)(2,1)}, u32[]{:S(2)}, u32[]{:S(2)}) collective-permute-start(bf16[1024,512]{1,0:T(8,128)(2,1)} %bitcast.6), channel_id=1, source_target_pairs={{0,16},{16,0},{1,17},{17,1},{2,18},{18,2},{3,19},{19,3},{4,20},{20... | collective-permute-start | bytes 3145736 | tf_op jit(solution)/shard_map/cond/branch_1_fun/ppermute | solution.py:291
  129.4 14.7 %collective-permute-start.12 = (bf16[256,512]{1,0:T(8,128)(2,1)S(1)}, bf16[256,512]{1,0:T(8,128)(2,1)S(1)}, u32[]{:S(2)}, u32[]{:S(2)}) collective-permute-start(bf16[256,512]{1,0:T(8,128)(2,1)S(1)} %get-tuple-element.96), channel_id=1, source_target_pairs={{4,8},{8,12},{5,9},{9,13},{6,10},{10,14},{7,11},{11,15},{20,24},{2... | collective-permute-start | bytes 786440 | tf_op jit(solution)/shard_map/ppermute | solution.py:296
  131.3 23.8 %collective-permute-start.13 = (bf16[256,512]{1,0:T(8,128)(2,1)S(1)}, bf16[256,512]{1,0:T(8,128)(2,1)S(1)}, u32[]{:S(2)}, u32[]{:S(2)}) collective-permute-start(bf16[256,512]{1,0:T(8,128)(2,1)S(1)} %get-tuple-element.95), channel_id=1, source_target_pairs={{12,8},{0,12},{13,9},{1,13},{14,10},{2,14},{15,11},{3,15},{28,24},... | collective-permute-start | bytes 786440 | tf_op jit(solution)/shard_map/ppermute | solution.py:297

commit v7 on v5

--- a/solution.py
+++ b/solution.py
@@ -280,7 +280,7 @@
     got_a = lax.ppermute(own, "zh", [(0, 1), (1, 2), (2, 3)])
 
     def whole_anchor(strip, where):
-        here = gathered(exchange(of_heads(strip), "x"), "y", 4)
+        here = gathered(of_heads(strip), ("y", "x"), 4)
         return here, lax.ppermute(here, "c", [(0, 1), (1, 0)]), where
 
     here, there, where = step(whole_anchor, strip, where)

time: 160 us -> 156 us (0.975)
  blocking collectives: 51.3 us -> 46.9 us
  waiting for transfers between devices: 59.4 us -> 57.7 us
    all_to_all x4 -> x3, blocking collectives: 51.3 us -> 46.9 us  [exchange(): return lax.all_to_all(block, axes, split_axis=0, concat_axis=0, tiled=True)]
    ppermute x1, waiting for transfers between devices: 10.1 us -> 8.42 us  [local(): lax.ppermute(jnp.where(arrived, got_b[half:], own[half:]), 'zh', [(3, 2),...]
  transfers between devices with their start and end apart: 15 -> 15, of which waited for: 4 -> 4; matrix products, arithmetic and copies ran while one was open for 2% -> 2% of each run, Pallas kernels for 7% -> 8%
where the time goes in v7:
time: 156 us; the launch traced here: 154 us
  waiting for transfers between devices  57.7 us (37%)
  blocking collectives  46.9 us (30%)
  starting transfers between devices  28.7 us (18%)
  Pallas kernels  13 us (8%)
  local copies, waits for them, and re-layouts  3.48 us (2%)
  other arithmetic  3.32 us (2%)
    all_to_all x3, blocking collectives, exchange(): return lax.all_to_all(block, axes, split_axis=0, concat_axis=0, tiled=True)  46.9 us
    ppermute x1, waiting for transfers between devices, over_z(): moved = lax.ppermute(strip[half:], 'c', [(0, 1)])  43.6 us
    pallas_call x3, Pallas kernels, attention_call(): pl.pallas_call(body, grid_spec=pltpu.PrefetchScalarGridSpec(num_scalar_pr...  13 us
    ppermute x1, waiting for transfers between devices, local(): lax.ppermute(jnp.where(arrived, got_b[half:], own[half:]), 'zh', [(3, 2),...  8.42 us
    ppermute x8, starting transfers between devices, send(): lax.ppermute(block, AXES, [(device_index(*place), device_index(*to)) for...  5.57 us
    ppermute x1, starting transfers between devices, local(): got_a = lax.ppermute(own, 'zh', [(0, 1), (1, 2), (2, 3)])  5.21 us
    all_to_all x1, starting transfers between devices, exchange(): return lax.all_to_all(block, axes, split_axis=0, concat_axis=0, tiled=True)  4.84 us
    ppermute x1, starting transfers between devices, local(): lax.ppermute(jnp.where(arrived, got_b[half:], own[half:]), 'zh', [(3, 2),...  3.73 us
  transfers between devices with their start and end apart: 15, of which 4 were waited for; matrix products, arithmetic and copies ran while one was open for 2% of the time, Pallas kernels for 8%

profile of v7, /device:TPU:1, one launch (start us, length us, event | category | flops | bytes accessed | tf_op | source)
XLA Modules:
  0.0 154.1 jit_solution(2566088639154181640)
XLA Ops:
  0.0 1.0 fusion.4
  1.1 0.8 maximum_maximum_fusion
  1.9 4.8 %all-to-all-start.1 = ((bf16[4,128,512]{2,1,0:T(8,128)(2,1)}), bf16[4,128,512]{2,1,0:T(8,128)(2,1)S(1)}, u32[]{:S(2)}, u32[]{:S(2)}) async-start(bf16[4,128,512]{2,1,0:T(8,128)(2,1)} %bitcast.3), calls=%async_computation.1 | async-start | bytes 1048576 | tf_op jit(solution)/shard_map/all_to_all | solution.py:23
  6.8 0.9 copy-done.1
  7.8 0.8 collective-permute-start.7
  8.6 0.7 collective-permute-start.8
  9.3 0.7 collective-permute-start.9
  10.0 0.7 fusion.1
  10.7 3.0 %all-to-all-done.1 = bf16[4,128,512]{2,1,0:T(8,128)(2,1)S(1)} async-done(((bf16[4,128,512]{2,1,0:T(8,128)(2,1)}), bf16[4,128,512]{2,1,0:T(8,128)(2,1)S(1)}, u32[]{:S(2)}, u32[]{:S(2)}) %all-to-all-start.1) | async-done | bytes 524320 | tf_op jit(solution)/shard_map/all_to_all | solution.py:23
  13.7 49.0 %conditional.2 = (bf16[64,2048]{1,0:T(8,128)(2,1)S(1)}, bf16[512,512]{1,0:T(8,128)(2,1)S(1)}) conditional(s32[]{:T(128)} %convert_element_type.4, () %tuple.29, (s32[]{:T(128)}, s32[]{:T(128)}, s32[]{:T(128)}, bf16[128,2048]{1,0:T(8,128)(2,1)S(1)}, bf16[32,2048]{1,0:T(8,128)(2,1)S(1)}, /*index=5*/bf16[32,2048]{1,0:T(8,128)(2,1)S(1)}, ...), branch_computations={%region_0.1_spmd, %region_1.2_spmd} | conditional | flops 4784135 | bytes 16122182 | solution.py:245
  14.5 0.7 collective-permute-start.1
  15.2 0.7 collective-permute-start.2
  15.9 0.7 collective-permute-start.3
  16.6 0.7 collective-permute-start.4
  17.7 1.3 collective-permute-start.5
  19.1 43.6 %collective-permute-done.5 = bf16[64,2048]{1,0:T(8,128)(2,1)S(1)} collective-permute-done((bf16[64,2048]{1,0:T(8,128)(2,1)S(1)}, bf16[64,2048]{1,0:T(8,128)(2,1)S(1)}, u32[]{:S(2)}, u32[]{:S(2)}) %collective-permute-start.5) | collective-permute-done | bytes 262176 | tf_op jit(solution)/shard_map/cond/branch_1_fun/ppermute | solution.py:273
  62.7 5.2 %collective-permute-start.10 = (bf16[512,512]{1,0:T(8,128)(2,1)S(1)}, bf16[512,512]{1,0:T(8,128)(2,1)S(1)}, u32[]{:S(2)}, u32[]{:S(2)}) collective-permute-start(bf16[512,512]{1,0:T(8,128)(2,1)S(1)} %get-tuple-element.65.ok.ov), channel_id=1, source_target_pairs={{0,4},{4,8},{8,12},{1,5},{5,9},{9,13},{2,6},{6,10},{10,14},{3,7},{... | collective-permute-start | bytes 1572872 | tf_op jit(solution)/shard_map/ppermute | solution.py:280
  68.0 3.6 %collective-permute-start.11 = (bf16[512,512]{1,0:T(8,128)(2,1)S(1)}, bf16[512,512]{1,0:T(8,128)(2,1)S(1)}, u32[]{:S(2)}, u32[]{:S(2)}) collective-permute-start(bf16[512,512]{1,0:T(8,128)(2,1)S(1)} %get-tuple-element.65.ok.ov), channel_id=1, source_target_pairs={{0,12},{4,0},{1,13},{5,1},{2,14},{6,2},{3,15},{7,3},{16,28},{20,16... | collective-permute-start | bytes 1572872 | tf_op jit(solution)/shard_map/ppermute | solution.py:279
  71.7 0.9 pad_maximum_fusion.6
  72.6 30.5 %conditional.3 = (bf16[1024,512]{1,0:T(8,128)(2,1)}, bf16[1024,512]{1,0:T(8,128)(2,1)}, s32[3]{0:T(128)S(1)}) conditional(s32[]{:T(128)} %convert_element_type.4, () %tuple.28, (bf16[64,2048]{1,0:T(8,128)(2,1)S(1)}, s32[3]{0:T(128)S(1)}) %tuple.31), branch_computations={%region_2.3_spmd, %region_3.4_spmd} | conditional | flops 2097151 | bytes 8912960 | solution.py:245
  72.9 23.9 %all_to_all.40 = bf16[16,64,512]{2,1,0:T(8,128)(2,1)} all-to-all(bf16[16,64,512]{2,1,0:T(8,128)(2,1)S(1)} %bitcast.25), channel_id=1, replica_groups=mesh['zl'=4,'y'=4,'c'=2,'zh'=4,'x'=4] {'y','x'}, dimensions={0} | all-to-all | bytes 2097152 | tf_op jit(solution)/shard_map/cond/branch_1_fun/all_to_all | solution.py:23
  96.8 3.7 %collective-permute-start.6 = (bf16[1024,512]{1,0:T(8,128)(2,1)}, bf16[1024,512]{1,0:T(8,128)(2,1)}, u32[]{:S(2)}, u32[]{:S(2)}) collective-permute-start(bf16[1024,512]{1,0:T(8,128)(2,1)} %bitcast.2), channel_id=1, source_target_pairs={{0,16},{16,0},{1,17},{17,1},{2,18},{18,2},{3,19},{19,3},{4,20},{20... | collective-permute-start | bytes 3145736 | tf_op jit(solution)/shard_map/cond/branch_1_fun/ppermute | solution.py:284
  100.5 2.6 %collective-permute-done.6 = bf16[1024,512]{1,0:T(8,128)(2,1)} collective-permute-done((bf16[1024,512]{1,0:T(8,128)(2,1)}, bf16[1024,512]{1,0:T(8,128)(2,1)}, u32[]{:S(2)}, u32[]{:S(2)}) %collective-permute-start.6) | collective-permute-done | bytes 1048608 | tf_op jit(solution)/shard_map/cond/branch_1_fun/ppermute | solution.py:284
  103.1 11.6 %all_to_all.41 = bf16[4,128,512]{2,1,0:T(8,128)(2,1)S(1)} all-to-all(bf16[4,128,512]{2,1,0:T(8,128)(2,1)S(1)} %bitcast.24), channel_id=1, replica_groups=mesh['zl'=4,'y'=4,'c'=2,'zh'=4,'x'=4] {'x'}, dimensions={0} | all-to-all | bytes 1048576 | tf_op jit(solution)/shard_map/all_to_all | solution.py:23
  114.8 2.8 %own_attention.1 = (f32[4,1,512]{2,1,0:T(1,128)S(1)}, f32[4,1,512]{2,1,0:T(1,128)S(1)}, f32[4,128,512]{2,1,0:T(8,128)S(1)}, s32[3]{0:T(128)S(1)}) custom-call(s32[3]{0:T(128)S(1)} %get-tuple-element.64.where_ref, bf16[512,512]{1,0:T(8,128)(2,1)S(1)} %bitcast.19, bf16[512,512]{1,0:T(8,128)(2,1)S(1)} %get-tuple-element.65.ok.ov, ...), custom_call_target="tpu_custom_call" | custom-call | flops 8388608 | bytes 131072 | tf_op jit(solution)/shard_map/own_attention/pallas_call | solution.py:144
  118.9 0.7 collective-permute-start.12
  119.6 3.7 %collective-permute-start.13 = (bf16[256,512]{1,0:T(8,128)(2,1)S(1)}, bf16[256,512]{1,0:T(8,128)(2,1)S(1)}, u32[]{:S(2)}, u32[]{:S(2)}) collective-permute-start(bf16[256,512]{1,0:T(8,128)(2,1)S(1)} %get-tuple-element.87), channel_id=1, source_target_pairs={{12,8},{0,12},{13,9},{1,13},{14,10},{2,14},{15,11},{3,15},{28,24},... | collective-permute-start | bytes 786440 | tf_op jit(solution)/shard_map/ppermute | solution.py:293
  123.3 9.0 %middle_attention.1 = (f32[4,1,512]{2,1,0:T(1,128)S(1)}, f32[4,1,512]{2,1,0:T(1,128)S(1)}, f32[4,128,512]{2,1,0:T(8,128)S(1)}) custom-call(s32[3]{0:T(128)S(1)} %get-tuple-element.66.where_ref, bf16[512,512]{1,0:T(8,128)(2,1)S(1)} %bitcast.20, f32[4,1,512]{2,1,0:T(1,128)S(1)} %get-tuple-element.67.p_ref, f32[4,1,512]{2,1,0:T(1,128)S(1)} %get-tuple-element.68.t_ref, ...), custom_call_target="tpu_custom_call" | custom-call | flops 3221225472 | bytes 8388608 | tf_op jit(solution)/shard_map/middle_attention/pallas_call | solution.py:144
  132.4 8.4 %collective-permute-done.13.bk.bv = bf16[256,512]{1,0:T(8,128)(2,1)S(1)} collective-permute-done((bf16[256,512]{1,0:T(8,128)(2,1)S(1)}, bf16[256,512]{1,0:T(8,128)(2,1)S(1)}, u32[]{:S(2)}, u32[]{:S(2)}) %collective-permute-start.13) | collective-permute-done | bytes 262176 | tf_op jit(solution)/shard_map/ppermute | solution.py:293
  140.8 1.2 last_attention.1
  141.9 11.3 %all_to_all.42 = bf16[4,128,512]{2,1,0:T(8,128)(2,1)S(1)} all-to-all(bf16[4,128,512]{2,1,0:T(8,128)(2,1)S(1)} %bitcast.22), channel_id=1, replica_groups=mesh['zl'=4,'y'=4,'c'=2,'zh'=4,'x'=4] {'x'}, dimensions={0} | all-to-all | bytes 1048576 | tf_op jit(solution)/shard_map/all_to_all | solution.py:23
  153.3 0.8 pad_maximum_fusion.7
  (49 shorter events, 2.3 us)
Async XLA Ops:
  0.0 1.1 copy-start
  1.9 11.8 %all-to-all-start.1 = ((bf16[4,128,512]{2,1,0:T(8,128)(2,1)}), bf16[4,128,512]{2,1,0:T(8,128)(2,1)S(1)}, u32[]{:S(2)}, u32[]{:S(2)}) async-start(bf16[4,128,512]{2,1,0:T(8,128)(2,1)} %bitcast.3), calls=%async_computation.1 | async-start | bytes 1048576 | tf_op jit(solution)/shard_map/all_to_all | solution.py:23
  6.8 0.9 copy-start.1
  7.8 2.2 %copy-start.2 = (bf16[128,2048]{1,0:T(8,128)(2,1)S(1)}, bf16[128,2048]{1,0:T(8,128)(2,1)}, u32[]{:S(2)}) copy-start(bf16[128,2048]{1,0:T(8,128)(2,1)} %param.7) | copy-start | bytes 1572868
  7.8 2.9 %collective-permute-start.7 = (bf16[32,2048]{1,0:T(8,128)(2,1)S(1)}, bf16[32,2048]{1,0:T(8,128)(2,1)S(1)}, u32[]{:S(2)}, u32[]{:S(2)}) collective-permute-start(bf16[32,2048]{1,0:T(8,128)(2,1)S(1)} %get-tuple-element.95), channel_id=1, source_target_pairs={{0,32},{1,33},{2,34},{3,35},{4,36},{5,37},{6,38},{7,39},{8,40},{9,... | collective-permute-start | bytes 393224 | tf_op jit(solution)/shard_map/ppermute | solution.py:216
  8.6 2.1 %collective-permute-start.8 = (bf16[32,2048]{1,0:T(8,128)(2,1)S(1)}, bf16[32,2048]{1,0:T(8,128)(2,1)S(1)}, u32[]{:S(2)}, u32[]{:S(2)}) collective-permute-start(bf16[32,2048]{1,0:T(8,128)(2,1)S(1)} %get-tuple-element.94), channel_id=1, source_target_pairs={{0,64},{1,65},{2,66},{3,67},{4,68},{5,69},{6,70},{7,71},{8,72},{9,... | collective-permute-start | bytes 393224 | tf_op jit(solution)/shard_map/ppermute | solution.py:216
  9.3 1.4 collective-permute-start.9
  13.7 0.7 collective-permute-start
  14.5 0.7 collective-permute-start.1
  15.2 2.1 %collective-permute-start.2 = (bf16[128,2048]{1,0:T(8,128)(2,1)S(1)}, bf16[128,2048]{1,0:T(8,128)(2,1)S(1)}, u32[]{:S(2)}, u32[]{:S(2)}) collective-permute-start(bf16[128,2048]{1,0:T(8,128)(2,1)S(1)} %pad_maximum_fusion), channel_id=1, source_target_pairs={{0,128},{1,129},{2,130},{3,131},{4,132},{5,133},{6,134},{7,135},{8... | collective-permute-start | bytes 1572872 | tf_op jit(solution)/shard_map/cond/branch_1_fun/ppermute | solution.py:216
  15.9 1.4 collective-permute-start.3
  16.6 0.7 collective-permute-start.4
  17.7 45.0 %collective-permute-start.5 = (bf16[64,2048]{1,0:T(8,128)(2,1)S(1)}, bf16[64,2048]{1,0:T(8,128)(2,1)S(1)}, u32[]{:S(2)}, u32[]{:S(2)}) collective-permute-start(bf16[64,2048]{1,0:T(8,128)(2,1)S(1)} %slice.147), channel_id=1, source_target_pairs={{0,16},{1,17},{2,18},{3,19},{4,20},{5,21},{6,22},{7,23},{8,24},{9,... | collective-permute-start | bytes 786440 | tf_op jit(solution)/shard_map/cond/branch_1_fun/ppermute | solution.py:273
  62.7 56.1 %collective-permute-start.10 = (bf16[512,512]{1,0:T(8,128)(2,1)S(1)}, bf16[512,512]{1,0:T(8,128)(2,1)S(1)}, u32[]{:S(2)}, u32[]{:S(2)}) collective-permute-start(bf16[512,512]{1,0:T(8,128)(2,1)S(1)} %get-tuple-element.65.ok.ov), channel_id=1, source_target_pairs={{0,4},{4,8},{8,12},{1,5},{5,9},{9,13},{2,6},{6,10},{10,14},{3,7},{... | collective-permute-start | bytes 1572872 | tf_op jit(solution)/shard_map/ppermute | solution.py:280
  68.0 50.8 %collective-permute-start.11 = (bf16[512,512]{1,0:T(8,128)(2,1)S(1)}, bf16[512,512]{1,0:T(8,128)(2,1)S(1)}, u32[]{:S(2)}, u32[]{:S(2)}) collective-permute-start(bf16[512,512]{1,0:T(8,128)(2,1)S(1)} %get-tuple-element.65.ok.ov), channel_id=1, source_target_pairs={{0,12},{4,0},{1,13},{5,1},{2,14},{6,2},{3,15},{7,3},{16,28},{20,16... | collective-permute-start | bytes 1572872 | tf_op jit(solution)/shard_map/ppermute | solution.py:279
  96.8 6.3 %collective-permute-start.6 = (bf16[1024,512]{1,0:T(8,128)(2,1)}, bf16[1024,512]{1,0:T(8,128)(2,1)}, u32[]{:S(2)}, u32[]{:S(2)}) collective-permute-start(bf16[1024,512]{1,0:T(8,128)(2,1)} %bitcast.2), channel_id=1, source_target_pairs={{0,16},{16,0},{1,17},{17,1},{2,18},{18,2},{3,19},{19,3},{4,20},{20... | collective-permute-start | bytes 3145736 | tf_op jit(solution)/shard_map/cond/branch_1_fun/ppermute | solution.py:284
  118.9 13.5 %collective-permute-start.12 = (bf16[256,512]{1,0:T(8,128)(2,1)S(1)}, bf16[256,512]{1,0:T(8,128)(2,1)S(1)}, u32[]{:S(2)}, u32[]{:S(2)}) collective-permute-start(bf16[256,512]{1,0:T(8,128)(2,1)S(1)} %get-tuple-element.88), channel_id=1, source_target_pairs={{4,8},{8,12},{5,9},{9,13},{6,10},{10,14},{7,11},{11,15},{20,24},{2... | collective-permute-start | bytes 786440 | tf_op jit(solution)/shard_map/ppermute | solution.py:292
  119.6 21.2 %collective-permute-start.13 = (bf16[256,512]{1,0:T(8,128)(2,1)S(1)}, bf16[256,512]{1,0:T(8,128)(2,1)S(1)}, u32[]{:S(2)}, u32[]{:S(2)}) collective-permute-start(bf16[256,512]{1,0:T(8,128)(2,1)S(1)} %get-tuple-element.87), channel_id=1, source_target_pairs={{12,8},{0,12},{13,9},{1,13},{14,10},{2,14},{15,11},{3,15},{28,24},... | collective-permute-start | bytes 786440 | tf_op jit(solution)/shard_map/ppermute | solution.py:293

commit v8 on v7

--- a/solution.py
+++ b/solution.py
@@ -188,6 +188,7 @@
         state_specs(rows),
         [jax.ShapeDtypeStruct(shape, F32) for shape in state_shapes(4, rows)],
         [],
+        10**6,
     )
 
 
@@ -284,13 +285,16 @@
         return here, lax.ppermute(here, "c", [(0, 1), (1, 0)]), where
 
     here, there, where = step(whole_anchor, strip, where)
-    q = exchange(
-        jnp.concatenate([queries[:, n * 512 : (n + 1) * 512] for n in range(HEADS_X)], 0), "x"
-    )
-    *state, where = own_part(where, q, own)
     arrived = where[2] >= 0
     got_a2 = lax.ppermute(jnp.where(arrived, got_a[:half], own[:half]), "zh", [(1, 2), (2, 3)])
     got_b2 = lax.ppermute(jnp.where(arrived, got_b[half:], own[half:]), "zh", [(3, 2), (0, 3)])
+    def queries_and_own(where):
+        q = exchange(
+            jnp.concatenate([queries[:, n * 512 : (n + 1) * 512] for n in range(HEADS_X)], 0), "x"
+        )
+        return q, *own_part(where, q, own)
+
+    q, *state, where = step(queries_and_own, where)
     state = middle(where, q, state, (got_a, got_b, here, there))
     out = exchange(last(where, q, state, (got_a2, got_b2)), "x")
     width = rows // HEADS_X

time: 156 us -> 171 us (1.096)
  the two profiles are of different devices: /device:TPU:1 before, /device:TPU:472 now
where the time goes in v8:
time: 171 us; the launch traced here: 170 us
  waiting for transfers between devices  51.7 us (30%)
  blocking collectives  47.9 us (28%)
  starting transfers between devices  43.3 us (25%)
  Pallas kernels  20.1 us (12%)
  other arithmetic  3.12 us (2%)
  local copies, waits for them, and re-layouts  2.82 us (2%)
    all_to_all x3, blocking collectives, exchange(): return lax.all_to_all(block, axes, split_axis=0, concat_axis=0, tiled=True)  47.9 us
    ppermute x8, waiting for transfers between devices, send(): lax.ppermute(block, AXES, [(device_index(*place), device_index(*to)) for...  36.1 us
    ppermute x1, starting transfers between devices, local(): lax.ppermute(jnp.where(arrived, got_b[half:], own[half:]), 'zh', [(3, 2),...  25.9 us
    pallas_call x3, Pallas kernels, attention_call(): pl.pallas_call(body, grid_spec=pltpu.PrefetchScalarGridSpec(num_scalar_pr...  20.1 us
    all_to_all x1, waiting for transfers between devices, exchange(): return lax.all_to_all(block, axes, split_axis=0, concat_axis=0, tiled=True)  6.4 us
    ppermute x8, starting transfers between devices, send(): lax.ppermute(block, AXES, [(device_index(*place), device_index(*to)) for...  6.03 us
    ppermute x1, waiting for transfers between devices, local(): got_a = lax.ppermute(own, 'zh', [(0, 1), (1, 2), (2, 3)])  5.1 us
    all_to_all x1, starting transfers between devices, exchange(): return lax.all_to_all(block, axes, split_axis=0, concat_axis=0, tiled=True)  4.29 us
  transfers between devices with their start and end apart: 15, of which 5 were waited for; matrix products, arithmetic and copies ran while one was open for 1% of the time, Pallas kernels for 9%

profile of v8, /device:TPU:472, one launch (start us, length us, event | category | flops | bytes accessed | tf_op | source)
XLA Modules:
  0.0 170.0 jit_solution(18149951252169464622)
XLA Ops:
  0.0 1.0 fusion.4
  1.1 0.8 maximum_maximum_fusion
  1.9 4.3 %all-to-all-start.2 = ((bf16[4,128,512]{2,1,0:T(8,128)(2,1)}), bf16[4,128,512]{2,1,0:T(8,128)(2,1)S(1)}, u32[]{:S(2)}, u32[]{:S(2)}) async-start(bf16[4,128,512]{2,1,0:T(8,128)(2,1)} %bitcast.5), calls=%async_computation.2 | async-start | bytes 1048576 | tf_op jit(solution)/shard_map/all_to_all | solution.py:23
  6.3 0.9 copy-done.1
  7.2 0.7 collective-permute-start.7
  7.9 0.7 collective-permute-start.8
  9.3 6.4 %all-to-all-done.2 = bf16[4,128,512]{2,1,0:T(8,128)(2,1)S(1)} async-done(((bf16[4,128,512]{2,1,0:T(8,128)(2,1)}), bf16[4,128,512]{2,1,0:T(8,128)(2,1)S(1)}, u32[]{:S(2)}, u32[]{:S(2)}) %all-to-all-start.2) | async-done | bytes 524320 | tf_op jit(solution)/shard_map/all_to_all | solution.py:23
  15.7 43.2 %conditional.3 = (bf16[64,2048]{1,0:T(8,128)(2,1)S(1)}, bf16[512,512]{1,0:T(8,128)(2,1)S(1)}) conditional(s32[]{:T(128)} %convert_element_type.2, () %tuple.38, (s32[]{:T(128)}, s32[]{:T(128)}, s32[]{:T(128)}, bf16[128,2048]{1,0:T(8,128)(2,1)S(1)}, bf16[32,2048]{1,0:T(8,128)(2,1)S(1)}, /*index=5*/bf16[32,2048]{1,0:T(8,128)(2,1)S(1)}, ...), branch_computations={%region_0.1_spmd, %region_1.2_spmd} | conditional | flops 4784135 | bytes 16122182 | solution.py:246
  16.5 0.7 collective-permute-start.1
  17.2 0.7 collective-permute-start.2
  17.9 1.3 collective-permute-start.3
  19.2 0.7 collective-permute-start.4
  19.9 36.1 %collective-permute-done.3 = bf16[128,2048]{1,0:T(8,128)(2,1)S(1)} collective-permute-done((bf16[128,2048]{1,0:T(8,128)(2,1)S(1)}, bf16[128,2048]{1,0:T(8,128)(2,1)S(1)}, u32[]{:S(2)}, u32[]{:S(2)}) %collective-permute-start.3) | collective-permute-done | bytes 524320 | tf_op jit(solution)/shard_map/cond/branch_1_fun/ppermute | solution.py:217
  56.4 1.3 collective-permute-start.5
  57.8 1.1 collective-permute-done.5
  58.9 1.3 collective-permute-start.10
  60.2 1.3 collective-permute-start.11
  61.6 28.0 %conditional.4 = (bf16[1024,512]{1,0:T(8,128)(2,1)}, bf16[1024,512]{1,0:T(8,128)(2,1)}, s32[3]{0:T(128)S(1)}) conditional(s32[]{:T(128)} %convert_element_type.2, () %tuple.37, (bf16[64,2048]{1,0:T(8,128)(2,1)S(1)}, s32[3]{0:T(128)S(1)}) %tuple.40), branch_computations={%region_2.3_spmd, %region_3.4_spmd} | conditional | flops 2097151 | bytes 8912960 | solution.py:246
  61.8 22.8 %all_to_all.37 = bf16[16,64,512]{2,1,0:T(8,128)(2,1)} all-to-all(bf16[16,64,512]{2,1,0:T(8,128)(2,1)S(1)} %bitcast.22), channel_id=1, replica_groups=mesh['zl'=4,'y'=4,'c'=2,'zh'=4,'x'=4] {'y','x'}, dimensions={0} | all-to-all | bytes 2097152 | tf_op jit(solution)/shard_map/cond/branch_1_fun/all_to_all | solution.py:23
  84.7 1.9 %collective-permute-start.6 = (bf16[1024,512]{1,0:T(8,128)(2,1)}, bf16[1024,512]{1,0:T(8,128)(2,1)}, u32[]{:S(2)}, u32[]{:S(2)}) collective-permute-start(bf16[1024,512]{1,0:T(8,128)(2,1)} %bitcast.2), channel_id=1, source_target_pairs={{0,16},{16,0},{1,17},{17,1},{2,18},{18,2},{3,19},{19,3},{4,20},{20... | collective-permute-start | bytes 3145736 | tf_op jit(solution)/shard_map/cond/branch_1_fun/ppermute | solution.py:285
  86.6 3.0 %collective-permute-done.6 = bf16[1024,512]{1,0:T(8,128)(2,1)} collective-permute-done((bf16[1024,512]{1,0:T(8,128)(2,1)}, bf16[1024,512]{1,0:T(8,128)(2,1)}, u32[]{:S(2)}, u32[]{:S(2)}) %collective-permute-start.6) | collective-permute-done | bytes 1048608 | tf_op jit(solution)/shard_map/cond/branch_1_fun/ppermute | solution.py:285
  90.8 5.1 %collective-permute-done.10.ak.av = bf16[512,512]{1,0:T(8,128)(2,1)S(1)} collective-permute-done((bf16[512,512]{1,0:T(8,128)(2,1)S(1)}, bf16[512,512]{1,0:T(8,128)(2,1)S(1)}, u32[]{:S(2)}, u32[]{:S(2)}) %collective-permute-start.10) | collective-permute-done | bytes 524320 | tf_op jit(solution)/shard_map/ppermute | solution.py:281
  95.9 0.8 slice_select_fusion.1
  96.6 1.3 collective-permute-start.12
  97.9 25.9 %collective-permute-start.13 = (bf16[256,512]{1,0:T(8,128)(2,1)S(1)}, bf16[256,512]{1,0:T(8,128)(2,1)S(1)}, u32[]{:S(2)}, u32[]{:S(2)}) collective-permute-start(bf16[256,512]{1,0:T(8,128)(2,1)S(1)} %get-tuple-element.108), channel_id=1, source_target_pairs={{12,8},{0,12},{13,9},{1,13},{14,10},{2,14},{15,11},{3,15},{28,24},... | collective-permute-start | bytes 786440 | tf_op jit(solution)/shard_map/ppermute | solution.py:290
  123.9 17.7 %conditional.5 = (bf16[512,512]{1,0:T(8,128)(2,1)}, f32[4,1,512]{2,1,0:T(1,128)S(1)}, f32[4,1,512]{2,1,0:T(1,128)S(1)}, f32[4,128,512]{2,1,0:T(8,128)S(1)}, s32[3]{0:T(128)S(1)}) conditional(s32[]{:T(128)} %convert_element_type.2, () %tuple.36, (bf16[128,2048]{1,0:T(8,128)(2,1)S(1)}, s32[3]{0:T(128)S(1)}, bf16[512,512]{1,0:T(8,128)(2,1)S(1)}) %tuple.70), branch_computations={%region_4.5_spmd, %region_5.6_spmd} | conditional | flops 10485760 | bytes 3276840 | solution.py:246
  124.0 14.1 %all_to_all.38 = bf16[4,128,512]{2,1,0:T(8,128)(2,1)} all-to-all(bf16[4,128,512]{2,1,0:T(8,128)(2,1)S(1)} %bitcast.21), channel_id=1, replica_groups=mesh['zl'=4,'y'=4,'c'=2,'zh'=4,'x'=4] {'x'}, dimensions={0} | all-to-all | bytes 1048576 | tf_op jit(solution)/shard_map/cond/branch_1_fun/all_to_all | solution.py:23
  138.1 3.4 %own_attention.1 = (f32[4,1,512]{2,1,0:T(1,128)S(1)}, f32[4,1,512]{2,1,0:T(1,128)S(1)}, f32[4,128,512]{2,1,0:T(8,128)S(1)}, s32[3]{0:T(128)S(1)}) custom-call(s32[3]{0:T(128)S(1)} %get-tuple-element.58.where_ref, bf16[512,512]{1,0:T(8,128)(2,1)} %bitcast.4.q_ref, bf16[512,512]{1,0:T(8,128)(2,1)S(1)} %get-tuple-element.59.ok.ov, ...), custom_call_target="tpu_custom_call" | custom-call | flops 8388608 | bytes 131072 | tf_op jit(solution)/shard_map/cond/branch_1_fun/own_attention/pallas_call | solution.py:144
  141.5 12.5 %middle_attention.1 = (f32[4,1,512]{2,1,0:T(1,128)S(1)}, f32[4,1,512]{2,1,0:T(1,128)S(1)}, f32[4,128,512]{2,1,0:T(8,128)S(1)}) custom-call(s32[3]{0:T(128)S(1)} %get-tuple-element.80.where_ref, bf16[512,512]{1,0:T(8,128)(2,1)} %get-tuple-element.81.q_ref, f32[4,1,512]{2,1,0:T(1,128)S(1)} %get-tuple-element.82.p_ref, ...), custom_call_target="tpu_custom_call" | custom-call | flops 3221 | bytes 8 | tf_op jit(solution)/shard_map/middle_attention/pallas_call | solution.py:144
  154.1 4.2 %last_attention.1 = bf16[512,512]{1,0:T(8,128)(2,1)S(1)} custom-call(s32[3]{0:T(128)S(1)} %get-tuple-element.80.where_ref, bf16[512,512]{1,0:T(8,128)(2,1)} %get-tuple-element.81.q_ref, f32[4,1,512]{2,1,0:T(1,128)S(1)} %get-tuple-element.87.peak_ref, f32[4,1,512]{2,1,0:T(1,128)S(1)} %get-tuple-element.88.total_ref, ...), custom_call_target="tpu_custom_call" | custom-call | flops 536870912 | bytes 8388608 | tf_op jit(solution)/shard_map/last_attention/pallas_call | solution.py:144
  158.2 10.9 %all_to_all.39 = bf16[4,128,512]{2,1,0:T(8,128)(2,1)S(1)} all-to-all(bf16[4,128,512]{2,1,0:T(8,128)(2,1)S(1)} %bitcast.19), channel_id=1, replica_groups=mesh['zl'=4,'y'=4,'c'=2,'zh'=4,'x'=4] {'x'}, dimensions={0} | all-to-all | bytes 1048576 | tf_op jit(solution)/shard_map/all_to_all | solution.py:23
  169.2 0.8 pad_maximum_fusion.7
  (50 shorter events, 2.9 us)
Async XLA Ops:
  0.0 1.1 copy-start
  1.9 13.8 %all-to-all-start.2 = ((bf16[4,128,512]{2,1,0:T(8,128)(2,1)}), bf16[4,128,512]{2,1,0:T(8,128)(2,1)S(1)}, u32[]{:S(2)}, u32[]{:S(2)}) async-start(bf16[4,128,512]{2,1,0:T(8,128)(2,1)} %bitcast.5), calls=%async_computation.2 | async-start | bytes 1048576 | tf_op jit(solution)/shard_map/all_to_all | solution.py:23
  6.2 0.9 copy-start.1
  7.2 2.0 %collective-permute-start.7 = (bf16[32,2048]{1,0:T(8,128)(2,1)S(1)}, bf16[32,2048]{1,0:T(8,128)(2,1)S(1)}, u32[]{:S(2)}, u32[]{:S(2)}) collective-permute-start(bf16[32,2048]{1,0:T(8,128)(2,1)S(1)} %get-tuple-element.112), channel_id=1, source_target_pairs={{0,32},{1,33},{2,34},{3,35},{4,36},{5,37},{6,38},{7,39},{8,40},{9,... | collective-permute-start | bytes 393224 | tf_op jit(solution)/shard_map/ppermute | solution.py:217
  7.9 1.4 collective-permute-start.8
  8.6 0.7 collective-permute-start.9
  15.7 0.7 collective-permute-start
  16.5 0.7 collective-permute-start.1
  17.2 2.7 %collective-permute-start.2 = (bf16[128,2048]{1,0:T(8,128)(2,1)S(1)}, bf16[128,2048]{1,0:T(8,128)(2,1)S(1)}, u32[]{:S(2)}, u32[]{:S(2)}) collective-permute-start(bf16[128,2048]{1,0:T(8,128)(2,1)S(1)} %pad_maximum_fusion), channel_id=1, source_target_pairs={{0,128},{1,129},{2,130},{3,131},{4,132},{5,133},{6,134},{7,135},{8... | collective-permute-start | bytes 1572872 | tf_op jit(solution)/shard_map/cond/branch_1_fun/ppermute | solution.py:217
  17.9 38.1 %collective-permute-start.3 = (bf16[128,2048]{1,0:T(8,128)(2,1)S(1)}, bf16[128,2048]{1,0:T(8,128)(2,1)S(1)}, u32[]{:S(2)}, u32[]{:S(2)}) collective-permute-start(bf16[128,2048]{1,0:T(8,128)(2,1)S(1)} %pad_maximum_fusion), channel_id=1, source_target_pairs={{0,256},{1,257},{2,258},{3,259},{4,260},{5,261},{6,262},{7,263},{8... | collective-permute-start | bytes 1572872 | tf_op jit(solution)/shard_map/cond/branch_1_fun/ppermute | solution.py:217
  19.2 36.8 %collective-permute-start.4 = (bf16[128,2048]{1,0:T(8,128)(2,1)S(1)}, bf16[128,2048]{1,0:T(8,128)(2,1)S(1)}, u32[]{:S(2)}, u32[]{:S(2)}) collective-permute-start(bf16[128,2048]{1,0:T(8,128)(2,1)S(1)} %pad_maximum_fusion), channel_id=1, source_target_pairs={{0,396},{1,397},{2,398},{3,399},{4,384},{5,385},{6,386},{7,387},{8... | collective-permute-start | bytes 1572872 | tf_op jit(solution)/shard_map/cond/branch_1_fun/ppermute | solution.py:217
  56.4 2.4 %collective-permute-start.5 = (bf16[64,2048]{1,0:T(8,128)(2,1)S(1)}, bf16[64,2048]{1,0:T(8,128)(2,1)S(1)}, u32[]{:S(2)}, u32[]{:S(2)}) collective-permute-start(bf16[64,2048]{1,0:T(8,128)(2,1)S(1)} %slice.143), channel_id=1, source_target_pairs={{0,16},{1,17},{2,18},{3,19},{4,20},{5,21},{6,22},{7,23},{8,24},{9,... | collective-permute-start | bytes 786440 | tf_op jit(solution)/shard_map/cond/branch_1_fun/ppermute | solution.py:274
  58.9 37.0 %collective-permute-start.10 = (bf16[512,512]{1,0:T(8,128)(2,1)S(1)}, bf16[512,512]{1,0:T(8,128)(2,1)S(1)}, u32[]{:S(2)}, u32[]{:S(2)}) collective-permute-start(bf16[512,512]{1,0:T(8,128)(2,1)S(1)} %get-tuple-element.79), channel_id=1, source_target_pairs={{0,4},{4,8},{8,12},{1,5},{5,9},{9,13},{2,6},{6,10},{10,14},{3,7},{... | collective-permute-start | bytes 1572872 | tf_op jit(solution)/shard_map/ppermute | solution.py:281
  60.2 35.7 %collective-permute-start.11 = (bf16[512,512]{1,0:T(8,128)(2,1)S(1)}, bf16[512,512]{1,0:T(8,128)(2,1)S(1)}, u32[]{:S(2)}, u32[]{:S(2)}) collective-permute-start(bf16[512,512]{1,0:T(8,128)(2,1)S(1)} %get-tuple-element.79), channel_id=1, source_target_pairs={{0,12},{4,0},{1,13},{5,1},{2,14},{6,2},{3,15},{7,3},{16,28},{20,16... | collective-permute-start | bytes 1572872 | tf_op jit(solution)/shard_map/ppermute | solution.py:280
  84.7 4.9 %collective-permute-start.6 = (bf16[1024,512]{1,0:T(8,128)(2,1)}, bf16[1024,512]{1,0:T(8,128)(2,1)}, u32[]{:S(2)}, u32[]{:S(2)}) collective-permute-start(bf16[1024,512]{1,0:T(8,128)(2,1)} %bitcast.2), channel_id=1, source_target_pairs={{0,16},{16,0},{1,17},{17,1},{2,18},{18,2},{3,19},{19,3},{4,20},{20... | collective-permute-start | bytes 3145736 | tf_op jit(solution)/shard_map/cond/branch_1_fun/ppermute | solution.py:285
  95.9 28.0 %copy-start.2 = (bf16[128,2048]{1,0:T(8,128)(2,1)S(1)}, bf16[128,2048]{1,0:T(8,128)(2,1)}, u32[]{:S(2)}) copy-start(bf16[128,2048]{1,0:T(8,128)(2,1)} %param.9) | copy-start | bytes 1572868
  96.6 57.4 %collective-permute-start.12 = (bf16[256,512]{1,0:T(8,128)(2,1)}, bf16[256,512]{1,0:T(8,128)(2,1)S(1)}, u32[]{:S(2)}, u32[]{:S(2)}) collective-permute-start(bf16[256,512]{1,0:T(8,128)(2,1)} %get-tuple-element.109), channel_id=1, source_target_pairs={{4,8},{8,12},{5,9},{9,13},{6,10},{10,14},{7,11},{11,15},{20,24},{2... | collective-permute-start | bytes 786440 | tf_op jit(solution)/shard_map/ppermute | solution.py:289
  97.9 56.1 %collective-permute-start.13 = (bf16[256,512]{1,0:T(8,128)(2,1)S(1)}, bf16[256,512]{1,0:T(8,128)(2,1)S(1)}, u32[]{:S(2)}, u32[]{:S(2)}) collective-permute-start(bf16[256,512]{1,0:T(8,128)(2,1)S(1)} %get-tuple-element.108), channel_id=1, source_target_pairs={{12,8},{0,12},{13,9},{1,13},{14,10},{2,14},{15,11},{3,15},{28,24},... | collective-permute-start | bytes 786440 | tf_op jit(solution)/shard_map/ppermute | solution.py:290
